TPU v7x, 1024 devices: a whole 4x8x16 slice. The times are simulated.
1024 devices in a mesh: lat: 16 (over z_lo, core), lon: 8 (over y), lev: 8 (over x, z_hi).
Axes of the slice: x: 4, y: 8, z: 16 (z_hi: 2, z_lo: 8; z = z_hi * 8 + z_lo), core: 2. Of those that a mesh axis runs over, the one named last changes fastest.
Arguments:
- outer_increment: bfloat16 [32, 1024, 4096], P('lev', 'lat', 'lon'), may hold values from -6 to 6
- courant: bfloat16 [3, 32, 256, 1024], P(None, 'lev', 'lat', 'lon'), may hold values from -0.29882812 to 0.29882812
- obs_column: int32 [262144], P(('lat', 'lon')), may hold values from 0 to 2047
- obs_level: int32 [262144], P(('lat', 'lon')), may hold values from 0 to 31
- obs_value: float32 [262144], P(('lat', 'lon')), may hold values from -6 to 6
Outputs:
- inner_state: float32 [32, 256, 1024], P('lev', 'lat', 'lon')
- adjoint: float32 [32, 256, 1024], P('lev', 'lat', 'lon')
- outer_next: bfloat16 [32, 1024, 4096], P('lev', 'lat', 'lon')
Inputs may be any that keep to these rules, and one draw needn't show every extreme that they name: obs_column numbers a column of the 16 x 512 / 4 inner block of its latitude-longitude block, row by row.
All inputs are finite; a program needn't handle non-finite values.
Results may differ from a plain program's by a relative error of at most 0.001.
Values sent between devices are 32-bit elements; how exact they have to be, the bound alone decides.
No kernel may reach another device: no remote copies, remote signals or barrier semaphores. Data moves between devices by JAX's collectives and lax.ppermute only.
A program may use at most 32 MiB of HBM per device.

v0:
```python
import jax
import jax.numpy as jnp
from jax import lax
from jax.sharding import PartitionSpec as P


def with_halo(array, sides, width, wrap):
    for axis, dim in sides:
        size, length = (lax.axis_size(axis), array.shape[dim])
        up = [(i, (i + 1) % size) for i in range(size if wrap else size - 1)]
        down = [(j, i) for i, j in up]
        last = lax.slice_in_dim(array, length - width, length, axis=dim)
        first = lax.slice_in_dim(array, 0, width, axis=dim)
        before = lax.ppermute(last, axis, up)
        after = lax.ppermute(first, axis, down)
        array = jnp.concatenate([before, array, after], axis=dim)
    return array


def extend_deep(field):
    wrapped = with_halo(field, (("lon", 3),), 2, True)
    return with_halo(wrapped, (("lat", 2), ("lev", 1)), 2, False)


def window_of(field, axis, shift):
    sizes = [field.shape[1] - 2, field.shape[2] - 2, field.shape[3] - 2]
    begins = [1, 1, 1]
    begins[axis - 1] = begins[axis - 1] + shift
    return field[
        :,
        begins[0] : begins[0] + sizes[0],
        begins[1] : begins[1] + sizes[1],
        begins[2] : begins[2] + sizes[2],
    ]


def advance(padded, speeds):
    numbers = window_of(speeds, 1, 0)
    result = (1.0 - jnp.sum(jnp.abs(numbers), axis=0, keepdims=True)) * window_of(padded, 1, 0)
    for direction in range(3):
        lower = jnp.maximum(numbers[direction : direction + 1], 0.0)
        upper = jnp.maximum(-numbers[direction : direction + 1], 0.0)
        result = (
            result
            + lower * window_of(padded, direction + 1, -1)
            + upper * window_of(padded, direction + 1, 1)
        )
    return result


def retreat(padded, speeds):
    numbers = window_of(speeds, 1, 0)
    result = (1.0 - jnp.sum(jnp.abs(numbers), axis=0, keepdims=True)) * window_of(padded, 1, 0)
    for direction in range(3):
        lower = jnp.maximum(speeds[direction : direction + 1], 0.0)
        upper = jnp.maximum(-speeds[direction : direction + 1], 0.0)
        result = (
            result
            + window_of(lower * padded, direction + 1, 1)
            + window_of(upper * padded, direction + 1, -1)
        )
    return result


def shards(outer_increment, courant, obs_column, obs_level, obs_value):
    levels_dev, rows, columns = outer_increment.shape
    inner_rows = rows // 4
    inner_cols = columns // 4
    owner = lax.iota(jnp.int32, columns)[:, None] // 4 == lax.iota(jnp.int32, inner_cols)[None, :]
    column_table = owner.astype(jnp.bfloat16)
    column_sums = jnp.dot(
        outer_increment.reshape(levels_dev * rows, columns),
        column_table,
        preferred_element_type=jnp.float32,
    )
    coarse = jnp.sum(column_sums.reshape(levels_dev, inner_rows, 4, inner_cols), axis=2) * 0.0625
    numbers = courant.astype(jnp.float32)
    stacked = jnp.concatenate([coarse[None], numbers], axis=0)
    widened = extend_deep(stacked)
    speeds = widened[1:]
    state = advance(widened[0:1], speeds)
    state = advance(state, window_of(speeds, 1, 0))
    lowest = lax.axis_index("lev") * levels_dev
    levels_held = state.shape[1]
    local_level = obs_level - lowest
    inside = (local_level >= 0) & (local_level < levels_held)
    flat = jnp.clip(local_level, 0, levels_held - 1) * (inner_rows * inner_cols) + obs_column
    innovation = jnp.where(inside, state.reshape(-1)[flat] - obs_value, 0.0)
    forcing = (
        jnp.zeros((levels_held * inner_rows * inner_cols,), jnp.float32).at[flat].add(innovation)
    )
    adjoint = forcing.reshape(1, levels_held, inner_rows, inner_cols)
    widened = extend_deep(adjoint)
    first = retreat(widened, speeds)
    level_index = lowest - 1 + lax.iota(jnp.int32, levels_dev + 2)
    row_index = lax.axis_index("lat") * inner_rows - 1 + lax.iota(jnp.int32, inner_rows + 2)
    level_keep = (level_index >= 0) & (level_index < lax.axis_size("lev") * levels_dev)
    row_keep = (row_index >= 0) & (row_index < lax.axis_size("lat") * inner_rows)
    keeper = level_keep[:, None, None] & row_keep[None, :, None]
    first = jnp.where(keeper[None], first, 0.0)
    adjoint = retreat(first, window_of(speeds, 1, 0))
    spread_table = jnp.transpose(owner).astype(jnp.float32)
    widened_cols = jnp.dot(
        adjoint[0].reshape(levels_dev * inner_rows, inner_cols),
        spread_table,
        precision=lax.Precision.HIGHEST,
        preferred_element_type=jnp.float32,
    )
    spread = jnp.broadcast_to(
        widened_cols.reshape(levels_dev, inner_rows, 1, columns),
        (levels_dev, inner_rows, 4, columns),
    ).reshape(levels_dev, rows, columns)
    outer_next = (outer_increment.astype(jnp.float32) - spread).astype(jnp.bfloat16)
    return (state[0], adjoint[0], outer_next)


def solution(mesh):
    placed = (
        P("lev", "lat", "lon"),
        P(None, "lev", "lat", "lon"),
        P(("lat", "lon")),
        P(("lat", "lon")),
        P(("lat", "lon")),
    )
    return jax.shard_map(
        shards,
        mesh=mesh,
        in_specs=placed,
        out_specs=(P("lev", "lat", "lon"), P("lev", "lat", "lon"), P("lev", "lat", "lon")),
        check_vma=False,
    )
```

profile of v0, /device:TPU:21, one launch (start us, length us, event | category | flops | bytes accessed | tf_op | source)
XLA Modules:
  0.0 149.8 jit_solution(16473269482493508123)
XLA Ops:
  0.6 1.3 convolution_bitcast_fusion
  1.9 0.1 copy.8
  2.0 0.1 reduce_sum.28
  2.1 0.8 copy-done.2
  2.9 0.1 slice_maximum_fusion.6
  3.0 3.2 %collective-permute-start = (f32[4,4,16,2]{3,2,1,0:T(8,128)S(1)}, f32[4,4,16,2]{3,2,1,0:T(8,128)S(1)}, u32[]{:S(2)}, u32[]{:S(2)}) collective-permute-start(f32[4,4,16,2]{3,2,1,0:T(8,128)S(1)} %get-tuple-element.18), channel_id=1, source_target_pairs={{0,8},{8,16},{16,24},{24,32},{32,40},{40,48},{48,56},{56,0},{1,9},... | collective-permute-start | bytes 6152 | tf_op jit(solution)/shard_map/ppermute | solution.py:14
  6.3 2.1 %collective-permute-start.1 = (f32[4,4,16,2]{3,2,1,0:T(8,128)S(1)}, f32[4,4,16,2]{3,2,1,0:T(8,128)S(1)}, u32[]{:S(2)}, u32[]{:S(2)}) collective-permute-start(f32[4,4,16,2]{3,2,1,0:T(8,128)S(1)} %get-tuple-element.19), channel_id=1, source_target_pairs={{8,0},{16,8},{24,16},{32,24},{40,32},{48,40},{56,48},{0,56},{9,1},... | collective-permute-start | bytes 6152 | tf_op jit(solution)/shard_map/ppermute | solution.py:15
  8.4 0.9 collective-permute-done
  9.3 4.3 %collective-permute-done.1 = f32[4,4,16,2]{3,2,1,0:T(8,128)S(1)} collective-permute-done((f32[4,4,16,2]{3,2,1,0:T(8,128)S(1)}, f32[4,4,16,2]{3,2,1,0:T(8,128)S(1)}, u32[]{:S(2)}, u32[]{:S(2)}) %collective-permute-start.1) | collective-permute-done | bytes 2080 | tf_op jit(solution)/shard_map/ppermute | solution.py:15
  13.6 0.2 pad_maximum_fusion.20
  13.7 5.4 %collective-permute-start.2 = (f32[4,4,2,132]{3,2,1,0:T(2,128)S(1)}, f32[4,4,2,132]{3,2,1,0:T(2,128)S(1)}, u32[]{:S(2)}, u32[]{:S(2)}) collective-permute-start(f32[4,4,2,132]{3,2,1,0:T(2,128)S(1)} %get-tuple-element.16), channel_id=1, source_target_pairs={{0,64},{64,128},{128,192},{192,256},{256,320},{320,384},{384,448},... | collective-permute-start | bytes 50696 | tf_op jit(solution)/shard_map/ppermute | solution.py:14
  19.2 1.9 %collective-permute-start.3 = (f32[4,4,2,132]{3,2,1,0:T(2,128)S(1)}, f32[4,4,2,132]{3,2,1,0:T(2,128)S(1)}, u32[]{:S(2)}, u32[]{:S(2)}) collective-permute-start(f32[4,4,2,132]{3,2,1,0:T(2,128)S(1)} %get-tuple-element.17), channel_id=1, source_target_pairs={{64,0},{128,64},{192,128},{256,192},{320,256},{384,320},{448,384},... | collective-permute-start | bytes 50696 | tf_op jit(solution)/shard_map/ppermute | solution.py:15
  21.1 3.3 %collective-permute-done.3 = f32[4,4,2,132]{3,2,1,0:T(2,128)S(1)} collective-permute-done((f32[4,4,2,132]{3,2,1,0:T(2,128)S(1)}, f32[4,4,2,132]{3,2,1,0:T(2,128)S(1)}, u32[]{:S(2)}, u32[]{:S(2)}) %collective-permute-start.3) | collective-permute-done | bytes 16928 | tf_op jit(solution)/shard_map/ppermute | solution.py:15
  24.4 0.2 pad_maximum_fusion.1
  24.7 18.2 %collective-permute-start.4 = (f32[4,2,20,132]{3,2,1,0:T(8,128)S(1)}, f32[4,2,20,132]{3,2,1,0:T(8,128)S(1)}, u32[]{:S(2)}, u32[]{:S(2)}) collective-permute-start(f32[4,2,20,132]{3,2,1,0:T(8,128)S(1)} %get-tuple-element.14), channel_id=1, source_target_pairs={{0,1},{1,2},{2,3},{3,4},{4,5},{5,6},{6,7},{8,9},{9,10},{10,11},{11... | collective-permute-start | bytes 253448 | tf_op jit(solution)/shard_map/ppermute | solution.py:14
  42.9 1.9 %collective-permute-start.5 = (f32[4,2,20,132]{3,2,1,0:T(8,128)S(1)}, f32[4,2,20,132]{3,2,1,0:T(8,128)S(1)}, u32[]{:S(2)}, u32[]{:S(2)}) collective-permute-start(f32[4,2,20,132]{3,2,1,0:T(8,128)S(1)} %get-tuple-element.15), channel_id=1, source_target_pairs={{1,0},{2,1},{3,2},{4,3},{5,4},{6,5},{7,6},{9,8},{10,9},{11,10},{12... | collective-permute-start | bytes 253448 | tf_op jit(solution)/shard_map/ppermute | solution.py:15
  44.8 11.0 %collective-permute-done.4 = f32[4,2,20,132]{3,2,1,0:T(8,128)S(1)} collective-permute-done((f32[4,2,20,132]{3,2,1,0:T(8,128)S(1)}, f32[4,2,20,132]{3,2,1,0:T(8,128)S(1)}, u32[]{:S(2)}, u32[]{:S(2)}) %collective-permute-start.4) | collective-permute-done | bytes 84512 | tf_op jit(solution)/shard_map/ppermute | solution.py:14
  55.8 19.8 %collective-permute-done.5 = f32[4,2,20,132]{3,2,1,0:T(8,128)S(1)} collective-permute-done((f32[4,2,20,132]{3,2,1,0:T(8,128)S(1)}, f32[4,2,20,132]{3,2,1,0:T(8,128)S(1)}, u32[]{:S(2)}, u32[]{:S(2)}) %collective-permute-start.5) | collective-permute-done | bytes 84512 | tf_op jit(solution)/shard_map/ppermute | solution.py:15
  75.7 0.2 pad_maximum_fusion
  75.9 0.2 fusion
  76.1 0.5 fusion.15
  76.6 0.1 fusion.33
  76.7 0.0 copy-start
  76.7 11.8 %gather_fusion = f32[2048]{0:T(1024)S(1)} fusion(f32[8192]{0:T(1024)S(1)} %bitcast.24, s32[2048]{0:T(1024)S(1)} %get-tuple-element.3), kind=kCustom, calls=%fused_computation | custom fusion | bytes 24576 | tf_op jit(solution)/shard_map/gather | solution.py:88
  88.6 11.3 %scatter_custom_fusion = f32[8192]{0:T(1024)S(1)} fusion(s32[2048]{0:T(1024)S(1)} %get-tuple-element.4, f32[2048]{0:T(1024)S(1)} %subtract_select_fusion, f32[]{:T(128)} %constant.18.clone.1), kind=kCustom, calls=%fused_computation.107 | custom fusion | flops 2048 | bytes 32772 | tf_op jit(solution)/shard_map/scatter-add | solution.py:90
  99.8 0.1 fusion.47
  99.9 4.6 %collective-permute-start.6 = (f32[1,4,16,2]{3,2,1,0:T(8,128)S(1)}, f32[1,4,16,2]{3,2,1,0:T(8,128)S(1)}, u32[]{:S(2)}, u32[]{:S(2)}) collective-permute-start(f32[1,4,16,2]{3,2,1,0:T(8,128)S(1)} %get-tuple-element.24), channel_id=1, source_target_pairs={{0,8},{8,16},{16,24},{24,32},{32,40},{40,48},{48,56},{56,0},{1,9},... | collective-permute-start | bytes 1544 | tf_op jit(solution)/shard_map/ppermute | solution.py:14
  104.5 1.9 %collective-permute-start.7 = (f32[1,4,16,2]{3,2,1,0:T(8,128)S(1)}, f32[1,4,16,2]{3,2,1,0:T(8,128)S(1)}, u32[]{:S(2)}, u32[]{:S(2)}) collective-permute-start(f32[1,4,16,2]{3,2,1,0:T(8,128)S(1)} %get-tuple-element.25), channel_id=1, source_target_pairs={{8,0},{16,8},{24,16},{32,24},{40,32},{48,40},{56,48},{0,56},{9,1},... | collective-permute-start | bytes 1544 | tf_op jit(solution)/shard_map/ppermute | solution.py:15
  106.4 0.1 broadcast_and_fusion
  106.5 2.7 %collective-permute-done.7 = f32[1,4,16,2]{3,2,1,0:T(8,128)S(1)} collective-permute-done((f32[1,4,16,2]{3,2,1,0:T(8,128)S(1)}, f32[1,4,16,2]{3,2,1,0:T(8,128)S(1)}, u32[]{:S(2)}, u32[]{:S(2)}) %collective-permute-start.7) | collective-permute-done | bytes 544 | tf_op jit(solution)/shard_map/ppermute | solution.py:15
  109.2 0.1 pad_maximum_fusion.23
  109.2 5.9 %collective-permute-start.8 = (f32[1,4,2,132]{3,2,1,0:T(2,128)S(1)}, f32[1,4,2,132]{3,2,1,0:T(2,128)S(1)}, u32[]{:S(2)}, u32[]{:S(2)}) collective-permute-start(f32[1,4,2,132]{3,2,1,0:T(2,128)S(1)} %get-tuple-element.22), channel_id=1, source_target_pairs={{0,64},{64,128},{128,192},{192,256},{256,320},{320,384},{384,448},... | collective-permute-start | bytes 12680 | tf_op jit(solution)/shard_map/ppermute | solution.py:14
  115.1 1.9 %collective-permute-start.9 = (f32[1,4,2,132]{3,2,1,0:T(2,128)S(1)}, f32[1,4,2,132]{3,2,1,0:T(2,128)S(1)}, u32[]{:S(2)}, u32[]{:S(2)}) collective-permute-start(f32[1,4,2,132]{3,2,1,0:T(2,128)S(1)} %get-tuple-element.23), channel_id=1, source_target_pairs={{64,0},{128,64},{192,128},{256,192},{320,256},{384,320},{448,384},... | collective-permute-start | bytes 12680 | tf_op jit(solution)/shard_map/ppermute | solution.py:15
  117.0 0.2 slice_maximum_fusion.5
  117.2 2.8 %collective-permute-done.9 = f32[1,4,2,132]{3,2,1,0:T(2,128)S(1)} collective-permute-done((f32[1,4,2,132]{3,2,1,0:T(2,128)S(1)}, f32[1,4,2,132]{3,2,1,0:T(2,128)S(1)}, u32[]{:S(2)}, u32[]{:S(2)}) %collective-permute-start.9) | collective-permute-done | bytes 4256 | tf_op jit(solution)/shard_map/ppermute | solution.py:15
  120.1 0.1 pad_maximum_fusion.16
  120.2 12.7 %collective-permute-start.10 = (f32[1,2,20,132]{3,2,1,0:T(8,128)S(1)}, f32[1,2,20,132]{3,2,1,0:T(8,128)S(1)}, u32[]{:S(2)}, u32[]{:S(2)}) collective-permute-start(f32[1,2,20,132]{3,2,1,0:T(8,128)S(1)} %get-tuple-element.20), channel_id=1, source_target_pairs={{0,1},{1,2},{2,3},{3,4},{4,5},{5,6},{6,7},{8,9},{9,10},{10,11},{11... | collective-permute-start | bytes 63368 | tf_op jit(solution)/shard_map/ppermute | solution.py:14
  132.9 2.2 %collective-permute-start.11 = (f32[1,2,20,132]{3,2,1,0:T(8,128)S(1)}, f32[1,2,20,132]{3,2,1,0:T(8,128)S(1)}, u32[]{:S(2)}, u32[]{:S(2)}) collective-permute-start(f32[1,2,20,132]{3,2,1,0:T(8,128)S(1)} %get-tuple-element.21), channel_id=1, source_target_pairs={{1,0},{2,1},{3,2},{4,3},{5,4},{6,5},{7,6},{9,8},{10,9},{11,10},{12... | collective-permute-start | bytes 63368 | tf_op jit(solution)/shard_map/ppermute | solution.py:15
  135.2 11.4 %collective-permute-done.11 = f32[1,2,20,132]{3,2,1,0:T(8,128)S(1)} collective-permute-done((f32[1,2,20,132]{3,2,1,0:T(8,128)S(1)}, f32[1,2,20,132]{3,2,1,0:T(8,128)S(1)}, u32[]{:S(2)}, u32[]{:S(2)}) %collective-permute-start.11) | collective-permute-done | bytes 21152 | tf_op jit(solution)/shard_map/ppermute | solution.py:15
  146.6 0.1 pad_maximum_fusion.2
  146.7 0.5 fusion.6
  147.2 0.2 fusion.27
  147.4 0.4 fusion.3
  147.8 0.2 copy-done.3
  148.0 0.1 broadcast_in_dim.24
  148.1 0.2 reshape.195
  148.3 0.8 copy-done.1
  149.0 0.8 subtract_convert_fusion
  (25 shorter events, 0.2 us)
Async XLA Ops:
  2.1 0.8 copy-start.2
  2.9 5.4 %copy-start.5 = (s32[2048]{0:T(1024)S(1)}, s32[2048]{0:T(1024)}, u32[]{:S(2)}) copy-start(s32[2048]{0:T(1024)} %param.7) | copy-start | bytes 24580
  3.0 5.3 %copy-start.4 = (s32[2048]{0:T(1024)S(1)}, s32[2048]{0:T(1024)}, u32[]{:S(2)}) copy-start(s32[2048]{0:T(1024)} %param.8) | copy-start | bytes 24580
  3.0 6.3 %collective-permute-start = (f32[4,4,16,2]{3,2,1,0:T(8,128)S(1)}, f32[4,4,16,2]{3,2,1,0:T(8,128)S(1)}, u32[]{:S(2)}, u32[]{:S(2)}) collective-permute-start(f32[4,4,16,2]{3,2,1,0:T(8,128)S(1)} %get-tuple-element.18), channel_id=1, source_target_pairs={{0,8},{8,16},{16,24},{24,32},{32,40},{40,48},{48,56},{56,0},{1,9},... | collective-permute-start | bytes 6152 | tf_op jit(solution)/shard_map/ppermute | solution.py:14
  6.3 7.3 %collective-permute-start.1 = (f32[4,4,16,2]{3,2,1,0:T(8,128)S(1)}, f32[4,4,16,2]{3,2,1,0:T(8,128)S(1)}, u32[]{:S(2)}, u32[]{:S(2)}) collective-permute-start(f32[4,4,16,2]{3,2,1,0:T(8,128)S(1)} %get-tuple-element.19), channel_id=1, source_target_pairs={{8,0},{16,8},{24,16},{32,24},{40,32},{48,40},{56,48},{0,56},{9,1},... | collective-permute-start | bytes 6152 | tf_op jit(solution)/shard_map/ppermute | solution.py:15
  13.7 7.4 %collective-permute-start.2 = (f32[4,4,2,132]{3,2,1,0:T(2,128)S(1)}, f32[4,4,2,132]{3,2,1,0:T(2,128)S(1)}, u32[]{:S(2)}, u32[]{:S(2)}) collective-permute-start(f32[4,4,2,132]{3,2,1,0:T(2,128)S(1)} %get-tuple-element.16), channel_id=1, source_target_pairs={{0,64},{64,128},{128,192},{192,256},{256,320},{320,384},{384,448},... | collective-permute-start | bytes 50696 | tf_op jit(solution)/shard_map/ppermute | solution.py:14
  19.2 5.2 %collective-permute-start.3 = (f32[4,4,2,132]{3,2,1,0:T(2,128)S(1)}, f32[4,4,2,132]{3,2,1,0:T(2,128)S(1)}, u32[]{:S(2)}, u32[]{:S(2)}) collective-permute-start(f32[4,4,2,132]{3,2,1,0:T(2,128)S(1)} %get-tuple-element.17), channel_id=1, source_target_pairs={{64,0},{128,64},{192,128},{256,192},{320,256},{384,320},{448,384},... | collective-permute-start | bytes 50696 | tf_op jit(solution)/shard_map/ppermute | solution.py:15
  24.7 31.1 %collective-permute-start.4 = (f32[4,2,20,132]{3,2,1,0:T(8,128)S(1)}, f32[4,2,20,132]{3,2,1,0:T(8,128)S(1)}, u32[]{:S(2)}, u32[]{:S(2)}) collective-permute-start(f32[4,2,20,132]{3,2,1,0:T(8,128)S(1)} %get-tuple-element.14), channel_id=1, source_target_pairs={{0,1},{1,2},{2,3},{3,4},{4,5},{5,6},{6,7},{8,9},{9,10},{10,11},{11... | collective-permute-start | bytes 253448 | tf_op jit(solution)/shard_map/ppermute | solution.py:14
  42.9 32.8 %collective-permute-start.5 = (f32[4,2,20,132]{3,2,1,0:T(8,128)S(1)}, f32[4,2,20,132]{3,2,1,0:T(8,128)S(1)}, u32[]{:S(2)}, u32[]{:S(2)}) collective-permute-start(f32[4,2,20,132]{3,2,1,0:T(8,128)S(1)} %get-tuple-element.15), channel_id=1, source_target_pairs={{1,0},{2,1},{3,2},{4,3},{5,4},{6,5},{7,6},{9,8},{10,9},{11,10},{12... | collective-permute-start | bytes 253448 | tf_op jit(solution)/shard_map/ppermute | solution.py:15
  76.7 11.8 %copy-start = (f32[1,4,16,128]{3,2,1,0:T(8,128)}, f32[1,4,16,128]{3,2,1,0:T(8,128)S(1)}, u32[]{:S(2)}) copy-start(f32[1,4,16,128]{3,2,1,0:T(8,128)S(1)} %fusion.33) | copy-start | bytes 98308
  76.7 11.8 %copy-start.6 = (f32[2048]{0:T(1024)S(1)}, f32[2048]{0:T(1024)}, u32[]{:S(2)}) copy-start(f32[2048]{0:T(1024)} %param.9) | copy-start | bytes 24580
  99.9 6.6 %collective-permute-start.6 = (f32[1,4,16,2]{3,2,1,0:T(8,128)S(1)}, f32[1,4,16,2]{3,2,1,0:T(8,128)S(1)}, u32[]{:S(2)}, u32[]{:S(2)}) collective-permute-start(f32[1,4,16,2]{3,2,1,0:T(8,128)S(1)} %get-tuple-element.24), channel_id=1, source_target_pairs={{0,8},{8,16},{16,24},{24,32},{32,40},{40,48},{48,56},{56,0},{1,9},... | collective-permute-start | bytes 1544 | tf_op jit(solution)/shard_map/ppermute | solution.py:14
  104.5 4.7 %collective-permute-start.7 = (f32[1,4,16,2]{3,2,1,0:T(8,128)S(1)}, f32[1,4,16,2]{3,2,1,0:T(8,128)S(1)}, u32[]{:S(2)}, u32[]{:S(2)}) collective-permute-start(f32[1,4,16,2]{3,2,1,0:T(8,128)S(1)} %get-tuple-element.25), channel_id=1, source_target_pairs={{8,0},{16,8},{24,16},{32,24},{40,32},{48,40},{56,48},{0,56},{9,1},... | collective-permute-start | bytes 1544 | tf_op jit(solution)/shard_map/ppermute | solution.py:15
  109.2 8.0 %collective-permute-start.8 = (f32[1,4,2,132]{3,2,1,0:T(2,128)S(1)}, f32[1,4,2,132]{3,2,1,0:T(2,128)S(1)}, u32[]{:S(2)}, u32[]{:S(2)}) collective-permute-start(f32[1,4,2,132]{3,2,1,0:T(2,128)S(1)} %get-tuple-element.22), channel_id=1, source_target_pairs={{0,64},{64,128},{128,192},{192,256},{256,320},{320,384},{384,448},... | collective-permute-start | bytes 12680 | tf_op jit(solution)/shard_map/ppermute | solution.py:14
  115.1 5.0 %collective-permute-start.9 = (f32[1,4,2,132]{3,2,1,0:T(2,128)S(1)}, f32[1,4,2,132]{3,2,1,0:T(2,128)S(1)}, u32[]{:S(2)}, u32[]{:S(2)}) collective-permute-start(f32[1,4,2,132]{3,2,1,0:T(2,128)S(1)} %get-tuple-element.23), channel_id=1, source_target_pairs={{64,0},{128,64},{192,128},{256,192},{320,256},{384,320},{448,384},... | collective-permute-start | bytes 12680 | tf_op jit(solution)/shard_map/ppermute | solution.py:15
  120.2 15.0 %collective-permute-start.10 = (f32[1,2,20,132]{3,2,1,0:T(8,128)S(1)}, f32[1,2,20,132]{3,2,1,0:T(8,128)S(1)}, u32[]{:S(2)}, u32[]{:S(2)}) collective-permute-start(f32[1,2,20,132]{3,2,1,0:T(8,128)S(1)} %get-tuple-element.20), channel_id=1, source_target_pairs={{0,1},{1,2},{2,3},{3,4},{4,5},{5,6},{6,7},{8,9},{9,10},{10,11},{11... | collective-permute-start | bytes 63368 | tf_op jit(solution)/shard_map/ppermute | solution.py:14
  132.9 13.7 %collective-permute-start.11 = (f32[1,2,20,132]{3,2,1,0:T(8,128)S(1)}, f32[1,2,20,132]{3,2,1,0:T(8,128)S(1)}, u32[]{:S(2)}, u32[]{:S(2)}) collective-permute-start(f32[1,2,20,132]{3,2,1,0:T(8,128)S(1)} %get-tuple-element.21), channel_id=1, source_target_pairs={{1,0},{2,1},{3,2},{4,3},{5,4},{6,5},{7,6},{9,8},{10,9},{11,10},{12... | collective-permute-start | bytes 63368 | tf_op jit(solution)/shard_map/ppermute | solution.py:15
  147.4 0.6 copy-start.3
  148.1 1.0 copy-start.1
where the time goes:
time: 150 us
  starting transfers between devices  61.9 us (41%)
  waiting for transfers between devices  56.2 us (37%)
  other arithmetic  14.9 us (10%)
  local copies, waits for them, and re-layouts  14.1 us (9%)
  matrix products  1.64 us (1%)
    ppermute x6, starting transfers between devices, with_halo(): before = lax.ppermute(last, axis, up)  50 us
    ppermute x6, waiting for transfers between devices, with_halo(): after = lax.ppermute(first, axis, down)  44.3 us
    ppermute x6, starting transfers between devices, with_halo(): after = lax.ppermute(first, axis, down)  12 us
    ppermute x6, waiting for transfers between devices, with_halo(): before = lax.ppermute(last, axis, up)  11.9 us
    gather x1, local copies, waits for them, and re-layouts, shards(): innovation = jnp.where(inside, state.reshape(-1)[flat] - obs_value, 0.0)  11.8 us
    scatter-add x1, other arithmetic, shards(): jnp.zeros((levels_held * inner_rows * inner_cols,), jnp.float32).at[flat]  11.3 us
  transfers between devices with their start and end apart: 12, of which 8 were waited for; matrix products, arithmetic and copies ran while one was open for 0% of the time, Pallas kernels for 0%

commit v1 on v0

v1 whole, which is shorter than its diff:
```python
import functools

import jax
import jax.numpy as jnp
from jax import lax
from jax.experimental import pallas as pl
from jax.experimental.pallas import tpu as pltpu
from jax.sharding import PartitionSpec as P

F32 = jnp.float32
BF16 = jnp.bfloat16
VMEM = pl.BlockSpec(memory_space=pltpu.VMEM)
SMEM = pl.BlockSpec(memory_space=pltpu.SMEM)

LEV = 4
ROW = 16
COL = 128
DEEP = 12
TALL = 24
OWN = 16 * ROW
NEAR = 40
STRIP = 56


def column_table(wide, narrow, wide_axis):
    shape = (wide, narrow) if wide_axis == 0 else (narrow, wide)
    fine = lax.broadcasted_iota(jnp.int32, shape, wide_axis) >> 2
    coarse = lax.broadcasted_iota(jnp.int32, shape, 1 - wide_axis)
    return (fine == coarse).astype(F32).astype(BF16)


def coarse_kernel(outer_ref, courant_ref, block_ref, up_ref, down_ref, sums_ref):
    sums_ref[...] = jnp.dot(
        outer_ref[...].reshape(LEV * ROW * 4, COL * 4),
        column_table(COL * 4, COL, 0),
        preferred_element_type=F32,
    )
    rows = LEV * ROW
    total = sums_ref[pl.ds(0, rows, stride=4), :]
    for part in range(1, 4):
        total = total + sums_ref[pl.ds(part, rows, stride=4), :]
    block_ref[0:rows, :] = total * 0.0625
    block_ref[rows:OWN, :] = courant_ref[...].astype(F32).reshape(OWN - rows, COL)
    for ref, edge, step in ((up_ref, ROW - 1, -1), (down_ref, 0, 1)):
        for i in range(3):
            ref[4 * i : 4 * i + 4, :] = block_ref[pl.ds(edge + step * i, 4, stride=ROW), :]
        for i in range(2):
            ref[12 + 12 * i : 24 + 12 * i, :] = block_ref[
                pl.ds(rows + edge + step * i, 12, stride=ROW), :
            ]
        ref[36:40, :] = jnp.zeros((4, COL), F32)
        ref[40:44, :] = block_ref[pl.ds(edge + step * 3, 4, stride=ROW), :]
        ref[44:56, :] = block_ref[pl.ds(rows + edge + step * 2, 12, stride=ROW), :]


def obs_kernel(lowest_ref, column_ref, level_ref, value_ref, field_ref, up_ref, down_ref):
    count = column_ref.shape[1]
    chunk = 512
    total = jnp.zeros((4 * COL, COL), F32)
    for begin in range(0, count, chunk):
        cut = slice(begin, begin + chunk)
        cell = column_ref[:, cut]
        place = (level_ref[:, cut] - lowest_ref[0] + 2) * ROW + (cell >> 7)
        value = value_ref[:, cut]
        high = value.astype(BF16).astype(F32)
        rest = value - high
        middle = rest.astype(BF16).astype(F32)
        low = rest - middle
        index = lax.broadcasted_iota(jnp.int32, (COL, chunk), 0)
        here = index == place
        across = jnp.where(index == (cell & 127), 1.0, 0.0).astype(BF16)
        down = jnp.concatenate(
            [jnp.where(here, part, 0.0).astype(BF16) for part in (1.0, high, middle, low)], axis=0
        )
        total = total + lax.dot_general(
            down, across, (((1,), (1,)), ((), ())), preferred_element_type=F32
        )
    field_ref[0:128, :] = total[0:128]
    field_ref[128:256, :] = (total[128:256] + total[256:384]) + total[384:512]
    for ref, edge, step in ((up_ref, ROW - 1, -1), (down_ref, 0, 1)):
        for i in range(2):
            ref[16 * i : 16 * i + 16, :] = field_ref[pl.ds(edge + step * i, 16, stride=ROW), :]


def edge_tiles():
    tiles = []
    for level in range(1, 11):
        off = max(0, 4 - level, level - 7)
        for part in range(3 if off <= 2 else 2):
            tiles.append((0, level, part))
    for k in range(3):
        for level in range(2, 10):
            off = max(0, 4 - level, level - 7)
            for part in range(3 if off <= 1 else 2):
                tiles.append((1 + k, level, part))
    for k in range(2):
        for level in range(3, 9):
            off = max(0, 4 - level, level - 7)
            for part in range(3 if off <= 0 else 2):
                tiles.append((4 + k, level, part))
    return tiles


EDGES = edge_tiles()
PACKS = -(-len(EDGES) // 32)


def gather_kernel(
    parity_ref,
    block_ref,
    before_ref,
    after_ref,
    pair_ref,
    far_ref,
    field_ref,
    field_before_ref,
    field_after_ref,
    all_ref,
    right_ref,
    left_ref,
):
    odd = parity_ref[0]
    pair_level = (1 - odd) * 8
    far_level = odd * 8
    rows = LEV * ROW
    for base, ref in ((4, block_ref), (pair_level, pair_ref), (far_level, far_ref)):
        for f in range(4):
            for l in range(LEV):
                begin = (f * LEV + l) * ROW
                all_ref[f, base + l, 0:ROW, :] = ref[begin : begin + ROW, :]
    for side, (own, offset) in enumerate(((before_ref, OWN), (after_ref, OWN + NEAR))):
        for base, ref, start, reach in (
            (4, own, 0, 4),
            (pair_level, pair_ref, offset, 3),
            (far_level, far_ref, offset, 3),
        ):
            for f in range(4):
                for i in range(reach if f == 0 else reach - 1):
                    if f == 0:
                        begin = 4 * i if i < 3 else 40
                    else:
                        begin = (12 + 12 * i if i < 2 else 44) + (f - 1) * 4
                    row = TALL - 1 - i if side == 0 else ROW + i
                    for l in range(LEV):
                        at = start + begin + l
                        all_ref[f, base + l, row : row + 1, :] = ref[at : at + 1, :]
    for f in range(2):
        for l in range(8):
            begin = (f * 8 + l) * ROW
            all_ref[4 + f, 2 + l, 0:ROW, :] = field_ref[begin : begin + ROW, :]
            for i in range(2):
                at = 16 * i + f * 8 + l
                all_ref[4 + f, 2 + l, TALL - 1 - i : TALL - i, :] = field_before_ref[at : at + 1, :]
                all_ref[4 + f, 2 + l, ROW + i : ROW + i + 1, :] = field_after_ref[at : at + 1, :]
    group = lax.broadcasted_iota(jnp.int32, (8, COL), 1) >> 2
    for pack in range(PACKS):
        right = jnp.zeros((8, COL), F32)
        left = jnp.zeros((8, COL), F32)
        for slot, (f, level, part) in enumerate(EDGES[32 * pack : 32 * pack + 32]):
            tile = all_ref[f, level, 8 * part : 8 * part + 8, :]
            here = group == slot
            right = jnp.where(here, pltpu.roll(tile, (4 * slot + 4) % COL, 1), right)
            left = jnp.where(here, pltpu.roll(tile, 4 * slot, 1) if slot else tile, left)
        right_ref[8 * pack : 8 * pack + 8, :] = right
        left_ref[8 * pack : 8 * pack + 8, :] = left


def turn(tile, shift, axis):
    return pltpu.roll(tile, shift % tile.shape[axis], axis)


def step_kernel(
    all_ref,
    west_ref,
    east_ref,
    outer_ref,
    state_ref,
    adjoint_ref,
    next_ref,
    wide_ref,
    first_ref,
    force_ref,
    back_ref,
    flat_ref,
    spread_ref,
):
    near = lax.broadcasted_iota(jnp.int32, (8, COL), 1) < 64
    wide_ref[:, :, :, 0:COL] = all_ref[...]
    for slot, (f, level, part) in enumerate(EDGES):
        pack, lane = divmod(slot, 32)
        east = east_ref[8 * pack : 8 * pack + 8, :]
        west = west_ref[8 * pack : 8 * pack + 8, :]
        wide_ref[f, level, 8 * part : 8 * part + 8, COL : 2 * COL] = jnp.where(
            near,
            turn(east, -4 * lane, 1) if lane else east,
            turn(west, -4 * lane - 4, 1),
        )

    def plus(x):
        return jnp.maximum(x, 0.0)

    def centre(level):
        return 1.0 - (
            jnp.abs(wide_ref[1, level]) + jnp.abs(wide_ref[2, level]) + jnp.abs(wide_ref[3, level])
        )

    def advance(get, level):
        here = get(level)
        c0, c1, c2 = (wide_ref[1 + k, level] for k in range(3))
        result = centre(level) * here
        result = result + plus(c0) * get(level - 1) + plus(-c0) * get(level + 1)
        result = result + plus(c1) * turn(here, 1, 0) + plus(-c1) * turn(here, -1, 0)
        return result + plus(c2) * turn(here, 1, 1) + plus(-c2) * turn(here, -1, 1)

    def retreat(get, level):
        here = get(level)
        c1, c2 = (wide_ref[2 + k, level] for k in range(2))
        result = centre(level) * here
        result = (
            result
            + plus(wide_ref[1, level + 1]) * get(level + 1)
            + plus(-wide_ref[1, level - 1]) * get(level - 1)
        )
        result = result + turn(plus(c1) * here, -1, 0) + turn(plus(-c1) * here, 1, 0)
        return result + turn(plus(c2) * here, -1, 1) + turn(plus(-c2) * here, 1, 1)

    for level in range(1, 11):
        first_ref[level] = advance(lambda l: wide_ref[0, l], level)
    for level in range(2, 10):
        state = advance(lambda l: first_ref[l], level)
        if 4 <= level < 8:
            state_ref[level - 4] = state[0:ROW, 0:COL]
        force_ref[level] = wide_ref[4, level] * state - wide_ref[5, level]
    for level in range(3, 9):
        back_ref[level] = retreat(lambda l: force_ref[l], level)
    for level in range(4, 8):
        result = retreat(lambda l: back_ref[l], level)[0:ROW, 0:COL]
        adjoint_ref[level - 4] = result
        flat_ref[ROW * (level - 4) : ROW * (level - 3), :] = result
    flat = flat_ref[...]
    high = flat.astype(BF16)
    rest = flat - high.astype(F32)
    middle = rest.astype(BF16)
    low = (rest - middle.astype(F32)).astype(BF16)
    table = column_table(COL * 4, COL, 1)
    spread = jnp.dot(high, table, preferred_element_type=F32)
    spread = spread + jnp.dot(middle, table, preferred_element_type=F32)
    spread = spread + jnp.dot(low, table, preferred_element_type=F32)
    for tile in range(4):
        cut = slice(COL * tile, COL * tile + COL)
        for part in range(4):
            spread_ref[pl.ds(part, LEV * ROW, stride=4), :] = spread[:, cut]
        outer = outer_ref[:, :, cut].astype(F32).reshape(LEV * ROW * 4, COL)
        result = (outer - spread_ref[...]).reshape(LEV, ROW * 4, COL)
        next_ref[:, :, cut] = result.astype(BF16)


def call(kernel, outs, ins, scratch=(), scalars=0, flops=1000000, name=None):
    single = len(outs) == 1
    shapes = [jax.ShapeDtypeStruct(shape, kind) for shape, kind in outs]
    return pl.pallas_call(
        kernel,
        out_shape=shapes[0] if single else shapes,
        in_specs=[SMEM] * scalars + [VMEM] * (len(ins) - scalars),
        out_specs=VMEM if single else [VMEM] * len(outs),
        scratch_shapes=list(scratch),
        compiler_params=pltpu.CompilerParams(vmem_limit_bytes=16 * 1024 * 1024),
        cost_estimate=pl.CostEstimate(flops=flops, bytes_accessed=500000, transcendentals=0),
        name=name,
    )(*ins)


def shift(size, by, wrap):
    return [
        (i, (i + by) % size) for i in range(size) if wrap or 0 <= i + by < size
    ]


def shards(outer_increment, courant, obs_column, obs_level, obs_value):
    lev = lax.axis_size("lev")
    lat_up, lat_down = (shift(lax.axis_size("lat"), by, False) for by in (1, -1))
    lon_up, lon_down = (shift(lax.axis_size("lon"), by, True) for by in (1, -1))
    pairs = [(i, i ^ 1) for i in range(lev)]
    far = [(i, i + 2) for i in range(0, lev - 2, 2)] + [(i, i - 2) for i in range(3, lev, 2)]
    position = lax.axis_index("lev").astype(jnp.int32)
    parity = (position & 1).reshape(1)
    lowest = (position * LEV).reshape(1)

    block, up, down = call(
        coarse_kernel,
        [((OWN, COL), F32), ((STRIP, COL), F32), ((STRIP, COL), F32)],
        [outer_increment, courant],
        [pltpu.VMEM((LEV * ROW * 4, COL), F32)],
        name="coarse",
    )
    before = lax.ppermute(up, "lat", lat_up)
    after = lax.ppermute(down, "lat", lat_down)
    pair = lax.ppermute(
        jnp.concatenate([block, before[:NEAR], after[:NEAR]], axis=0), "lev", pairs
    )
    far_block = lax.ppermute(pair, "lev", far)

    count = obs_column.shape[0]
    fields, fields_up, fields_down = call(
        obs_kernel,
        [((256, COL), F32), ((32, COL), F32), ((32, COL), F32)],
        [lowest]
        + [array.reshape(1, count) for array in (obs_column, obs_level, obs_value)],
        scalars=1,
        name="observe",
    )
    fields_before = lax.ppermute(fields_up, "lat", lat_up)
    fields_after = lax.ppermute(fields_down, "lat", lat_down)

    everything, right, left = call(
        gather_kernel,
        [((6, DEEP, TALL, COL), F32), ((8 * PACKS, COL), F32), ((8 * PACKS, COL), F32)],
        [parity, block, before, after, pair, far_block, fields, fields_before, fields_after],
        scalars=1,
        name="assemble",
    )
    west = lax.ppermute(right, "lon", lon_up)
    east = lax.ppermute(left, "lon", lon_down)
    wide = (DEEP, TALL, 2 * COL)
    state, adjoint, outer_next = call(
        step_kernel,
        [
            ((LEV, ROW, COL), F32),
            ((LEV, ROW, COL), F32),
            (outer_increment.shape, BF16),
        ],
        [everything, west, east, outer_increment],
        [
            pltpu.VMEM((6,) + wide, F32),
            pltpu.VMEM(wide, F32),
            pltpu.VMEM(wide, F32),
            pltpu.VMEM(wide, F32),
            pltpu.VMEM((LEV * ROW, COL), F32),
            pltpu.VMEM((LEV * ROW * 4, COL), F32),
        ],
        name="steps",
    )
    return state, adjoint, outer_next


def solution(mesh):
    placed = (
        P("lev", "lat", "lon"),
        P(None, "lev", "lat", "lon"),
        P(("lat", "lon")),
        P(("lat", "lon")),
        P(("lat", "lon")),
    )
    return jax.shard_map(
        shards,
        mesh=mesh,
        in_specs=placed,
        out_specs=(P("lev", "lat", "lon"), P("lev", "lat", "lon"), P("lev", "lat", "lon")),
        check_vma=False,
    )
```

time: 150 us -> 68.9 us (0.46)
  the two profiles are of different devices: /device:TPU:21 before, /device:TPU:25 now
where the time goes in v1:
time: 68.9 us; the launch traced here: 68.4 us
  starting transfers between devices  38.6 us (56%)
  waiting for transfers between devices  22.7 us (33%)
  Pallas kernels  3.22 us (5%)
  local copies, waits for them, and re-layouts  3.09 us (4%)
  between operations  0.79 us (1%)
    ppermute x1, starting transfers between devices, shards(): lax.ppermute(jnp.concatenate([block, before[:NEAR], after[:NEAR]], axis=0...  18.3 us
    ppermute x1, waiting for transfers between devices, shards(): lax.ppermute(jnp.concatenate([block, before[:NEAR], after[:NEAR]], axis=0...  13.4 us
    ppermute x1, starting transfers between devices, shards(): before = lax.ppermute(up, 'lat', lat_up)  4.56 us
    ppermute x1, starting transfers between devices, shards(): west = lax.ppermute(right, 'lon', lon_up)  4.42 us
    ppermute x1, waiting for transfers between devices, shards(): east = lax.ppermute(left, 'lon', lon_down)  3.75 us
    pallas_call x4, Pallas kernels, call(): pl.pallas_call(kernel, out_shape=shapes[0] if single else shapes, in_spec...  3.22 us
    ppermute x1, starting transfers between devices, shards(): far_block = lax.ppermute(pair, 'lev', far)  3.12 us
    ppermute x1, waiting for transfers between devices, shards(): fields_after = lax.ppermute(fields_down, 'lat', lat_down)  2.95 us
  transfers between devices with their start and end apart: 8, of which 4 were waited for; matrix products, arithmetic and copies ran while one was open for 0% of the time, Pallas kernels for 1%

profile of v1, /device:TPU:25, one launch (start us, length us, event | category | flops | bytes accessed | tf_op | source)
XLA Modules:
  0.0 68.4 jit_solution(16182857034605945701)
XLA Ops:
  0.6 0.0 copy-start
  0.6 0.9 %copy-done = bf16[4,64,512]{2,1,0:T(8,128)(2,1)S(1)} copy-done((bf16[4,64,512]{2,1,0:T(8,128)(2,1)S(1)}, bf16[4,64,512]{2,1,0:T(8,128)(2,1)}, u32[]{:S(2)}) %copy-start) | copy-done | bytes 262168
  1.6 0.0 copy-start.4
  1.6 0.8 %copy-done.4 = bf16[3,4,16,128]{3,2,1,0:T(8,128)(2,1)S(1)} copy-done((bf16[3,4,16,128]{3,2,1,0:T(8,128)(2,1)S(1)}, bf16[3,4,16,128]{3,2,1,0:T(8,128)(2,1)}, u32[]{:S(2)}) %copy-start.4) | copy-done | bytes 49176
  2.4 0.2 coarse.1
  2.6 4.6 %collective-permute-start = (f32[56,128]{1,0:T(8,128)S(1)}, f32[56,128]{1,0:T(8,128)S(1)}, u32[]{:S(2)}, u32[]{:S(2)}) collective-permute-start(f32[56,128]{1,0:T(8,128)S(1)} %get-tuple-element.13), channel_id=1, source_target_pairs={{0,64},{64,128},{128,192},{192,256},{256,320},{320,384},{384,448},... | collective-permute-start | bytes 86024 | tf_op jit(solution)/shard_map/ppermute | solution.py:296
  7.2 1.9 %collective-permute-start.1 = (f32[56,128]{1,0:T(8,128)S(1)}, f32[56,128]{1,0:T(8,128)S(1)}, u32[]{:S(2)}, u32[]{:S(2)}) collective-permute-start(f32[56,128]{1,0:T(8,128)S(1)} %get-tuple-element.14), channel_id=1, source_target_pairs={{64,0},{128,64},{192,128},{256,192},{320,256},{384,320},{448,384},... | collective-permute-start | bytes 86024 | tf_op jit(solution)/shard_map/ppermute | solution.py:297
  9.1 0.0 collective-permute-done.before_ref
  9.1 0.0 copy-start.2
  9.1 0.6 copy-done.2
  9.7 2.6 %collective-permute-done.1.after_ref = f32[56,128]{1,0:T(8,128)S(1)} collective-permute-done((f32[56,128]{1,0:T(8,128)S(1)}, f32[56,128]{1,0:T(8,128)S(1)}, u32[]{:S(2)}, u32[]{:S(2)}) %collective-permute-start.1) | collective-permute-done | bytes 28704 | tf_op jit(solution)/shard_map/ppermute | solution.py:297
  12.4 0.0 slice-start
  12.4 0.7 %slice-done = f32[40,128]{1,0:T(8,128)S(1)} async-done(((f32[56,128]{1,0:T(8,128)}), f32[40,128]{1,0:T(8,128)S(1)}, s32[]{:S(2)}) %slice-start) | async-done | bytes 20504 | tf_op jit(solution)/shard_map/slice | solution.py:299
  13.1 0.0 copy-start.5
  13.1 0.0 copy-start.6
  13.1 0.0 copy-start.7
  13.1 0.0 copy-start.3
  13.1 18.3 %collective-permute-start.2 = (f32[336,128]{1,0:T(8,128)S(1)}, f32[336,128]{1,0:T(8,128)S(1)}, u32[]{:S(2)}, u32[]{:S(2)}) collective-permute-start(f32[336,128]{1,0:T(8,128)S(1)} %pad_maximum_fusion), channel_id=1, source_target_pairs={{0,1},{1,0},{2,3},{3,2},{4,5},{5,4},{6,7},{7,6},{8,9},{9,8},{10,11... | collective-permute-start | bytes 516104 | tf_op jit(solution)/shard_map/ppermute | solution.py:298
  31.5 13.4 %collective-permute-done.2.pair_ref = f32[336,128]{1,0:T(8,128)S(1)} collective-permute-done((f32[336,128]{1,0:T(8,128)S(1)}, f32[336,128]{1,0:T(8,128)S(1)}, u32[]{:S(2)}, u32[]{:S(2)}) %collective-permute-start.2) | collective-permute-done | bytes 172064 | tf_op jit(solution)/shard_map/ppermute | solution.py:298
  44.8 3.1 %collective-permute-start.3 = (f32[336,128]{1,0:T(8,128)S(1)}, f32[336,128]{1,0:T(8,128)S(1)}, u32[]{:S(2)}, u32[]{:S(2)}) collective-permute-start(f32[336,128]{1,0:T(8,128)S(1)} %collective-permute-done.2.pair_ref), channel_id=1, source_target_pairs={{0,2},{2,4},{4,6},{3,1},{5,3},{7,5},{8,10},{10,12},{12,14},{11,9},... | collective-permute-start | bytes 516104 | tf_op jit(solution)/shard_map/ppermute | solution.py:301
  48.0 0.0 copy-done.5
  48.0 0.0 copy-done.6
  48.0 0.0 copy-done.7
  48.0 0.7 %observe.1 = (f32[256,128]{1,0:T(8,128)S(1)}, f32[32,128]{1,0:T(8,128)S(1)}, f32[32,128]{1,0:T(8,128)S(1)}) custom-call(s32[1]{0:T(128)} %bitcast.1.lowest_ref, s32[1,2048]{1,0:T(1,128)S(1)} %bitcast.5, s32[1,2048]{1,0:T(1,128)S(1)} %bitcast.6, f32[1,2048]{1,0:T(1,128)S(1)} %bitcast.7), custom_call_target="tpu_custom_call" | custom-call | flops 1000000 | bytes 500000 | tf_op jit(solution)/shard_map/observe/pallas_call | solution.py:261
  48.7 2.2 %collective-permute-start.4 = (f32[32,128]{1,0:T(8,128)S(1)}, f32[32,128]{1,0:T(8,128)S(1)}, u32[]{:S(2)}, u32[]{:S(2)}) collective-permute-start(f32[32,128]{1,0:T(8,128)S(1)} %get-tuple-element.16), channel_id=1, source_target_pairs={{0,64},{64,128},{128,192},{192,256},{256,320},{320,384},{384,448},... | collective-permute-start | bytes 49160 | tf_op jit(solution)/shard_map/ppermute | solution.py:312
  51.0 2.1 %collective-permute-start.5 = (f32[32,128]{1,0:T(8,128)S(1)}, f32[32,128]{1,0:T(8,128)S(1)}, u32[]{:S(2)}, u32[]{:S(2)}) collective-permute-start(f32[32,128]{1,0:T(8,128)S(1)} %get-tuple-element.17), channel_id=1, source_target_pairs={{64,0},{128,64},{192,128},{256,192},{320,256},{384,320},{448,384},... | collective-permute-start | bytes 49160 | tf_op jit(solution)/shard_map/ppermute | solution.py:313
  53.1 0.0 collective-permute-done.4.field_before_ref
  53.1 3.0 %collective-permute-done.5.field_after_ref = f32[32,128]{1,0:T(8,128)S(1)} collective-permute-done((f32[32,128]{1,0:T(8,128)S(1)}, f32[32,128]{1,0:T(8,128)S(1)}, u32[]{:S(2)}, u32[]{:S(2)}) %collective-permute-start.5) | collective-permute-done | bytes 16416 | tf_op jit(solution)/shard_map/ppermute | solution.py:313
  56.0 0.0 collective-permute-done.3.far_ref
  56.0 0.0 copy-done.3
  56.0 0.0 copy-start.1
  56.0 0.4 assemble.1
  56.5 4.4 %collective-permute-start.6 = (f32[32,128]{1,0:T(8,128)S(1)}, f32[32,128]{1,0:T(8,128)S(1)}, u32[]{:S(2)}, u32[]{:S(2)}) collective-permute-start(f32[32,128]{1,0:T(8,128)S(1)} %get-tuple-element.19), channel_id=1, source_target_pairs={{0,8},{8,16},{16,24},{24,32},{32,40},{40,48},{48,56},{56,0},{1,9},... | collective-permute-start | bytes 49160 | tf_op jit(solution)/shard_map/ppermute | solution.py:322
  60.9 1.9 %collective-permute-start.7 = (f32[32,128]{1,0:T(8,128)S(1)}, f32[32,128]{1,0:T(8,128)S(1)}, u32[]{:S(2)}, u32[]{:S(2)}) collective-permute-start(f32[32,128]{1,0:T(8,128)S(1)} %get-tuple-element.20), channel_id=1, source_target_pairs={{0,56},{8,0},{16,8},{24,16},{32,24},{40,32},{48,40},{56,48},{1,57}... | collective-permute-start | bytes 49160 | tf_op jit(solution)/shard_map/ppermute | solution.py:323
  62.8 0.0 collective-permute-done.6.west_ref
  62.9 3.8 %collective-permute-done.7.east_ref = f32[32,128]{1,0:T(8,128)S(1)} collective-permute-done((f32[32,128]{1,0:T(8,128)S(1)}, f32[32,128]{1,0:T(8,128)S(1)}, u32[]{:S(2)}, u32[]{:S(2)}) %collective-permute-start.7) | collective-permute-done | bytes 16416 | tf_op jit(solution)/shard_map/ppermute | solution.py:323
  66.6 0.0 copy-done.1
  66.6 1.8 %steps.1 = (f32[4,16,128]{2,1,0:T(8,128)}, f32[4,16,128]{2,1,0:T(8,128)}, bf16[4,64,512]{2,1,0:T(8,128)(2,1)}) custom-call(f32[6,12,24,128]{3,2,1,0:T(8,128)S(1)} %get-tuple-element.18.all_ref, f32[32,128]{1,0:T(8,128)S(1)} %collective-permute-done.6.west_ref, f32[32,128]{1,0:T(8,128)S(1)} %collective-permute-done.7.east_ref, bf16[4,64,512]{2,1,0:T(8,128)(2,1)S(1)} %copy-done.1), custom_call_target="tpu_custom_call" | custom-call | flops 1000000 | bytes 500000 | tf_op jit(solution)/shard_map/steps/pallas_call | solution.py:261
  (2 shorter events, 0.0 us)
Async XLA Ops:
  0.6 1.0 %copy-start = (bf16[4,64,512]{2,1,0:T(8,128)(2,1)S(1)}, bf16[4,64,512]{2,1,0:T(8,128)(2,1)}, u32[]{:S(2)}) copy-start(bf16[4,64,512]{2,1,0:T(8,128)(2,1)} %outer_ref.3) | copy-start | bytes 786436
  1.6 0.8 %copy-start.4 = (bf16[3,4,16,128]{3,2,1,0:T(8,128)(2,1)S(1)}, bf16[3,4,16,128]{3,2,1,0:T(8,128)(2,1)}, u32[]{:S(2)}) copy-start(bf16[3,4,16,128]{3,2,1,0:T(8,128)(2,1)} %courant_ref.1) | copy-start | bytes 147460
  2.6 6.5 %collective-permute-start = (f32[56,128]{1,0:T(8,128)S(1)}, f32[56,128]{1,0:T(8,128)S(1)}, u32[]{:S(2)}, u32[]{:S(2)}) collective-permute-start(f32[56,128]{1,0:T(8,128)S(1)} %get-tuple-element.13), channel_id=1, source_target_pairs={{0,64},{64,128},{128,192},{192,256},{256,320},{320,384},{384,448},... | collective-permute-start | bytes 86024 | tf_op jit(solution)/shard_map/ppermute | solution.py:296
  7.2 5.2 %collective-permute-start.1 = (f32[56,128]{1,0:T(8,128)S(1)}, f32[56,128]{1,0:T(8,128)S(1)}, u32[]{:S(2)}, u32[]{:S(2)}) collective-permute-start(f32[56,128]{1,0:T(8,128)S(1)} %get-tuple-element.14), channel_id=1, source_target_pairs={{64,0},{128,64},{192,128},{256,192},{320,256},{384,320},{448,384},... | collective-permute-start | bytes 86024 | tf_op jit(solution)/shard_map/ppermute | solution.py:297
  9.1 0.6 copy-start.2
  12.4 0.7 %slice-start = ((f32[56,128]{1,0:T(8,128)}), f32[40,128]{1,0:T(8,128)S(1)}, s32[]{:S(2)}) async-start(f32[56,128]{1,0:T(8,128)} %copy-done.2), calls=%async_computation | async-start | bytes 40960 | tf_op jit(solution)/shard_map/slice | solution.py:299
  13.1 34.9 %copy-start.5 = (s32[2048]{0:T(1024)S(1)}, s32[2048]{0:T(1024)}, u32[]{:S(2)}) copy-start(s32[2048]{0:T(1024)} %param.7) | copy-start | bytes 24580
  13.1 34.9 %copy-start.6 = (s32[2048]{0:T(1024)S(1)}, s32[2048]{0:T(1024)}, u32[]{:S(2)}) copy-start(s32[2048]{0:T(1024)} %param.8) | copy-start | bytes 24580
  13.1 34.9 %copy-start.7 = (f32[2048]{0:T(1024)S(1)}, f32[2048]{0:T(1024)}, u32[]{:S(2)}) copy-start(f32[2048]{0:T(1024)} %param.9) | copy-start | bytes 24580
  13.1 42.9 %copy-start.3 = (f32[56,128]{1,0:T(8,128)S(1)}, f32[56,128]{1,0:T(8,128)}, u32[]{:S(2)}) copy-start(f32[56,128]{1,0:T(8,128)} %copy-done.2) | copy-start | bytes 86020
  13.1 31.7 %collective-permute-start.2 = (f32[336,128]{1,0:T(8,128)S(1)}, f32[336,128]{1,0:T(8,128)S(1)}, u32[]{:S(2)}, u32[]{:S(2)}) collective-permute-start(f32[336,128]{1,0:T(8,128)S(1)} %pad_maximum_fusion), channel_id=1, source_target_pairs={{0,1},{1,0},{2,3},{3,2},{4,5},{5,4},{6,7},{7,6},{8,9},{9,8},{10,11... | collective-permute-start | bytes 516104 | tf_op jit(solution)/shard_map/ppermute | solution.py:298
  44.8 11.2 %collective-permute-start.3 = (f32[336,128]{1,0:T(8,128)S(1)}, f32[336,128]{1,0:T(8,128)S(1)}, u32[]{:S(2)}, u32[]{:S(2)}) collective-permute-start(f32[336,128]{1,0:T(8,128)S(1)} %collective-permute-done.2.pair_ref), channel_id=1, source_target_pairs={{0,2},{2,4},{4,6},{3,1},{5,3},{7,5},{8,10},{10,12},{12,14},{11,9},... | collective-permute-start | bytes 516104 | tf_op jit(solution)/shard_map/ppermute | solution.py:301
  48.7 4.3 %collective-permute-start.4 = (f32[32,128]{1,0:T(8,128)S(1)}, f32[32,128]{1,0:T(8,128)S(1)}, u32[]{:S(2)}, u32[]{:S(2)}) collective-permute-start(f32[32,128]{1,0:T(8,128)S(1)} %get-tuple-element.16), channel_id=1, source_target_pairs={{0,64},{64,128},{128,192},{192,256},{256,320},{320,384},{384,448},... | collective-permute-start | bytes 49160 | tf_op jit(solution)/shard_map/ppermute | solution.py:312
  51.0 5.1 %collective-permute-start.5 = (f32[32,128]{1,0:T(8,128)S(1)}, f32[32,128]{1,0:T(8,128)S(1)}, u32[]{:S(2)}, u32[]{:S(2)}) collective-permute-start(f32[32,128]{1,0:T(8,128)S(1)} %get-tuple-element.17), channel_id=1, source_target_pairs={{64,0},{128,64},{192,128},{256,192},{320,256},{384,320},{448,384},... | collective-permute-start | bytes 49160 | tf_op jit(solution)/shard_map/ppermute | solution.py:313
  56.0 10.6 %copy-start.1 = (bf16[4,64,512]{2,1,0:T(8,128)(2,1)S(1)}, bf16[4,64,512]{2,1,0:T(8,128)(2,1)}, u32[]{:S(2)}) copy-start(bf16[4,64,512]{2,1,0:T(8,128)(2,1)} %outer_ref.3) | copy-start | bytes 786436
  56.5 6.4 %collective-permute-start.6 = (f32[32,128]{1,0:T(8,128)S(1)}, f32[32,128]{1,0:T(8,128)S(1)}, u32[]{:S(2)}, u32[]{:S(2)}) collective-permute-start(f32[32,128]{1,0:T(8,128)S(1)} %get-tuple-element.19), channel_id=1, source_target_pairs={{0,8},{8,16},{16,24},{24,32},{32,40},{40,48},{48,56},{56,0},{1,9},... | collective-permute-start | bytes 49160 | tf_op jit(solution)/shard_map/ppermute | solution.py:322
  60.9 5.7 %collective-permute-start.7 = (f32[32,128]{1,0:T(8,128)S(1)}, f32[32,128]{1,0:T(8,128)S(1)}, u32[]{:S(2)}, u32[]{:S(2)}) collective-permute-start(f32[32,128]{1,0:T(8,128)S(1)} %get-tuple-element.20), channel_id=1, source_target_pairs={{0,56},{8,0},{16,8},{24,16},{32,24},{40,32},{48,40},{56,48},{1,57}... | collective-permute-start | bytes 49160 | tf_op jit(solution)/shard_map/ppermute | solution.py:323

commit v2 on v1

--- a/solution.py
+++ b/solution.py
@@ -1,5 +1,3 @@
-import functools
-
 import jax
 import jax.numpy as jnp
 from jax import lax
@@ -17,9 +15,23 @@
 COL = 128
 DEEP = 12
 TALL = 24
-OWN = 16 * ROW
-NEAR = 40
-STRIP = 56
+ANY = pl.BlockSpec(memory_space=pl.ANY)
+HBM = pl.BlockSpec(memory_space=pltpu.HBM)
+PLANES = [(1, 0), (2, 0), (3, 0), (0, 0)]
+PLANES += [(f, l) for l in (1, 2) for f in range(4)]
+PLANES += [(0, 3), (1, 3), (2, 3), (3, 3)]
+OWN = len(PLANES) * ROW
+FAR = OWN - 3 * ROW
+
+
+def reach(f, off):
+    return max(0, (4 if f == 0 else 3) - off)
+
+
+STRIP = [(p, i) for i in range(4) for p, (f, l) in enumerate(PLANES) if i < reach(f, 1 + min(l, 3 - l))]
+NEAR = -(-len(STRIP) // 8) * 8
+STRIP += [(p, i) for i in range(4) for p, (f, l) in enumerate(PLANES) if i < reach(f, 0) and (p, i) not in STRIP]
+TALLY = -(-len(STRIP) // 8) * 8
 
 
 def column_table(wide, narrow, wide_axis):
@@ -29,28 +41,33 @@
     return (fine == coarse).astype(F32).astype(BF16)
 
 
-def coarse_kernel(outer_ref, courant_ref, block_ref, up_ref, down_ref, sums_ref):
+def coarse_kernel(outer_hbm, courant_hbm, block_ref, up_ref, down_ref, outer_ref, courant_ref, sums_ref, sems):
+    copies = [
+        pltpu.make_async_copy(outer_hbm, outer_ref, sems.at[0]),
+        pltpu.make_async_copy(courant_hbm, courant_ref, sems.at[1]),
+    ]
+    for copy in copies:
+        copy.start()
+    table = column_table(COL * 4, COL, 0)
+    copies[1].wait()
+    for p, (f, l) in enumerate(PLANES):
+        if f > 0:
+            block_ref[ROW * p : ROW * p + ROW, :] = courant_ref[f - 1, l].astype(F32)
+    copies[0].wait()
     sums_ref[...] = jnp.dot(
-        outer_ref[...].reshape(LEV * ROW * 4, COL * 4),
-        column_table(COL * 4, COL, 0),
-        preferred_element_type=F32,
-    )
-    rows = LEV * ROW
-    total = sums_ref[pl.ds(0, rows, stride=4), :]
-    for part in range(1, 4):
-        total = total + sums_ref[pl.ds(part, rows, stride=4), :]
-    block_ref[0:rows, :] = total * 0.0625
-    block_ref[rows:OWN, :] = courant_ref[...].astype(F32).reshape(OWN - rows, COL)
+        outer_ref[...].reshape(LEV * ROW * 4, COL * 4), table, preferred_element_type=F32
+    )
+    for p, (f, l) in enumerate(PLANES):
+        if f == 0:
+            total = sums_ref[pl.ds(ROW * 4 * l, ROW, stride=4), :]
+            for part in range(1, 4):
+                total = total + sums_ref[pl.ds(ROW * 4 * l + part, ROW, stride=4), :]
+            block_ref[ROW * p : ROW * p + ROW, :] = total * 0.0625
     for ref, edge, step in ((up_ref, ROW - 1, -1), (down_ref, 0, 1)):
-        for i in range(3):
-            ref[4 * i : 4 * i + 4, :] = block_ref[pl.ds(edge + step * i, 4, stride=ROW), :]
-        for i in range(2):
-            ref[12 + 12 * i : 24 + 12 * i, :] = block_ref[
-                pl.ds(rows + edge + step * i, 12, stride=ROW), :
-            ]
-        ref[36:40, :] = jnp.zeros((4, COL), F32)
-        ref[40:44, :] = block_ref[pl.ds(edge + step * 3, 4, stride=ROW), :]
-        ref[44:56, :] = block_ref[pl.ds(rows + edge + step * 2, 12, stride=ROW), :]
+        for at, (p, i) in enumerate(STRIP):
+            row = ROW * p + edge + step * i
+            ref[at : at + 1, :] = block_ref[row : row + 1, :]
+        ref[len(STRIP) : TALLY, :] = jnp.zeros((TALLY - len(STRIP), COL), F32)
 
 
 def obs_kernel(lowest_ref, column_ref, level_ref, value_ref, field_ref, up_ref, down_ref):
@@ -105,12 +122,24 @@
 PACKS = -(-len(EDGES) // 32)
 
 
+def join_kernel(before_ref, after_ref, strips_ref, own_ref):
+    for side, ref in enumerate((before_ref, after_ref)):
+        strips_ref[NEAR * side : NEAR * side + NEAR, :] = ref[0:NEAR, :]
+        own_ref[TALLY * side : TALLY * side + TALLY, :] = ref[...]
+
+
+def forward_kernel(parity_ref, pair_ref, strips_ref, first_ref, second_ref, far_ref):
+    begin = pl.multiple_of((1 - parity_ref[0]) * (3 * ROW), ROW)
+    far_ref[0:FAR, :] = pair_ref[pl.ds(begin, FAR), :]
+    far_ref[FAR:, :] = strips_ref[...]
+
+
 def gather_kernel(
     parity_ref,
     block_ref,
-    before_ref,
-    after_ref,
+    own_ref,
     pair_ref,
+    strips_ref,
     far_ref,
     field_ref,
     field_before_ref,
@@ -122,28 +151,23 @@
     odd = parity_ref[0]
     pair_level = (1 - odd) * 8
     far_level = odd * 8
-    rows = LEV * ROW
-    for base, ref in ((4, block_ref), (pair_level, pair_ref), (far_level, far_ref)):
-        for f in range(4):
-            for l in range(LEV):
-                begin = (f * LEV + l) * ROW
-                all_ref[f, base + l, 0:ROW, :] = ref[begin : begin + ROW, :]
-    for side, (own, offset) in enumerate(((before_ref, OWN), (after_ref, OWN + NEAR))):
-        for base, ref, start, reach in (
-            (4, own, 0, 4),
-            (pair_level, pair_ref, offset, 3),
-            (far_level, far_ref, offset, 3),
-        ):
-            for f in range(4):
-                for i in range(reach if f == 0 else reach - 1):
-                    if f == 0:
-                        begin = 4 * i if i < 3 else 40
-                    else:
-                        begin = (12 + 12 * i if i < 2 else 44) + (f - 1) * 4
-                    row = TALL - 1 - i if side == 0 else ROW + i
-                    for l in range(LEV):
-                        at = start + begin + l
-                        all_ref[f, base + l, row : row + 1, :] = ref[at : at + 1, :]
+    for p, (f, l) in enumerate(PLANES):
+        begin = ROW * p
+        all_ref[f, 4 + l, 0:ROW, :] = block_ref[begin : begin + ROW, :]
+        all_ref[f, pair_level + l, 0:ROW, :] = pair_ref[begin : begin + ROW, :]
+        begin = pl.multiple_of(jnp.clip(begin - (1 - odd) * (3 * ROW), 0, FAR - ROW), ROW)
+        all_ref[f, far_level + l, 0:ROW, :] = far_ref[pl.ds(begin, ROW), :]
+    for side in range(2):
+        for at, (p, i) in enumerate(STRIP):
+            f, l = PLANES[p]
+            row = TALL - 1 - i if side == 0 else ROW + i
+            begin = TALLY * side + at
+            all_ref[f, 4 + l, row : row + 1, :] = own_ref[begin : begin + 1, :]
+            if at < NEAR and i < reach(f, 1 + min(l, 3 - l)):
+                at += NEAR * side
+                all_ref[f, pair_level + l, row : row + 1, :] = strips_ref[at : at + 1, :]
+                at += FAR
+                all_ref[f, far_level + l, row : row + 1, :] = far_ref[at : at + 1, :]
     for f in range(2):
         for l in range(8):
             begin = (f * 8 + l) * ROW
@@ -255,13 +279,13 @@
         next_ref[:, :, cut] = result.astype(BF16)
 
 
-def call(kernel, outs, ins, scratch=(), scalars=0, flops=1000000, name=None):
+def call(kernel, outs, ins, scratch=(), scalars=0, places={}, flops=1000000, name=None):
     single = len(outs) == 1
     shapes = [jax.ShapeDtypeStruct(shape, kind) for shape, kind in outs]
     return pl.pallas_call(
         kernel,
         out_shape=shapes[0] if single else shapes,
-        in_specs=[SMEM] * scalars + [VMEM] * (len(ins) - scalars),
+        in_specs=[SMEM if i < scalars else places.get(i, VMEM) for i in range(len(ins))],
         out_specs=VMEM if single else [VMEM] * len(outs),
         scratch_shapes=list(scratch),
         compiler_params=pltpu.CompilerParams(vmem_limit_bytes=16 * 1024 * 1024),
@@ -288,17 +312,27 @@
 
     block, up, down = call(
         coarse_kernel,
-        [((OWN, COL), F32), ((STRIP, COL), F32), ((STRIP, COL), F32)],
+        [((OWN, COL), F32), ((TALLY, COL), F32), ((TALLY, COL), F32)],
         [outer_increment, courant],
-        [pltpu.VMEM((LEV * ROW * 4, COL), F32)],
+        [
+            pltpu.VMEM(outer_increment.shape, BF16),
+            pltpu.VMEM(courant.shape, BF16),
+            pltpu.VMEM((LEV * ROW * 4, COL), F32),
+            pltpu.SemaphoreType.DMA((2,)),
+        ],
+        places={0: HBM, 1: HBM},
         name="coarse",
     )
+    pair = lax.ppermute(block, "lev", pairs)
     before = lax.ppermute(up, "lat", lat_up)
     after = lax.ppermute(down, "lat", lat_down)
-    pair = lax.ppermute(
-        jnp.concatenate([block, before[:NEAR], after[:NEAR]], axis=0), "lev", pairs
-    )
-    far_block = lax.ppermute(pair, "lev", far)
+    near, own = call(
+        join_kernel,
+        [((2 * NEAR, COL), F32), ((2 * TALLY, COL), F32)],
+        [before, after],
+        name="join",
+    )
+    strips = lax.ppermute(near, "lev", pairs)
 
     count = obs_column.shape[0]
     fields, fields_up, fields_down = call(
@@ -312,10 +346,19 @@
     fields_before = lax.ppermute(fields_up, "lat", lat_up)
     fields_after = lax.ppermute(fields_down, "lat", lat_down)
 
+    onward = call(
+        forward_kernel,
+        [((FAR + 2 * NEAR, COL), F32)],
+        [parity, pair, strips, fields_before, fields_after],
+        scalars=1,
+        places={3: ANY, 4: ANY},
+        name="forward",
+    )
+    far_block = lax.ppermute(onward, "lev", far)
     everything, right, left = call(
         gather_kernel,
         [((6, DEEP, TALL, COL), F32), ((8 * PACKS, COL), F32), ((8 * PACKS, COL), F32)],
-        [parity, block, before, after, pair, far_block, fields, fields_before, fields_after],
+        [parity, block, own, pair, strips, far_block, fields, fields_before, fields_after],
         scalars=1,
         name="assemble",
     )

time: 68.9 us -> 69.9 us (1.015)
  the two profiles are of different devices: /device:TPU:25 before, /device:TPU:92 now
where the time goes in v2:
time: 69.9 us; the launch traced here: 69.5 us
  starting transfers between devices  41.6 us (60%)
  waiting for transfers between devices  21.9 us (31%)
  Pallas kernels  3.4 us (5%)
  local copies, waits for them, and re-layouts  1.76 us (3%)
  between operations  0.8 us (1%)
    ppermute x1, starting transfers between devices, shards(): pair = lax.ppermute(block, 'lev', pairs)  18.5 us
    ppermute x1, waiting for transfers between devices, shards(): before = lax.ppermute(up, 'lat', lat_up)  5.74 us
    ppermute x1, waiting for transfers between devices, shards(): strips = lax.ppermute(near, 'lev', pairs)  5.37 us
    ppermute x1, waiting for transfers between devices, shards(): east = lax.ppermute(left, 'lon', lon_down)  4.9 us
    ppermute x1, starting transfers between devices, shards(): west = lax.ppermute(right, 'lon', lon_up)  4.75 us
    ppermute x1, waiting for transfers between devices, shards(): far_block = lax.ppermute(onward, 'lev', far)  4.29 us
    ppermute x1, starting transfers between devices, shards(): fields_before = lax.ppermute(fields_up, 'lat', lat_up)  3.98 us
    ppermute x1, starting transfers between devices, shards(): after = lax.ppermute(down, 'lat', lat_down)  3.64 us
  transfers between devices with their start and end apart: 9, of which 6 were waited for; matrix products, arithmetic and copies ran while one was open for 0% of the time, Pallas kernels for 1%

profile of v2, /device:TPU:92, one launch (start us, length us, event | category | flops | bytes accessed | tf_op | source)
XLA Modules:
  0.0 69.5 jit_solution(5484394062635269222)
XLA Ops:
  0.6 0.0 copy-start
  0.6 0.9 %copy-done = bf16[4,64,512]{2,1,0:T(8,128)(2,1)S(1)} copy-done((bf16[4,64,512]{2,1,0:T(8,128)(2,1)S(1)}, bf16[4,64,512]{2,1,0:T(8,128)(2,1)}, u32[]{:S(2)}) %copy-start) | copy-done | bytes 262168
  1.6 0.0 copy-start.2
  1.6 0.8 %copy-done.2 = bf16[3,4,16,128]{3,2,1,0:T(8,128)(2,1)S(1)} copy-done((bf16[3,4,16,128]{3,2,1,0:T(8,128)(2,1)S(1)}, bf16[3,4,16,128]{3,2,1,0:T(8,128)(2,1)}, u32[]{:S(2)}) %copy-start.2) | copy-done | bytes 49176
  2.4 0.4 coarse.1
  2.8 18.5 %collective-permute-start.2 = (f32[256,128]{1,0:T(8,128)S(1)}, f32[256,128]{1,0:T(8,128)S(1)}, u32[]{:S(2)}, u32[]{:S(2)}) collective-permute-start(f32[256,128]{1,0:T(8,128)S(1)} %get-tuple-element.14.block_ref), channel_id=1, source_target_pairs={{0,1},{1,0},{2,3},{3,2},{4,5},{5,4},{6,7},{7,6},{8,9},{9,8},{10,11... | collective-permute-start | bytes 393224 | tf_op jit(solution)/shard_map/ppermute | solution.py:326
  21.3 1.9 %collective-permute-start = (f32[56,128]{1,0:T(8,128)S(1)}, f32[56,128]{1,0:T(8,128)S(1)}, u32[]{:S(2)}, u32[]{:S(2)}) collective-permute-start(f32[56,128]{1,0:T(8,128)S(1)} %get-tuple-element.15), channel_id=1, source_target_pairs={{0,64},{64,128},{128,192},{192,256},{256,320},{320,384},{384,448},... | collective-permute-start | bytes 86024 | tf_op jit(solution)/shard_map/ppermute | solution.py:327
  23.2 3.6 %collective-permute-start.1 = (f32[56,128]{1,0:T(8,128)S(1)}, f32[56,128]{1,0:T(8,128)S(1)}, u32[]{:S(2)}, u32[]{:S(2)}) collective-permute-start(f32[56,128]{1,0:T(8,128)S(1)} %get-tuple-element.16), channel_id=1, source_target_pairs={{64,0},{128,64},{192,128},{256,192},{320,256},{384,320},{448,384},... | collective-permute-start | bytes 86024 | tf_op jit(solution)/shard_map/ppermute | solution.py:328
  26.8 5.7 %collective-permute-done.before_ref = f32[56,128]{1,0:T(8,128)S(1)} collective-permute-done((f32[56,128]{1,0:T(8,128)S(1)}, f32[56,128]{1,0:T(8,128)S(1)}, u32[]{:S(2)}, u32[]{:S(2)}) %collective-permute-start) | collective-permute-done | bytes 28704 | tf_op jit(solution)/shard_map/ppermute | solution.py:327
  32.6 0.2 collective-permute-done.1.after_ref
  32.8 0.0 copy-start.5
  32.8 0.0 copy-start.4
  32.8 0.0 copy-start.3
  32.8 1.9 %collective-permute-start.3 = (f32[64,128]{1,0:T(8,128)S(1)}, f32[64,128]{1,0:T(8,128)S(1)}, u32[]{:S(2)}, u32[]{:S(2)}) collective-permute-start(f32[64,128]{1,0:T(8,128)S(1)} %get-tuple-element.18), channel_id=1, source_target_pairs={{0,1},{1,0},{2,3},{3,2},{4,5},{5,4},{6,7},{7,6},{8,9},{9,8},{10,11... | collective-permute-start | bytes 98312 | tf_op jit(solution)/shard_map/ppermute | solution.py:335
  34.7 0.0 copy-done.5
  34.7 0.0 copy-done.4
  34.7 0.0 copy-done.3
  34.8 0.7 %observe.1 = (f32[256,128]{1,0:T(8,128)S(1)}, f32[32,128]{1,0:T(8,128)S(1)}, f32[32,128]{1,0:T(8,128)S(1)}) custom-call(s32[1]{0:T(128)} %bitcast.1.lowest_ref, s32[1,2048]{1,0:T(1,128)S(1)} %bitcast.5, s32[1,2048]{1,0:T(1,128)S(1)} %bitcast.6, f32[1,2048]{1,0:T(1,128)S(1)} %bitcast.7), custom_call_target="tpu_custom_call" | custom-call | flops 1000000 | bytes 500000 | tf_op jit(solution)/shard_map/observe/pallas_call | solution.py:285
  35.5 4.0 %collective-permute-start.4 = (f32[32,128]{1,0:T(8,128)S(1)}, f32[32,128]{1,0:T(8,128)S(1)}, u32[]{:S(2)}, u32[]{:S(2)}) collective-permute-start(f32[32,128]{1,0:T(8,128)S(1)} %get-tuple-element.19), channel_id=1, source_target_pairs={{0,64},{64,128},{128,192},{192,256},{256,320},{320,384},{384,448},... | collective-permute-start | bytes 49160 | tf_op jit(solution)/shard_map/ppermute | solution.py:346
  39.5 1.9 %collective-permute-start.5 = (f32[32,128]{1,0:T(8,128)S(1)}, f32[32,128]{1,0:T(8,128)S(1)}, u32[]{:S(2)}, u32[]{:S(2)}) collective-permute-start(f32[32,128]{1,0:T(8,128)S(1)} %get-tuple-element.20), channel_id=1, source_target_pairs={{64,0},{128,64},{192,128},{256,192},{320,256},{384,320},{448,384},... | collective-permute-start | bytes 49160 | tf_op jit(solution)/shard_map/ppermute | solution.py:347
  41.4 0.0 collective-permute-done.4.first_ref.field_before_ref
  41.4 1.4 %collective-permute-done.5.second_ref.field_after_ref = f32[32,128]{1,0:T(8,128)S(1)} collective-permute-done((f32[32,128]{1,0:T(8,128)S(1)}, f32[32,128]{1,0:T(8,128)S(1)}, u32[]{:S(2)}, u32[]{:S(2)}) %collective-permute-start.5) | collective-permute-done | bytes 16416 | tf_op jit(solution)/shard_map/ppermute | solution.py:347
  42.8 5.4 %collective-permute-done.3.strips_ref = f32[64,128]{1,0:T(8,128)S(1)} collective-permute-done((f32[64,128]{1,0:T(8,128)S(1)}, f32[64,128]{1,0:T(8,128)S(1)}, u32[]{:S(2)}, u32[]{:S(2)}) %collective-permute-start.3) | collective-permute-done | bytes 32800 | tf_op jit(solution)/shard_map/ppermute | solution.py:335
  48.2 0.0 collective-permute-done.2.pair_ref
  48.2 3.1 %collective-permute-start.6 = (f32[272,128]{1,0:T(8,128)S(1)}, f32[272,128]{1,0:T(8,128)S(1)}, u32[]{:S(2)}, u32[]{:S(2)}) collective-permute-start(f32[272,128]{1,0:T(8,128)S(1)} %forward.1), channel_id=1, source_target_pairs={{0,2},{2,4},{4,6},{3,1},{5,3},{7,5},{8,10},{10,12},{12,14},{11,9},... | collective-permute-start | bytes 417800 | tf_op jit(solution)/shard_map/ppermute | solution.py:357
  51.3 4.3 %collective-permute-done.6.far_ref = f32[272,128]{1,0:T(8,128)S(1)} collective-permute-done((f32[272,128]{1,0:T(8,128)S(1)}, f32[272,128]{1,0:T(8,128)S(1)}, u32[]{:S(2)}, u32[]{:S(2)}) %collective-permute-start.6) | collective-permute-done | bytes 139296 | tf_op jit(solution)/shard_map/ppermute | solution.py:357
  55.6 0.0 copy-start.1
  55.6 0.5 assemble.1
  56.1 4.7 %collective-permute-start.7 = (f32[32,128]{1,0:T(8,128)S(1)}, f32[32,128]{1,0:T(8,128)S(1)}, u32[]{:S(2)}, u32[]{:S(2)}) collective-permute-start(f32[32,128]{1,0:T(8,128)S(1)} %get-tuple-element.23), channel_id=1, source_target_pairs={{0,8},{8,16},{16,24},{24,32},{32,40},{40,48},{48,56},{56,0},{1,9},... | collective-permute-start | bytes 49160 | tf_op jit(solution)/shard_map/ppermute | solution.py:365
  60.8 1.9 %collective-permute-start.8 = (f32[32,128]{1,0:T(8,128)S(1)}, f32[32,128]{1,0:T(8,128)S(1)}, u32[]{:S(2)}, u32[]{:S(2)}) collective-permute-start(f32[32,128]{1,0:T(8,128)S(1)} %get-tuple-element.24), channel_id=1, source_target_pairs={{0,56},{8,0},{16,8},{24,16},{32,24},{40,32},{48,40},{56,48},{1,57}... | collective-permute-start | bytes 49160 | tf_op jit(solution)/shard_map/ppermute | solution.py:366
  62.8 0.0 collective-permute-done.7.west_ref
  62.8 4.9 %collective-permute-done.8.east_ref = f32[32,128]{1,0:T(8,128)S(1)} collective-permute-done((f32[32,128]{1,0:T(8,128)S(1)}, f32[32,128]{1,0:T(8,128)S(1)}, u32[]{:S(2)}, u32[]{:S(2)}) %collective-permute-start.8) | collective-permute-done | bytes 16416 | tf_op jit(solution)/shard_map/ppermute | solution.py:366
  67.7 0.0 copy-done.1
  67.7 1.8 %steps.1 = (f32[4,16,128]{2,1,0:T(8,128)}, f32[4,16,128]{2,1,0:T(8,128)}, bf16[4,64,512]{2,1,0:T(8,128)(2,1)}) custom-call(f32[6,12,24,128]{3,2,1,0:T(8,128)S(1)} %get-tuple-element.22.all_ref, f32[32,128]{1,0:T(8,128)S(1)} %collective-permute-done.7.west_ref, f32[32,128]{1,0:T(8,128)S(1)} %collective-permute-done.8.east_ref, bf16[4,64,512]{2,1,0:T(8,128)(2,1)S(1)} %copy-done.1), custom_call_target="tpu_custom_call" | custom-call | flops 1000000 | bytes 500000 | tf_op jit(solution)/shard_map/steps/pallas_call | solution.py:285
  (2 shorter events, 0.0 us)
Async XLA Ops:
  0.6 1.0 %copy-start = (bf16[4,64,512]{2,1,0:T(8,128)(2,1)S(1)}, bf16[4,64,512]{2,1,0:T(8,128)(2,1)}, u32[]{:S(2)}) copy-start(bf16[4,64,512]{2,1,0:T(8,128)(2,1)} %outer_ref.1) | copy-start | bytes 786436
  1.6 0.8 %copy-start.2 = (bf16[3,4,16,128]{3,2,1,0:T(8,128)(2,1)S(1)}, bf16[3,4,16,128]{3,2,1,0:T(8,128)(2,1)}, u32[]{:S(2)}) copy-start(bf16[3,4,16,128]{3,2,1,0:T(8,128)(2,1)} %courant_hbm.1) | copy-start | bytes 147460
  2.8 45.4 %collective-permute-start.2 = (f32[256,128]{1,0:T(8,128)S(1)}, f32[256,128]{1,0:T(8,128)S(1)}, u32[]{:S(2)}, u32[]{:S(2)}) collective-permute-start(f32[256,128]{1,0:T(8,128)S(1)} %get-tuple-element.14.block_ref), channel_id=1, source_target_pairs={{0,1},{1,0},{2,3},{3,2},{4,5},{5,4},{6,7},{7,6},{8,9},{9,8},{10,11... | collective-permute-start | bytes 393224 | tf_op jit(solution)/shard_map/ppermute | solution.py:326
  21.3 11.3 %collective-permute-start = (f32[56,128]{1,0:T(8,128)S(1)}, f32[56,128]{1,0:T(8,128)S(1)}, u32[]{:S(2)}, u32[]{:S(2)}) collective-permute-start(f32[56,128]{1,0:T(8,128)S(1)} %get-tuple-element.15), channel_id=1, source_target_pairs={{0,64},{64,128},{128,192},{192,256},{256,320},{320,384},{384,448},... | collective-permute-start | bytes 86024 | tf_op jit(solution)/shard_map/ppermute | solution.py:327
  23.2 9.6 %collective-permute-start.1 = (f32[56,128]{1,0:T(8,128)S(1)}, f32[56,128]{1,0:T(8,128)S(1)}, u32[]{:S(2)}, u32[]{:S(2)}) collective-permute-start(f32[56,128]{1,0:T(8,128)S(1)} %get-tuple-element.16), channel_id=1, source_target_pairs={{64,0},{128,64},{192,128},{256,192},{320,256},{384,320},{448,384},... | collective-permute-start | bytes 86024 | tf_op jit(solution)/shard_map/ppermute | solution.py:328
  32.8 2.0 %copy-start.5 = (f32[2048]{0:T(1024)S(1)}, f32[2048]{0:T(1024)}, u32[]{:S(2)}) copy-start(f32[2048]{0:T(1024)} %param.9) | copy-start | bytes 24580
  32.8 2.0 %copy-start.4 = (s32[2048]{0:T(1024)S(1)}, s32[2048]{0:T(1024)}, u32[]{:S(2)}) copy-start(s32[2048]{0:T(1024)} %param.8) | copy-start | bytes 24580
  32.8 2.0 %copy-start.3 = (s32[2048]{0:T(1024)S(1)}, s32[2048]{0:T(1024)}, u32[]{:S(2)}) copy-start(s32[2048]{0:T(1024)} %param.7) | copy-start | bytes 24580
  32.8 15.4 %collective-permute-start.3 = (f32[64,128]{1,0:T(8,128)S(1)}, f32[64,128]{1,0:T(8,128)S(1)}, u32[]{:S(2)}, u32[]{:S(2)}) collective-permute-start(f32[64,128]{1,0:T(8,128)S(1)} %get-tuple-element.18), channel_id=1, source_target_pairs={{0,1},{1,0},{2,3},{3,2},{4,5},{5,4},{6,7},{7,6},{8,9},{9,8},{10,11... | collective-permute-start | bytes 98312 | tf_op jit(solution)/shard_map/ppermute | solution.py:335
  35.5 5.9 %collective-permute-start.4 = (f32[32,128]{1,0:T(8,128)S(1)}, f32[32,128]{1,0:T(8,128)S(1)}, u32[]{:S(2)}, u32[]{:S(2)}) collective-permute-start(f32[32,128]{1,0:T(8,128)S(1)} %get-tuple-element.19), channel_id=1, source_target_pairs={{0,64},{64,128},{128,192},{192,256},{256,320},{320,384},{384,448},... | collective-permute-start | bytes 49160 | tf_op jit(solution)/shard_map/ppermute | solution.py:346
  39.5 3.4 %collective-permute-start.5 = (f32[32,128]{1,0:T(8,128)S(1)}, f32[32,128]{1,0:T(8,128)S(1)}, u32[]{:S(2)}, u32[]{:S(2)}) collective-permute-start(f32[32,128]{1,0:T(8,128)S(1)} %get-tuple-element.20), channel_id=1, source_target_pairs={{64,0},{128,64},{192,128},{256,192},{320,256},{384,320},{448,384},... | collective-permute-start | bytes 49160 | tf_op jit(solution)/shard_map/ppermute | solution.py:347
  48.2 7.4 %collective-permute-start.6 = (f32[272,128]{1,0:T(8,128)S(1)}, f32[272,128]{1,0:T(8,128)S(1)}, u32[]{:S(2)}, u32[]{:S(2)}) collective-permute-start(f32[272,128]{1,0:T(8,128)S(1)} %forward.1), channel_id=1, source_target_pairs={{0,2},{2,4},{4,6},{3,1},{5,3},{7,5},{8,10},{10,12},{12,14},{11,9},... | collective-permute-start | bytes 417800 | tf_op jit(solution)/shard_map/ppermute | solution.py:357
  55.6 12.1 %copy-start.1 = (bf16[4,64,512]{2,1,0:T(8,128)(2,1)S(1)}, bf16[4,64,512]{2,1,0:T(8,128)(2,1)}, u32[]{:S(2)}) copy-start(bf16[4,64,512]{2,1,0:T(8,128)(2,1)} %outer_ref.1) | copy-start | bytes 786436
  56.1 6.7 %collective-permute-start.7 = (f32[32,128]{1,0:T(8,128)S(1)}, f32[32,128]{1,0:T(8,128)S(1)}, u32[]{:S(2)}, u32[]{:S(2)}) collective-permute-start(f32[32,128]{1,0:T(8,128)S(1)} %get-tuple-element.23), channel_id=1, source_target_pairs={{0,8},{8,16},{16,24},{24,32},{32,40},{40,48},{48,56},{56,0},{1,9},... | collective-permute-start | bytes 49160 | tf_op jit(solution)/shard_map/ppermute | solution.py:365
  60.8 6.8 %collective-permute-start.8 = (f32[32,128]{1,0:T(8,128)S(1)}, f32[32,128]{1,0:T(8,128)S(1)}, u32[]{:S(2)}, u32[]{:S(2)}) collective-permute-start(f32[32,128]{1,0:T(8,128)S(1)} %get-tuple-element.24), channel_id=1, source_target_pairs={{0,56},{8,0},{16,8},{24,16},{32,24},{40,32},{48,40},{56,48},{1,57}... | collective-permute-start | bytes 49160 | tf_op jit(solution)/shard_map/ppermute | solution.py:366

commit v3 on v2

v3 whole, which is shorter than its diff:
```python
import jax
import jax.numpy as jnp
from jax import lax
from jax.experimental import pallas as pl
from jax.experimental.pallas import tpu as pltpu
from jax.sharding import PartitionSpec as P

F32 = jnp.float32
BF16 = jnp.bfloat16
VMEM = pl.BlockSpec(memory_space=pltpu.VMEM)
SMEM = pl.BlockSpec(memory_space=pltpu.SMEM)

LEV = 4
ROW = 16
COL = 128
DEEP = 12
TALL = 24
ANY = pl.BlockSpec(memory_space=pl.ANY)
HBM = pl.BlockSpec(memory_space=pltpu.HBM)
PLANES = [(1, 0), (2, 0), (3, 0), (0, 0)]
PLANES += [(f, l) for l in (1, 2) for f in range(4)]
PLANES += [(0, 3), (1, 3), (2, 3), (3, 3)]
OWN = len(PLANES) * ROW
FAR = OWN - 3 * ROW


def reach(f, off):
    return max(0, (4 if f == 0 else 3) - off)


STRIP = [(p, i) for i in range(4) for p, (f, l) in enumerate(PLANES) if i < reach(f, 1 + min(l, 3 - l))]
NEAR = -(-len(STRIP) // 8) * 8
STRIP += [(p, i) for i in range(4) for p, (f, l) in enumerate(PLANES) if i < reach(f, 0) and (p, i) not in STRIP]
TALLY = -(-len(STRIP) // 8) * 8
EDGE = TALLY + 32


def column_table(wide, narrow, wide_axis):
    shape = (wide, narrow) if wide_axis == 0 else (narrow, wide)
    fine = lax.broadcasted_iota(jnp.int32, shape, wide_axis) >> 2
    coarse = lax.broadcasted_iota(jnp.int32, shape, 1 - wide_axis)
    return (fine == coarse).astype(F32).astype(BF16)


def prepare_kernel(
    lowest_ref,
    outer_hbm,
    courant_hbm,
    column_hbm,
    level_hbm,
    value_hbm,
    block_ref,
    field_ref,
    up_ref,
    down_ref,
    outer_ref,
    courant_ref,
    column_ref,
    level_ref,
    value_ref,
    sums_ref,
    sems,
):
    copies = [
        pltpu.make_async_copy(source, target, sems.at[i])
        for i, (source, target) in enumerate(
            (
                (outer_hbm, outer_ref),
                (courant_hbm, courant_ref),
                (column_hbm, column_ref),
                (level_hbm, level_ref),
                (value_hbm, value_ref),
            )
        )
    ]
    for copy in copies:
        copy.start()
    table = column_table(COL * 4, COL, 0)
    copies[1].wait()
    for p, (f, l) in enumerate(PLANES):
        if f > 0:
            block_ref[ROW * p : ROW * p + ROW, :] = courant_ref[f - 1, l].astype(F32)
    for i in (2, 3, 4):
        copies[i].wait()
    observe(lowest_ref[0], column_ref, level_ref, value_ref, field_ref)
    copies[0].wait()
    sums_ref[...] = jnp.dot(
        outer_ref[...].reshape(LEV * ROW * 4, COL * 4), table, preferred_element_type=F32
    )
    for p, (f, l) in enumerate(PLANES):
        if f == 0:
            total = sums_ref[pl.ds(ROW * 4 * l, ROW, stride=4), :]
            for part in range(1, 4):
                total = total + sums_ref[pl.ds(ROW * 4 * l + part, ROW, stride=4), :]
            block_ref[ROW * p : ROW * p + ROW, :] = total * 0.0625
    for ref, edge, step in ((up_ref, ROW - 1, -1), (down_ref, 0, 1)):
        for at, (p, i) in enumerate(STRIP):
            row = ROW * p + edge + step * i
            ref[at : at + 1, :] = block_ref[row : row + 1, :]
        ref[len(STRIP) : TALLY, :] = jnp.zeros((TALLY - len(STRIP), COL), F32)
        for i in range(2):
            begin = TALLY + 16 * i
            ref[begin : begin + 16, :] = field_ref[pl.ds(edge + step * i, 16, stride=ROW), :]


def observe(lowest, column_ref, level_ref, value_ref, field_ref):
    count = column_ref.shape[1]
    chunk = 512
    total = jnp.zeros((4 * COL, COL), F32)
    for begin in range(0, count, chunk):
        cut = slice(begin, begin + chunk)
        cell = column_ref[:, cut]
        place = (level_ref[:, cut] - lowest + 2) * ROW + (cell >> 7)
        value = value_ref[:, cut]
        high = value.astype(BF16).astype(F32)
        rest = value - high
        middle = rest.astype(BF16).astype(F32)
        low = rest - middle
        index = lax.broadcasted_iota(jnp.int32, (COL, chunk), 0)
        here = index == place
        across = jnp.where(index == (cell & 127), 1.0, 0.0).astype(BF16)
        down = jnp.concatenate(
            [jnp.where(here, part, 0.0).astype(BF16) for part in (1.0, high, middle, low)], axis=0
        )
        total = total + lax.dot_general(
            down, across, (((1,), (1,)), ((), ())), preferred_element_type=F32
        )
    field_ref[0:128, :] = total[0:128]
    field_ref[128:256, :] = (total[128:256] + total[256:384]) + total[384:512]


def tile_table():
    own = [(f, l, part) for f in range(4) for l in range(LEV) for part in range(3)]
    first = [(f, l, part) for f, l, part in own if part < 2 or reach(f, 1 + min(l, 3 - l)) > 1]
    tiles = first + [tile for tile in own if tile not in first]
    for f in (4, 5):
        for l in range(1, 7):
            tiles += [(f, l, part) for part in range(3 if 2 <= l < 6 else 2)]
    return tiles, len(first)


TILES, SENT_ON = tile_table()
PACKS = -(-len(TILES) // 32) * 8
ON = -(-SENT_ON // 32) * 8
MORE = 2 * NEAR + 2 * ON


def edges_kernel(block_ref, field_ref, before_ref, after_ref, own_ref, obs_ref, near_ref, right_ref, left_ref):
    for p, (f, l) in enumerate(PLANES):
        own_ref[f, l, 0:ROW, :] = block_ref[ROW * p : ROW * p + ROW, :]
    for f in range(2):
        for l in range(8):
            begin = (f * 8 + l) * ROW
            obs_ref[f, l, 0:ROW, :] = field_ref[begin : begin + ROW, :]
    for side, ref in enumerate((before_ref, after_ref)):
        near_ref[NEAR * side : NEAR * side + NEAR, :] = ref[0:NEAR, :]
        for at, (p, i) in enumerate(STRIP):
            f, l = PLANES[p]
            row = TALL - 1 - i if side == 0 else ROW + i
            own_ref[f, l, row : row + 1, :] = ref[at : at + 1, :]
        for i in range(2):
            row = TALL - 1 - i if side == 0 else ROW + i
            for plane in range(16):
                at = TALLY + 16 * i + plane
                obs_ref[plane // 8, plane % 8, row : row + 1, :] = ref[at : at + 1, :]
    group = lax.broadcasted_iota(jnp.int32, (8, COL), 1) >> 2
    for pack in range(0, PACKS, 8):
        right = jnp.zeros((8, COL), F32)
        left = jnp.zeros((8, COL), F32)
        for slot, (f, l, part) in enumerate(TILES[4 * pack : 4 * pack + 32]):
            ref, f = (own_ref, f) if f < 4 else (obs_ref, f - 4)
            tile = ref[f, l, 8 * part : 8 * part + 8, :]
            right = jnp.where(group == slot, turn(tile, 4 * slot + 4, 1), right)
            left = jnp.where(group == slot, turn(tile, 4 * slot, 1), left)
        right_ref[pack : pack + 8, :] = right
        left_ref[pack : pack + 8, :] = left


def turn(tile, shift, axis):
    shift = shift % tile.shape[axis]
    return pltpu.roll(tile, shift, axis) if shift else tile


def join_kernel(near_ref, west_ref, east_ref, more_ref):
    more_ref[0 : 2 * NEAR, :] = near_ref[...]
    more_ref[2 * NEAR : 2 * NEAR + ON, :] = west_ref[0:ON, :]
    more_ref[2 * NEAR + ON : MORE, :] = east_ref[0:ON, :]


def forward_kernel(parity_ref, pair_ref, more_ref, far_ref):
    begin = pl.multiple_of((1 - parity_ref[0]) * (3 * ROW), ROW)
    far_ref[0:FAR, :] = pair_ref[pl.ds(begin, FAR), :]
    far_ref[FAR:, :] = more_ref[...]


def place_strips(wide_ref, base, ref, start):
    for side in range(2):
        for at, (p, i) in enumerate(STRIP[:NEAR]):
            f, l = PLANES[p]
            if i < reach(f, 1 + min(l, 3 - l)):
                row = TALL - 1 - i if side == 0 else ROW + i
                at += start + NEAR * side
                wide_ref[f, base + l, row : row + 1, 0:COL] = ref[at : at + 1, :]


def place_edges(wide_ref, base, tiles, west, east):
    half = lax.broadcasted_iota(jnp.int32, (8, COL), 1) < 64
    for slot, (f, l, part) in enumerate(tiles):
        pack, lane = divmod(slot, 32)
        level = base + l if f < 4 else 2 + l
        wide_ref[f, level, 8 * part : 8 * part + 8, COL : 2 * COL] = jnp.where(
            half, turn(east(8 * pack), -4 * lane, 1), turn(west(8 * pack), -4 * lane - 4, 1)
        )


def place_more(wide_ref, base, ref, start):
    place_strips(wide_ref, base, ref, start)
    west = start + 2 * NEAR
    place_edges(
        wide_ref,
        base,
        TILES[:SENT_ON],
        lambda row: ref[west + row : west + row + 8, :],
        lambda row: ref[west + ON + row : west + ON + row + 8, :],
    )


def assemble_kernel(parity_ref, own_ref, obs_ref, west_ref, east_ref, pair_ref, more_ref, wide_ref):
    wide_ref[0:4, 4:8, :, 0:COL] = own_ref[...]
    wide_ref[4:6, 2:10, :, 0:COL] = obs_ref[...]
    place_edges(
        wide_ref,
        4,
        TILES,
        lambda row: west_ref[row : row + 8, :],
        lambda row: east_ref[row : row + 8, :],
    )
    base = (1 - parity_ref[0]) * 8
    for p, (f, l) in enumerate(PLANES):
        wide_ref[f, base + l, 0:ROW, 0:COL] = pair_ref[ROW * p : ROW * p + ROW, :]
    place_more(wide_ref, base, more_ref, 0)


def step_kernel(
    parity_ref,
    given_ref,
    far_ref,
    outer_ref,
    state_ref,
    adjoint_ref,
    next_ref,
    wide_ref,
    first_ref,
    force_ref,
    back_ref,
    flat_ref,
    spread_ref,
):
    wide_ref[...] = given_ref[...]
    odd = parity_ref[0]
    for p, (f, l) in enumerate(PLANES):
        begin = pl.multiple_of(jnp.clip(ROW * p - (1 - odd) * (3 * ROW), 0, FAR - ROW), ROW)
        wide_ref[f, odd * 8 + l, 0:ROW, 0:COL] = far_ref[pl.ds(begin, ROW), :]
    place_more(wide_ref, odd * 8, far_ref, FAR)

    def plus(x):
        return jnp.maximum(x, 0.0)

    def centre(level):
        return 1.0 - (
            jnp.abs(wide_ref[1, level]) + jnp.abs(wide_ref[2, level]) + jnp.abs(wide_ref[3, level])
        )

    def advance(get, level):
        here = get(level)
        c0, c1, c2 = (wide_ref[1 + k, level] for k in range(3))
        result = centre(level) * here
        result = result + plus(c0) * get(level - 1) + plus(-c0) * get(level + 1)
        result = result + plus(c1) * turn(here, 1, 0) + plus(-c1) * turn(here, -1, 0)
        return result + plus(c2) * turn(here, 1, 1) + plus(-c2) * turn(here, -1, 1)

    def retreat(get, level):
        here = get(level)
        c1, c2 = (wide_ref[2 + k, level] for k in range(2))
        result = centre(level) * here
        result = (
            result
            + plus(wide_ref[1, level + 1]) * get(level + 1)
            + plus(-wide_ref[1, level - 1]) * get(level - 1)
        )
        result = result + turn(plus(c1) * here, -1, 0) + turn(plus(-c1) * here, 1, 0)
        return result + turn(plus(c2) * here, -1, 1) + turn(plus(-c2) * here, 1, 1)

    for level in range(1, 11):
        first_ref[level] = advance(lambda l: wide_ref[0, l], level)
    for level in range(2, 10):
        state = advance(lambda l: first_ref[l], level)
        if 4 <= level < 8:
            state_ref[level - 4] = state[0:ROW, 0:COL]
        force_ref[level] = wide_ref[4, level] * state - wide_ref[5, level]
    for level in range(3, 9):
        back_ref[level] = retreat(lambda l: force_ref[l], level)
    for level in range(4, 8):
        result = retreat(lambda l: back_ref[l], level)[0:ROW, 0:COL]
        adjoint_ref[level - 4] = result
        flat_ref[ROW * (level - 4) : ROW * (level - 3), :] = result
    flat = flat_ref[...]
    high = flat.astype(BF16)
    rest = flat - high.astype(F32)
    middle = rest.astype(BF16)
    low = (rest - middle.astype(F32)).astype(BF16)
    table = column_table(COL * 4, COL, 1)
    spread = jnp.dot(high, table, preferred_element_type=F32)
    spread = spread + jnp.dot(middle, table, preferred_element_type=F32)
    spread = spread + jnp.dot(low, table, preferred_element_type=F32)
    for tile in range(4):
        cut = slice(COL * tile, COL * tile + COL)
        for part in range(4):
            spread_ref[pl.ds(part, LEV * ROW, stride=4), :] = spread[:, cut]
        outer = outer_ref[:, :, cut].astype(F32).reshape(LEV * ROW * 4, COL)
        result = (outer - spread_ref[...]).reshape(LEV, ROW * 4, COL)
        next_ref[:, :, cut] = result.astype(BF16)


def call(kernel, outs, ins, scratch=(), scalars=0, places={}, cost=500000, name=None):
    single = len(outs) == 1
    shapes = [jax.ShapeDtypeStruct(shape, kind) for shape, kind in outs]
    return pl.pallas_call(
        kernel,
        out_shape=shapes[0] if single else shapes,
        in_specs=[SMEM if i < scalars else places.get(i, VMEM) for i in range(len(ins))],
        out_specs=VMEM if single else [VMEM] * len(outs),
        scratch_shapes=list(scratch),
        compiler_params=pltpu.CompilerParams(vmem_limit_bytes=16 * 1024 * 1024),
        cost_estimate=pl.CostEstimate(flops=cost, bytes_accessed=cost, transcendentals=0),
        name=name,
    )(*ins)


def shift(size, by, wrap):
    return [
        (i, (i + by) % size) for i in range(size) if wrap or 0 <= i + by < size
    ]


def shards(outer_increment, courant, obs_column, obs_level, obs_value):
    lev = lax.axis_size("lev")
    lat_up, lat_down = (shift(lax.axis_size("lat"), by, False) for by in (1, -1))
    lon_up, lon_down = (shift(lax.axis_size("lon"), by, True) for by in (1, -1))
    pairs = [(i, i ^ 1) for i in range(lev)]
    far = [(i, i + 2) for i in range(0, lev - 2, 2)] + [(i, i - 2) for i in range(3, lev, 2)]
    position = lax.axis_index("lev").astype(jnp.int32)
    parity = (position & 1).reshape(1)
    lowest = (position * LEV).reshape(1)

    count = obs_column.shape[0]
    given = [outer_increment, courant]
    given += [array.reshape(1, count) for array in (obs_column, obs_level, obs_value)]
    block, fields, up, down = call(
        prepare_kernel,
        [((OWN, COL), F32), ((OWN, COL), F32), ((EDGE, COL), F32), ((EDGE, COL), F32)],
        [lowest] + [pltpu.with_memory_space_constraint(array, pltpu.HBM) for array in given],
        [pltpu.VMEM(array.shape, array.dtype) for array in given]
        + [pltpu.VMEM((LEV * ROW * 4, COL), F32), pltpu.SemaphoreType.DMA((5,))],
        scalars=1,
        places={i: HBM for i in range(1, 6)},
        name="prepare",
    )
    before = lax.ppermute(up, "lat", lat_up)
    after = lax.ppermute(down, "lat", lat_down)
    pair = lax.ppermute(block, "lev", pairs)
    own, obs, near, right, left = call(
        edges_kernel,
        [
            ((4, LEV, TALL, COL), F32),
            ((2, 8, TALL, COL), F32),
            ((2 * NEAR, COL), F32),
            ((PACKS, COL), F32),
            ((PACKS, COL), F32),
        ],
        [block, fields, before, after],
        cost=500000000,
        name="edges",
    )
    west = lax.ppermute(right, "lon", lon_up)
    east = lax.ppermute(left, "lon", lon_down)
    more = lax.ppermute(
        call(join_kernel, [((MORE, COL), F32)], [near, west, east], cost=500000000, name="join"), "lev", pairs
    )
    onward = call(
        forward_kernel, [((FAR + MORE, COL), F32)], [parity, pair, more], scalars=1, name="forward"
    )
    far_block = lax.ppermute(onward, "lev", far)
    tall = (DEEP, TALL, 2 * COL)
    wide = call(
        assemble_kernel,
        [((6,) + tall, F32)],
        [parity, own, obs, west, east, pair, more],
        scalars=1,
        cost=1000000,
        name="assemble",
    )
    state, adjoint, outer_next = call(
        step_kernel,
        [
            ((LEV, ROW, COL), F32),
            ((LEV, ROW, COL), F32),
            (outer_increment.shape, BF16),
        ],
        [parity, wide, far_block, outer_increment],
        [
            pltpu.VMEM((6,) + tall, F32),
            pltpu.VMEM(tall, F32),
            pltpu.VMEM(tall, F32),
            pltpu.VMEM(tall, F32),
            pltpu.VMEM((LEV * ROW, COL), F32),
            pltpu.VMEM((LEV * ROW * 4, COL), F32),
        ],
        scalars=1,
        name="steps",
    )
    return state, adjoint, outer_next


def solution(mesh):
    placed = (
        P("lev", "lat", "lon"),
        P(None, "lev", "lat", "lon"),
        P(("lat", "lon")),
        P(("lat", "lon")),
        P(("lat", "lon")),
    )
    return jax.shard_map(
        shards,
        mesh=mesh,
        in_specs=placed,
        out_specs=(P("lev", "lat", "lon"), P("lev", "lat", "lon"), P("lev", "lat", "lon")),
        check_vma=False,
    )
```

time: 69.9 us -> 62.8 us (0.90)
  the two profiles are of different devices: /device:TPU:92 before, /device:TPU:30 now
where the time goes in v3:
time: 62.8 us; the launch traced here: 62.5 us
  starting transfers between devices  33.5 us (53%)
  waiting for transfers between devices  23.9 us (38%)
  Pallas kernels  4.37 us (7%)
  between operations  0.75 us (1%)
    ppermute x1, starting transfers between devices, shards(): pair = lax.ppermute(block, 'lev', pairs)  19.4 us
    ppermute x1, waiting for transfers between devices, shards(): lax.ppermute(call(join_kernel, [((MORE, COL), F32)], [near, west, east],...  13 us
    ppermute x1, waiting for transfers between devices, shards(): far_block = lax.ppermute(onward, 'lev', far)  6.04 us
    ppermute x1, waiting for transfers between devices, shards(): east = lax.ppermute(left, 'lon', lon_down)  4.86 us
    ppermute x1, starting transfers between devices, shards(): west = lax.ppermute(right, 'lon', lon_up)  4.7 us
    pallas_call x6, Pallas kernels, call(): pl.pallas_call(kernel, out_shape=shapes[0] if single else shapes, in_spec...  4.37 us
    ppermute x1, starting transfers between devices, shards(): lax.ppermute(call(join_kernel, [((MORE, COL), F32)], [near, west, east],...  3.17 us
    ppermute x1, starting transfers between devices, shards(): east = lax.ppermute(left, 'lon', lon_down)  1.92 us
  transfers between devices with their start and end apart: 7, of which 3 were waited for; matrix products, arithmetic and copies ran while one was open for 0% of the time, Pallas kernels for 1%

profile of v3, /device:TPU:30, one launch (start us, length us, event | category | flops | bytes accessed | tf_op | source)
XLA Modules:
  0.0 62.5 jit_solution(6713013730880666622)
XLA Ops:
  0.6 2.0 %prepare.1 = (f32[256,128]{1,0:T(8,128)S(1)}, f32[256,128]{1,0:T(8,128)S(1)}, f32[88,128]{1,0:T(8,128)S(1)}, f32[88,128]{1,0:T(8,128)S(1)}) custom-call(s32[1]{0:T(128)} %bitcast.1.lowest_ref, bf16[4,64,512]{2,1,0:T(8,128)(2,1)} %outer_ref.1, bf16[3,4,16,128]{3,2,1,0:T(8,128)(2,1)} %courant_hbm.1, s32[1,2048]{1,0:T(1,128)} %bitcast.5, s32[1,2048]{1,0:T(1,128)} %bitcast.6, ...), custom_call_target="tpu_custom_call" | custom-call | flops 500000 | bytes 500000 | tf_op jit(solution)/shard_map/prepare/pallas_call | solution.py:328
  2.7 1.7 %collective-permute-start = (f32[88,128]{1,0:T(8,128)S(1)}, f32[88,128]{1,0:T(8,128)S(1)}, u32[]{:S(2)}, u32[]{:S(2)}) collective-permute-start(f32[88,128]{1,0:T(8,128)S(1)} %get-tuple-element.14), channel_id=1, source_target_pairs={{0,64},{64,128},{128,192},{192,256},{256,320},{320,384},{384,448},... | collective-permute-start | bytes 135176 | tf_op jit(solution)/shard_map/ppermute | solution.py:369
  4.4 1.3 %collective-permute-start.1 = (f32[88,128]{1,0:T(8,128)S(1)}, f32[88,128]{1,0:T(8,128)S(1)}, u32[]{:S(2)}, u32[]{:S(2)}) collective-permute-start(f32[88,128]{1,0:T(8,128)S(1)} %get-tuple-element.15), channel_id=1, source_target_pairs={{64,0},{128,64},{192,128},{256,192},{320,256},{384,320},{448,384},... | collective-permute-start | bytes 135176 | tf_op jit(solution)/shard_map/ppermute | solution.py:370
  5.7 19.4 %collective-permute-start.4 = (f32[256,128]{1,0:T(8,128)S(1)}, f32[256,128]{1,0:T(8,128)S(1)}, u32[]{:S(2)}, u32[]{:S(2)}) collective-permute-start(f32[256,128]{1,0:T(8,128)S(1)} %get-tuple-element.12.block_ref), channel_id=1, source_target_pairs={{0,1},{1,0},{2,3},{3,2},{4,5},{5,4},{6,7},{7,6},{8,9},{9,8},{10,11... | collective-permute-start | bytes 393224 | tf_op jit(solution)/shard_map/ppermute | solution.py:371
  25.1 0.0 collective-permute-done.before_ref
  25.1 0.0 collective-permute-done.1.after_ref
  25.1 0.2 edges.1
  25.4 4.7 %collective-permute-start.2 = (f32[24,128]{1,0:T(8,128)S(1)}, f32[24,128]{1,0:T(8,128)S(1)}, u32[]{:S(2)}, u32[]{:S(2)}) collective-permute-start(f32[24,128]{1,0:T(8,128)S(1)} %get-tuple-element.18), channel_id=1, source_target_pairs={{0,8},{8,16},{16,24},{24,32},{32,40},{40,48},{48,56},{56,0},{1,9},... | collective-permute-start | bytes 36872 | tf_op jit(solution)/shard_map/ppermute | solution.py:385
  30.1 1.9 %collective-permute-start.3 = (f32[24,128]{1,0:T(8,128)S(1)}, f32[24,128]{1,0:T(8,128)S(1)}, u32[]{:S(2)}, u32[]{:S(2)}) collective-permute-start(f32[24,128]{1,0:T(8,128)S(1)} %get-tuple-element.19), channel_id=1, source_target_pairs={{0,56},{8,0},{16,8},{24,16},{32,24},{40,32},{48,40},{56,48},{1,57}... | collective-permute-start | bytes 36872 | tf_op jit(solution)/shard_map/ppermute | solution.py:386
  32.0 0.0 collective-permute-done.2.west_ref
  32.0 4.9 %collective-permute-done.3.east_ref = f32[24,128]{1,0:T(8,128)S(1)} collective-permute-done((f32[24,128]{1,0:T(8,128)S(1)}, f32[24,128]{1,0:T(8,128)S(1)}, u32[]{:S(2)}, u32[]{:S(2)}) %collective-permute-start.3) | collective-permute-done | bytes 12320 | tf_op jit(solution)/shard_map/ppermute | solution.py:386
  36.9 0.0 copy-start
  36.9 3.2 %collective-permute-start.5 = (f32[96,128]{1,0:T(8,128)S(1)}, f32[96,128]{1,0:T(8,128)S(1)}, u32[]{:S(2)}, u32[]{:S(2)}) collective-permute-start(f32[96,128]{1,0:T(8,128)S(1)} %join.1), channel_id=1, source_target_pairs={{0,1},{1,0},{2,3},{3,2},{4,5},{5,4},{6,7},{7,6},{8,9},{9,8},{10,11... | collective-permute-start | bytes 147464 | tf_op jit(solution)/shard_map/ppermute | solution.py:387
  40.1 13.0 %collective-permute-done.5.more_ref = f32[96,128]{1,0:T(8,128)S(1)} collective-permute-done((f32[96,128]{1,0:T(8,128)S(1)}, f32[96,128]{1,0:T(8,128)S(1)}, u32[]{:S(2)}, u32[]{:S(2)}) %collective-permute-start.5) | collective-permute-done | bytes 49184 | tf_op jit(solution)/shard_map/ppermute | solution.py:387
  53.0 0.0 collective-permute-done.4.pair_ref
  53.0 1.3 %collective-permute-start.6 = (f32[304,128]{1,0:T(8,128)S(1)}, f32[304,128]{1,0:T(8,128)S(1)}, u32[]{:S(2)}, u32[]{:S(2)}) collective-permute-start(f32[304,128]{1,0:T(8,128)S(1)} %forward.1), channel_id=1, source_target_pairs={{0,2},{2,4},{4,6},{3,1},{5,3},{7,5},{8,10},{10,12},{12,14},{11,9},... | collective-permute-start | bytes 466952 | tf_op jit(solution)/shard_map/ppermute | solution.py:393
  54.4 0.3 assemble.1.given_ref
  54.7 6.0 %collective-permute-done.6.far_ref = f32[304,128]{1,0:T(8,128)S(1)} collective-permute-done((f32[304,128]{1,0:T(8,128)S(1)}, f32[304,128]{1,0:T(8,128)S(1)}, u32[]{:S(2)}, u32[]{:S(2)}) %collective-permute-start.6) | collective-permute-done | bytes 155680 | tf_op jit(solution)/shard_map/ppermute | solution.py:393
  60.7 0.0 copy-done
  60.7 1.7 %steps.1 = (f32[4,16,128]{2,1,0:T(8,128)}, f32[4,16,128]{2,1,0:T(8,128)}, bf16[4,64,512]{2,1,0:T(8,128)(2,1)}) custom-call(s32[1]{0:T(128)} %bitcast.parity_ref, f32[6,12,24,256]{3,2,1,0:T(8,128)S(1)} %assemble.1.given_ref, f32[304,128]{1,0:T(8,128)S(1)} %collective-permute-done.6.far_ref, bf16[4,64,512]{2,1,0:T(8,128)(2,1)S(1)} %copy-done), custom_call_target="tpu_custom_call" | custom-call | flops 500000 | bytes 500000 | tf_op jit(solution)/shard_map/steps/pallas_call | solution.py:328
  (2 shorter events, 0.0 us)
Async XLA Ops:
  2.7 22.4 %collective-permute-start = (f32[88,128]{1,0:T(8,128)S(1)}, f32[88,128]{1,0:T(8,128)S(1)}, u32[]{:S(2)}, u32[]{:S(2)}) collective-permute-start(f32[88,128]{1,0:T(8,128)S(1)} %get-tuple-element.14), channel_id=1, source_target_pairs={{0,64},{64,128},{128,192},{192,256},{256,320},{320,384},{384,448},... | collective-permute-start | bytes 135176 | tf_op jit(solution)/shard_map/ppermute | solution.py:369
  4.4 20.7 %collective-permute-start.1 = (f32[88,128]{1,0:T(8,128)S(1)}, f32[88,128]{1,0:T(8,128)S(1)}, u32[]{:S(2)}, u32[]{:S(2)}) collective-permute-start(f32[88,128]{1,0:T(8,128)S(1)} %get-tuple-element.15), channel_id=1, source_target_pairs={{64,0},{128,64},{192,128},{256,192},{320,256},{384,320},{448,384},... | collective-permute-start | bytes 135176 | tf_op jit(solution)/shard_map/ppermute | solution.py:370
  5.7 47.3 %collective-permute-start.4 = (f32[256,128]{1,0:T(8,128)S(1)}, f32[256,128]{1,0:T(8,128)S(1)}, u32[]{:S(2)}, u32[]{:S(2)}) collective-permute-start(f32[256,128]{1,0:T(8,128)S(1)} %get-tuple-element.12.block_ref), channel_id=1, source_target_pairs={{0,1},{1,0},{2,3},{3,2},{4,5},{5,4},{6,7},{7,6},{8,9},{9,8},{10,11... | collective-permute-start | bytes 393224 | tf_op jit(solution)/shard_map/ppermute | solution.py:371
  25.4 6.6 %collective-permute-start.2 = (f32[24,128]{1,0:T(8,128)S(1)}, f32[24,128]{1,0:T(8,128)S(1)}, u32[]{:S(2)}, u32[]{:S(2)}) collective-permute-start(f32[24,128]{1,0:T(8,128)S(1)} %get-tuple-element.18), channel_id=1, source_target_pairs={{0,8},{8,16},{16,24},{24,32},{32,40},{40,48},{48,56},{56,0},{1,9},... | collective-permute-start | bytes 36872 | tf_op jit(solution)/shard_map/ppermute | solution.py:385
  30.1 6.8 %collective-permute-start.3 = (f32[24,128]{1,0:T(8,128)S(1)}, f32[24,128]{1,0:T(8,128)S(1)}, u32[]{:S(2)}, u32[]{:S(2)}) collective-permute-start(f32[24,128]{1,0:T(8,128)S(1)} %get-tuple-element.19), channel_id=1, source_target_pairs={{0,56},{8,0},{16,8},{24,16},{32,24},{40,32},{48,40},{56,48},{1,57}... | collective-permute-start | bytes 36872 | tf_op jit(solution)/shard_map/ppermute | solution.py:386
  36.9 23.8 %copy-start = (bf16[4,64,512]{2,1,0:T(8,128)(2,1)S(1)}, bf16[4,64,512]{2,1,0:T(8,128)(2,1)}, u32[]{:S(2)}) copy-start(bf16[4,64,512]{2,1,0:T(8,128)(2,1)} %outer_ref.1) | copy-start | bytes 786436
  36.9 16.1 %collective-permute-start.5 = (f32[96,128]{1,0:T(8,128)S(1)}, f32[96,128]{1,0:T(8,128)S(1)}, u32[]{:S(2)}, u32[]{:S(2)}) collective-permute-start(f32[96,128]{1,0:T(8,128)S(1)} %join.1), channel_id=1, source_target_pairs={{0,1},{1,0},{2,3},{3,2},{4,5},{5,4},{6,7},{7,6},{8,9},{9,8},{10,11... | collective-permute-start | bytes 147464 | tf_op jit(solution)/shard_map/ppermute | solution.py:387
  53.0 7.7 %collective-permute-start.6 = (f32[304,128]{1,0:T(8,128)S(1)}, f32[304,128]{1,0:T(8,128)S(1)}, u32[]{:S(2)}, u32[]{:S(2)}) collective-permute-start(f32[304,128]{1,0:T(8,128)S(1)} %forward.1), channel_id=1, source_target_pairs={{0,2},{2,4},{4,6},{3,1},{5,3},{7,5},{8,10},{10,12},{12,14},{11,9},... | collective-permute-start | bytes 466952 | tf_op jit(solution)/shard_map/ppermute | solution.py:393

commit v4 on v3

--- a/solution.py
+++ b/solution.py
@@ -33,6 +33,10 @@
 STRIP += [(p, i) for i in range(4) for p, (f, l) in enumerate(PLANES) if i < reach(f, 0) and (p, i) not in STRIP]
 TALLY = -(-len(STRIP) // 8) * 8
 EDGE = TALLY + 32
+CORNERS = EDGE // 8
+CORNER_AT = 2 * NEAR
+SIDE_AT = CORNER_AT + 16
+MORE = SIDE_AT + 16
 
 
 def column_table(wide, narrow, wide_axis):
@@ -51,8 +55,8 @@
     value_hbm,
     block_ref,
     field_ref,
-    up_ref,
-    down_ref,
+    right_ref,
+    left_ref,
     outer_ref,
     courant_ref,
     column_ref,
@@ -93,14 +97,16 @@
             for part in range(1, 4):
                 total = total + sums_ref[pl.ds(ROW * 4 * l + part, ROW, stride=4), :]
             block_ref[ROW * p : ROW * p + ROW, :] = total * 0.0625
-    for ref, edge, step in ((up_ref, ROW - 1, -1), (down_ref, 0, 1)):
-        for at, (p, i) in enumerate(STRIP):
-            row = ROW * p + edge + step * i
-            ref[at : at + 1, :] = block_ref[row : row + 1, :]
-        ref[len(STRIP) : TALLY, :] = jnp.zeros((TALLY - len(STRIP), COL), F32)
-        for i in range(2):
-            begin = TALLY + 16 * i
-            ref[begin : begin + 16, :] = field_ref[pl.ds(edge + step * i, 16, stride=ROW), :]
+    group = lax.broadcasted_iota(jnp.int32, (8, COL), 1) >> 2
+    for pack, (ref, begins) in enumerate(((block_ref, BLOCK_TILES), (field_ref, FIELD_TILES))):
+        right = jnp.zeros((8, COL), F32)
+        left = jnp.zeros((8, COL), F32)
+        for slot, begin in enumerate(begins):
+            tile = ref[begin : begin + 8, :]
+            right = jnp.where(group == slot, turn(tile, 4 * slot + 4, 1), right)
+            left = jnp.where(group == slot, turn(tile, 4 * slot, 1), left)
+        right_ref[8 * pack : 8 * pack + 8, :] = right
+        left_ref[8 * pack : 8 * pack + 8, :] = left
 
 
 def observe(lowest, column_ref, level_ref, value_ref, field_ref):
@@ -129,116 +135,147 @@
     field_ref[128:256, :] = (total[128:256] + total[256:384]) + total[384:512]
 
 
-def tile_table():
-    own = [(f, l, part) for f in range(4) for l in range(LEV) for part in range(3)]
-    first = [(f, l, part) for f, l, part in own if part < 2 or reach(f, 1 + min(l, 3 - l)) > 1]
-    tiles = first + [tile for tile in own if tile not in first]
-    for f in (4, 5):
-        for l in range(1, 7):
-            tiles += [(f, l, part) for part in range(3 if 2 <= l < 6 else 2)]
-    return tiles, len(first)
-
-
-TILES, SENT_ON = tile_table()
-PACKS = -(-len(TILES) // 32) * 8
-ON = -(-SENT_ON // 32) * 8
-MORE = 2 * NEAR + 2 * ON
-
-
-def edges_kernel(block_ref, field_ref, before_ref, after_ref, own_ref, obs_ref, near_ref, right_ref, left_ref):
+BLOCK_TILES = [8 * t for t in range(OWN // 8)]
+FIELD_TILES = [(8 * f + l) * ROW + 8 * part for f in range(2) for l in range(1, 7) for part in range(2)]
+
+
+def turn(tile, shift, axis):
+    shift = shift % tile.shape[axis]
+    return pltpu.roll(tile, shift, axis) if shift else tile
+
+
+def beyond(east, west, slot):
+    half = lax.broadcasted_iota(jnp.int32, (8, COL), 1) < 64
+    return jnp.where(half, turn(east, -4 * slot, 1), turn(west, -4 * slot - 4, 1))
+
+
+def strips_kernel(block_ref, field_ref, west_ref, east_ref, up_ref, down_ref, side_ref, strip_ref):
+    for pack, begins in enumerate((BLOCK_TILES, FIELD_TILES)):
+        rows = slice(8 * pack, 8 * pack + 8)
+        east, west = east_ref[rows, :], west_ref[rows, :]
+        for slot, begin in enumerate(begins):
+            begin += OWN * pack
+            side_ref[begin : begin + 8, :] = beyond(east, west, slot)
+    group = lax.broadcasted_iota(jnp.int32, (8, COL), 1) >> 3
+    for ref, edge, step in ((up_ref, ROW - 1, -1), (down_ref, 0, 1)):
+        for at, (p, i) in enumerate(STRIP):
+            row = ROW * p + edge + step * i
+            ref[at : at + 1, :] = block_ref[row : row + 1, :]
+            strip_ref[at : at + 1, :] = side_ref[row : row + 1, :]
+        ref[len(STRIP) : TALLY, :] = jnp.zeros((TALLY - len(STRIP), COL), F32)
+        for i in range(2):
+            begin = TALLY + 16 * i
+            row = edge + step * i
+            ref[begin : begin + 16, :] = field_ref[pl.ds(row, 16, stride=ROW), :]
+            strip_ref[begin : begin + 16, :] = side_ref[pl.ds(OWN + row, 16, stride=ROW), :]
+        corners = jnp.zeros((8, COL), F32)
+        for j in range(CORNERS):
+            tile = strip_ref[8 * j : 8 * j + 8, :]
+            corners = jnp.where(group == j, turn(tile, 8 * j + 4, 1), corners)
+        ref[EDGE:, :] = corners
+
+
+def join_kernel(before_ref, after_ref, west_ref, east_ref, more_ref):
+    for side, (strip, edge) in enumerate(((before_ref, west_ref), (after_ref, east_ref))):
+        more_ref[NEAR * side : NEAR * side + NEAR, :] = strip[0:NEAR, :]
+        begin = CORNER_AT + 8 * side
+        more_ref[begin : begin + 8, :] = strip[EDGE:, :]
+        begin = SIDE_AT + 8 * side
+        more_ref[begin : begin + 8, :] = edge[0:8, :]
+
+
+def forward_kernel(parity_ref, pair_ref, more_ref, far_ref):
+    begin = pl.multiple_of((1 - parity_ref[0]) * (3 * ROW), ROW)
+    far_ref[0:FAR, :] = pair_ref[pl.ds(begin, FAR), :]
+    far_ref[FAR:, :] = more_ref[...]
+
+
+def place_strip(wide_ref, base, side, strips, wanted, get, corners, corner_ref):
+    for j in range(-(-len(strips) // 8)):
+        corner_ref[8 * j : 8 * j + 8, :] = turn(corners, -8 * j - 4, 1)
+    for at, (p, i) in enumerate(strips):
+        f, l = PLANES[p]
+        if i < wanted(f, l):
+            row = TALL - 1 - i if side == 0 else ROW + i
+            wide_ref[f, base + l, row : row + 1, 0:COL] = get(at)
+            wide_ref[f, base + l, row : row + 1, COL : 2 * COL] = corner_ref[at : at + 1, :]
+
+
+def place_more(wide_ref, base, more_ref, corner_ref):
+    for side in range(2):
+        begin = CORNER_AT + 8 * side
+        place_strip(
+            wide_ref,
+            base,
+            side,
+            STRIP[:NEAR],
+            lambda f, l: reach(f, 1 + min(l, 3 - l)),
+            lambda at: more_ref[NEAR * side + at : NEAR * side + at + 1, :],
+            more_ref[begin : begin + 8, :],
+            corner_ref,
+        )
+    place_sides(
+        wide_ref, base, more_ref[SIDE_AT + 8 : SIDE_AT + 16, :], more_ref[SIDE_AT : SIDE_AT + 8, :]
+    )
+
+
+def place_sides(wide_ref, base, east, west):
+    for slot in range(len(BLOCK_TILES)):
+        f, l = PLANES[slot // 2]
+        rows = slice(8 * (slot % 2), 8 * (slot % 2) + 8)
+        wide_ref[f, base + l, rows, COL : 2 * COL] = beyond(east, west, slot)
+
+
+def assemble_kernel(
+    parity_ref,
+    block_ref,
+    field_ref,
+    before_ref,
+    after_ref,
+    west_ref,
+    east_ref,
+    pair_ref,
+    more_ref,
+    wide_ref,
+    corner_ref,
+):
+    base = (1 - parity_ref[0]) * 8
     for p, (f, l) in enumerate(PLANES):
-        own_ref[f, l, 0:ROW, :] = block_ref[ROW * p : ROW * p + ROW, :]
+        rows = slice(ROW * p, ROW * p + ROW)
+        wide_ref[f, 4 + l, 0:ROW, 0:COL] = block_ref[rows, :]
+        wide_ref[f, base + l, 0:ROW, 0:COL] = pair_ref[rows, :]
     for f in range(2):
         for l in range(8):
-            begin = (f * 8 + l) * ROW
-            obs_ref[f, l, 0:ROW, :] = field_ref[begin : begin + ROW, :]
+            begin = (8 * f + l) * ROW
+            wide_ref[4 + f, 2 + l, 0:ROW, 0:COL] = field_ref[begin : begin + ROW, :]
+    place_sides(wide_ref, 4, east_ref[0:8, :], west_ref[0:8, :])
+    for slot, begin in enumerate(FIELD_TILES):
+        plane, row = divmod(begin, ROW)
+        wide_ref[4 + plane // 8, 2 + plane % 8, row : row + 8, COL : 2 * COL] = beyond(
+            east_ref[8:16, :], west_ref[8:16, :], slot
+        )
     for side, ref in enumerate((before_ref, after_ref)):
-        near_ref[NEAR * side : NEAR * side + NEAR, :] = ref[0:NEAR, :]
-        for at, (p, i) in enumerate(STRIP):
-            f, l = PLANES[p]
-            row = TALL - 1 - i if side == 0 else ROW + i
-            own_ref[f, l, row : row + 1, :] = ref[at : at + 1, :]
+        corners = ref[EDGE:, :]
+        place_strip(
+            wide_ref,
+            4,
+            side,
+            STRIP,
+            lambda f, l: 4,
+            lambda at: ref[at : at + 1, :],
+            corners,
+            corner_ref,
+        )
+        for j in range(TALLY // 8, CORNERS):
+            corner_ref[8 * j : 8 * j + 8, :] = turn(corners, -8 * j - 4, 1)
         for i in range(2):
             row = TALL - 1 - i if side == 0 else ROW + i
             for plane in range(16):
                 at = TALLY + 16 * i + plane
-                obs_ref[plane // 8, plane % 8, row : row + 1, :] = ref[at : at + 1, :]
-    group = lax.broadcasted_iota(jnp.int32, (8, COL), 1) >> 2
-    for pack in range(0, PACKS, 8):
-        right = jnp.zeros((8, COL), F32)
-        left = jnp.zeros((8, COL), F32)
-        for slot, (f, l, part) in enumerate(TILES[4 * pack : 4 * pack + 32]):
-            ref, f = (own_ref, f) if f < 4 else (obs_ref, f - 4)
-            tile = ref[f, l, 8 * part : 8 * part + 8, :]
-            right = jnp.where(group == slot, turn(tile, 4 * slot + 4, 1), right)
-            left = jnp.where(group == slot, turn(tile, 4 * slot, 1), left)
-        right_ref[pack : pack + 8, :] = right
-        left_ref[pack : pack + 8, :] = left
-
-
-def turn(tile, shift, axis):
-    shift = shift % tile.shape[axis]
-    return pltpu.roll(tile, shift, axis) if shift else tile
-
-
-def join_kernel(near_ref, west_ref, east_ref, more_ref):
-    more_ref[0 : 2 * NEAR, :] = near_ref[...]
-    more_ref[2 * NEAR : 2 * NEAR + ON, :] = west_ref[0:ON, :]
-    more_ref[2 * NEAR + ON : MORE, :] = east_ref[0:ON, :]
-
-
-def forward_kernel(parity_ref, pair_ref, more_ref, far_ref):
-    begin = pl.multiple_of((1 - parity_ref[0]) * (3 * ROW), ROW)
-    far_ref[0:FAR, :] = pair_ref[pl.ds(begin, FAR), :]
-    far_ref[FAR:, :] = more_ref[...]
-
-
-def place_strips(wide_ref, base, ref, start):
-    for side in range(2):
-        for at, (p, i) in enumerate(STRIP[:NEAR]):
-            f, l = PLANES[p]
-            if i < reach(f, 1 + min(l, 3 - l)):
-                row = TALL - 1 - i if side == 0 else ROW + i
-                at += start + NEAR * side
-                wide_ref[f, base + l, row : row + 1, 0:COL] = ref[at : at + 1, :]
-
-
-def place_edges(wide_ref, base, tiles, west, east):
-    half = lax.broadcasted_iota(jnp.int32, (8, COL), 1) < 64
-    for slot, (f, l, part) in enumerate(tiles):
-        pack, lane = divmod(slot, 32)
-        level = base + l if f < 4 else 2 + l
-        wide_ref[f, level, 8 * part : 8 * part + 8, COL : 2 * COL] = jnp.where(
-            half, turn(east(8 * pack), -4 * lane, 1), turn(west(8 * pack), -4 * lane - 4, 1)
-        )
-
-
-def place_more(wide_ref, base, ref, start):
-    place_strips(wide_ref, base, ref, start)
-    west = start + 2 * NEAR
-    place_edges(
-        wide_ref,
-        base,
-        TILES[:SENT_ON],
-        lambda row: ref[west + row : west + row + 8, :],
-        lambda row: ref[west + ON + row : west + ON + row + 8, :],
-    )
-
-
-def assemble_kernel(parity_ref, own_ref, obs_ref, west_ref, east_ref, pair_ref, more_ref, wide_ref):
-    wide_ref[0:4, 4:8, :, 0:COL] = own_ref[...]
-    wide_ref[4:6, 2:10, :, 0:COL] = obs_ref[...]
-    place_edges(
-        wide_ref,
-        4,
-        TILES,
-        lambda row: west_ref[row : row + 8, :],
-        lambda row: east_ref[row : row + 8, :],
-    )
-    base = (1 - parity_ref[0]) * 8
-    for p, (f, l) in enumerate(PLANES):
-        wide_ref[f, base + l, 0:ROW, 0:COL] = pair_ref[ROW * p : ROW * p + ROW, :]
-    place_more(wide_ref, base, more_ref, 0)
+                place = (4 + plane // 8, 2 + plane % 8, slice(row, row + 1))
+                wide_ref[place + (slice(0, COL),)] = ref[at : at + 1, :]
+                wide_ref[place + (slice(COL, 2 * COL),)] = corner_ref[at : at + 1, :]
+    place_more(wide_ref, base, more_ref, corner_ref)
 
 
 def step_kernel(
@@ -255,13 +292,14 @@
     back_ref,
     flat_ref,
     spread_ref,
+    corner_ref,
 ):
     wide_ref[...] = given_ref[...]
     odd = parity_ref[0]
     for p, (f, l) in enumerate(PLANES):
         begin = pl.multiple_of(jnp.clip(ROW * p - (1 - odd) * (3 * ROW), 0, FAR - ROW), ROW)
         wide_ref[f, odd * 8 + l, 0:ROW, 0:COL] = far_ref[pl.ds(begin, ROW), :]
-    place_more(wide_ref, odd * 8, far_ref, FAR)
+    place_more(wide_ref, odd * 8, far_ref.at[pl.ds(FAR, MORE)], corner_ref)
 
     def plus(x):
         return jnp.maximum(x, 0.0)
@@ -356,9 +394,9 @@
     count = obs_column.shape[0]
     given = [outer_increment, courant]
     given += [array.reshape(1, count) for array in (obs_column, obs_level, obs_value)]
-    block, fields, up, down = call(
+    block, fields, right, left = call(
         prepare_kernel,
-        [((OWN, COL), F32), ((OWN, COL), F32), ((EDGE, COL), F32), ((EDGE, COL), F32)],
+        [((OWN, COL), F32), ((OWN, COL), F32), ((16, COL), F32), ((16, COL), F32)],
         [lowest] + [pltpu.with_memory_space_constraint(array, pltpu.HBM) for array in given],
         [pltpu.VMEM(array.shape, array.dtype) for array in given]
         + [pltpu.VMEM((LEV * ROW * 4, COL), F32), pltpu.SemaphoreType.DMA((5,))],
@@ -366,27 +404,27 @@
         places={i: HBM for i in range(1, 6)},
         name="prepare",
     )
+    west = lax.ppermute(right, "lon", lon_up)
+    east = lax.ppermute(left, "lon", lon_down)
+    pair = lax.ppermute(block, "lev", pairs)
+    up, down = call(
+        strips_kernel,
+        [((EDGE + 8, COL), F32), ((EDGE + 8, COL), F32)],
+        [block, fields, west, east],
+        [pltpu.VMEM((2 * OWN, COL), F32), pltpu.VMEM((EDGE, COL), F32)],
+        cost=2000000000,
+        name="strips",
+    )
     before = lax.ppermute(up, "lat", lat_up)
     after = lax.ppermute(down, "lat", lat_down)
-    pair = lax.ppermute(block, "lev", pairs)
-    own, obs, near, right, left = call(
-        edges_kernel,
-        [
-            ((4, LEV, TALL, COL), F32),
-            ((2, 8, TALL, COL), F32),
-            ((2 * NEAR, COL), F32),
-            ((PACKS, COL), F32),
-            ((PACKS, COL), F32),
-        ],
-        [block, fields, before, after],
-        cost=500000000,
-        name="edges",
-    )
-    west = lax.ppermute(right, "lon", lon_up)
-    east = lax.ppermute(left, "lon", lon_down)
-    more = lax.ppermute(
-        call(join_kernel, [((MORE, COL), F32)], [near, west, east], cost=500000000, name="join"), "lev", pairs
-    )
+    joined = call(
+        join_kernel,
+        [((MORE, COL), F32)],
+        [before, after, west, east],
+        cost=1000,
+        name="join",
+    )
+    more = lax.ppermute(joined, "lev", pairs)
     onward = call(
         forward_kernel, [((FAR + MORE, COL), F32)], [parity, pair, more], scalars=1, name="forward"
     )
@@ -395,7 +433,8 @@
     wide = call(
         assemble_kernel,
         [((6,) + tall, F32)],
-        [parity, own, obs, west, east, pair, more],
+        [parity, block, fields, before, after, west, east, pair, more],
+        [pltpu.VMEM((EDGE, COL), F32)],
         scalars=1,
         cost=1000000,
         name="assemble",
@@ -415,6 +454,7 @@
             pltpu.VMEM(tall, F32),
             pltpu.VMEM((LEV * ROW, COL), F32),
             pltpu.VMEM((LEV * ROW * 4, COL), F32),
+            pltpu.VMEM((EDGE, COL), F32),
         ],
         scalars=1,
         name="steps",

time: 62.8 us -> 66 us (1.051)
  the two profiles are of different devices: /device:TPU:30 before, /device:TPU:98 now
where the time goes in v4:
time: 66 us; the launch traced here: 65.7 us
  starting transfers between devices  36.5 us (55%)
  waiting for transfers between devices  23.9 us (36%)
  Pallas kernels  4.45 us (7%)
  between operations  0.74 us (1%)
    ppermute x1, starting transfers between devices, shards(): pair = lax.ppermute(block, 'lev', pairs)  18.5 us
    ppermute x1, waiting for transfers between devices, shards(): more = lax.ppermute(joined, 'lev', pairs)  15.1 us
    ppermute x1, waiting for transfers between devices, shards(): before = lax.ppermute(up, 'lat', lat_up)  5.42 us
    ppermute x1, starting transfers between devices, shards(): east = lax.ppermute(left, 'lon', lon_down)  4.47 us
    pallas_call x6, Pallas kernels, call(): pl.pallas_call(kernel, out_shape=shapes[0] if single else shapes, in_spec...  4.45 us
    ppermute x1, starting transfers between devices, shards(): after = lax.ppermute(down, 'lat', lat_down)  3.64 us
    ppermute x1, starting transfers between devices, shards(): far_block = lax.ppermute(onward, 'lev', far)  3.4 us
    ppermute x1, waiting for transfers between devices, shards(): far_block = lax.ppermute(onward, 'lev', far)  3.37 us
  transfers between devices with their start and end apart: 7, of which 3 were waited for; matrix products, arithmetic and copies ran while one was open for 0% of the time, Pallas kernels for 1%

profile of v4, /device:TPU:98, one launch (start us, length us, event | category | flops | bytes accessed | tf_op | source)
XLA Modules:
  0.0 65.7 jit_solution(4010733436200867965)
XLA Ops:
  0.6 2.1 %prepare.1 = (f32[256,128]{1,0:T(8,128)S(1)}, f32[256,128]{1,0:T(8,128)S(1)}, f32[16,128]{1,0:T(8,128)S(1)}, f32[16,128]{1,0:T(8,128)S(1)}) custom-call(s32[1]{0:T(128)} %bitcast.1.lowest_ref, bf16[4,64,512]{2,1,0:T(8,128)(2,1)} %outer_ref.1, bf16[3,4,16,128]{3,2,1,0:T(8,128)(2,1)} %courant_hbm.1, s32[1,2048]{1,0:T(1,128)} %bitcast.5, s32[1,2048]{1,0:T(1,128)} %bitcast.6, ...), custom_call_target="tpu_custom_call" | custom-call | flops 500000 | bytes 500000 | tf_op jit(solution)/shard_map/prepare/pallas_call | solution.py:366
  2.7 2.6 %collective-permute-start = (f32[16,128]{1,0:T(8,128)S(1)}, f32[16,128]{1,0:T(8,128)S(1)}, u32[]{:S(2)}, u32[]{:S(2)}) collective-permute-start(f32[16,128]{1,0:T(8,128)S(1)} %get-tuple-element.11), channel_id=1, source_target_pairs={{0,8},{8,16},{16,24},{24,32},{32,40},{40,48},{48,56},{56,0},{1,9},... | collective-permute-start | bytes 24584 | tf_op jit(solution)/shard_map/ppermute | solution.py:407
  5.3 4.5 %collective-permute-start.1 = (f32[16,128]{1,0:T(8,128)S(1)}, f32[16,128]{1,0:T(8,128)S(1)}, u32[]{:S(2)}, u32[]{:S(2)}) collective-permute-start(f32[16,128]{1,0:T(8,128)S(1)} %get-tuple-element.12), channel_id=1, source_target_pairs={{0,56},{8,0},{16,8},{24,16},{32,24},{40,32},{48,40},{56,48},{1,57}... | collective-permute-start | bytes 24584 | tf_op jit(solution)/shard_map/ppermute | solution.py:408
  9.8 18.5 %collective-permute-start.4 = (f32[256,128]{1,0:T(8,128)S(1)}, f32[256,128]{1,0:T(8,128)S(1)}, u32[]{:S(2)}, u32[]{:S(2)}) collective-permute-start(f32[256,128]{1,0:T(8,128)S(1)} %get-tuple-element.9.block_ref), channel_id=1, source_target_pairs={{0,1},{1,0},{2,3},{3,2},{4,5},{5,4},{6,7},{7,6},{8,9},{9,8},{10,11... | collective-permute-start | bytes 393224 | tf_op jit(solution)/shard_map/ppermute | solution.py:409
  28.3 0.0 collective-permute-done.west_ref
  28.3 0.0 collective-permute-done.1.east_ref
  28.3 0.3 strips.1
  28.6 0.0 copy-start
  28.6 2.0 %collective-permute-start.2 = (f32[96,128]{1,0:T(8,128)S(1)}, f32[96,128]{1,0:T(8,128)S(1)}, u32[]{:S(2)}, u32[]{:S(2)}) collective-permute-start(f32[96,128]{1,0:T(8,128)S(1)} %get-tuple-element.13), channel_id=1, source_target_pairs={{0,64},{64,128},{128,192},{192,256},{256,320},{320,384},{384,448},... | collective-permute-start | bytes 147464 | tf_op jit(solution)/shard_map/ppermute | solution.py:418
  30.6 3.6 %collective-permute-start.3 = (f32[96,128]{1,0:T(8,128)S(1)}, f32[96,128]{1,0:T(8,128)S(1)}, u32[]{:S(2)}, u32[]{:S(2)}) collective-permute-start(f32[96,128]{1,0:T(8,128)S(1)} %get-tuple-element.14), channel_id=1, source_target_pairs={{64,0},{128,64},{192,128},{256,192},{320,256},{384,320},{448,384},... | collective-permute-start | bytes 147464 | tf_op jit(solution)/shard_map/ppermute | solution.py:419
  34.3 5.4 %collective-permute-done.2.before_ref = f32[96,128]{1,0:T(8,128)S(1)} collective-permute-done((f32[96,128]{1,0:T(8,128)S(1)}, f32[96,128]{1,0:T(8,128)S(1)}, u32[]{:S(2)}, u32[]{:S(2)}) %collective-permute-start.2) | collective-permute-done | bytes 49184 | tf_op jit(solution)/shard_map/ppermute | solution.py:418
  39.7 0.0 collective-permute-done.3.after_ref
  39.7 1.9 %collective-permute-start.5 = (f32[96,128]{1,0:T(8,128)S(1)}, f32[96,128]{1,0:T(8,128)S(1)}, u32[]{:S(2)}, u32[]{:S(2)}) collective-permute-start(f32[96,128]{1,0:T(8,128)S(1)} %join.1), channel_id=1, source_target_pairs={{0,1},{1,0},{2,3},{3,2},{4,5},{5,4},{6,7},{7,6},{8,9},{9,8},{10,11... | collective-permute-start | bytes 147464 | tf_op jit(solution)/shard_map/ppermute | solution.py:427
  41.7 15.1 %collective-permute-done.5.more_ref = f32[96,128]{1,0:T(8,128)S(1)} collective-permute-done((f32[96,128]{1,0:T(8,128)S(1)}, f32[96,128]{1,0:T(8,128)S(1)}, u32[]{:S(2)}, u32[]{:S(2)}) %collective-permute-start.5) | collective-permute-done | bytes 49184 | tf_op jit(solution)/shard_map/ppermute | solution.py:427
  56.8 0.0 collective-permute-done.4.pair_ref
  56.8 3.4 %collective-permute-start.6 = (f32[304,128]{1,0:T(8,128)S(1)}, f32[304,128]{1,0:T(8,128)S(1)}, u32[]{:S(2)}, u32[]{:S(2)}) collective-permute-start(f32[304,128]{1,0:T(8,128)S(1)} %forward.1), channel_id=1, source_target_pairs={{0,2},{2,4},{4,6},{3,1},{5,3},{7,5},{8,10},{10,12},{12,14},{11,9},... | collective-permute-start | bytes 466952 | tf_op jit(solution)/shard_map/ppermute | solution.py:431
  60.2 0.3 assemble.1.given_ref
  60.6 3.4 %collective-permute-done.6.far_ref = f32[304,128]{1,0:T(8,128)S(1)} collective-permute-done((f32[304,128]{1,0:T(8,128)S(1)}, f32[304,128]{1,0:T(8,128)S(1)}, u32[]{:S(2)}, u32[]{:S(2)}) %collective-permute-start.6) | collective-permute-done | bytes 155680 | tf_op jit(solution)/shard_map/ppermute | solution.py:431
  63.9 0.0 copy-done
  63.9 1.7 %steps.1 = (f32[4,16,128]{2,1,0:T(8,128)}, f32[4,16,128]{2,1,0:T(8,128)}, bf16[4,64,512]{2,1,0:T(8,128)(2,1)}) custom-call(s32[1]{0:T(128)} %bitcast.parity_ref, f32[6,12,24,256]{3,2,1,0:T(8,128)S(1)} %assemble.1.given_ref, f32[304,128]{1,0:T(8,128)S(1)} %collective-permute-done.6.far_ref, bf16[4,64,512]{2,1,0:T(8,128)(2,1)S(1)} %copy-done), custom_call_target="tpu_custom_call" | custom-call | flops 500000 | bytes 500000 | tf_op jit(solution)/shard_map/steps/pallas_call | solution.py:366
  (2 shorter events, 0.0 us)
Async XLA Ops:
  2.7 25.5 %collective-permute-start = (f32[16,128]{1,0:T(8,128)S(1)}, f32[16,128]{1,0:T(8,128)S(1)}, u32[]{:S(2)}, u32[]{:S(2)}) collective-permute-start(f32[16,128]{1,0:T(8,128)S(1)} %get-tuple-element.11), channel_id=1, source_target_pairs={{0,8},{8,16},{16,24},{24,32},{32,40},{40,48},{48,56},{56,0},{1,9},... | collective-permute-start | bytes 24584 | tf_op jit(solution)/shard_map/ppermute | solution.py:407
  5.3 23.0 %collective-permute-start.1 = (f32[16,128]{1,0:T(8,128)S(1)}, f32[16,128]{1,0:T(8,128)S(1)}, u32[]{:S(2)}, u32[]{:S(2)}) collective-permute-start(f32[16,128]{1,0:T(8,128)S(1)} %get-tuple-element.12), channel_id=1, source_target_pairs={{0,56},{8,0},{16,8},{24,16},{32,24},{40,32},{48,40},{56,48},{1,57}... | collective-permute-start | bytes 24584 | tf_op jit(solution)/shard_map/ppermute | solution.py:408
  9.8 47.0 %collective-permute-start.4 = (f32[256,128]{1,0:T(8,128)S(1)}, f32[256,128]{1,0:T(8,128)S(1)}, u32[]{:S(2)}, u32[]{:S(2)}) collective-permute-start(f32[256,128]{1,0:T(8,128)S(1)} %get-tuple-element.9.block_ref), channel_id=1, source_target_pairs={{0,1},{1,0},{2,3},{3,2},{4,5},{5,4},{6,7},{7,6},{8,9},{9,8},{10,11... | collective-permute-start | bytes 393224 | tf_op jit(solution)/shard_map/ppermute | solution.py:409
  28.6 35.4 %copy-start = (bf16[4,64,512]{2,1,0:T(8,128)(2,1)S(1)}, bf16[4,64,512]{2,1,0:T(8,128)(2,1)}, u32[]{:S(2)}) copy-start(bf16[4,64,512]{2,1,0:T(8,128)(2,1)} %outer_ref.1) | copy-start | bytes 786436
  28.6 11.1 %collective-permute-start.2 = (f32[96,128]{1,0:T(8,128)S(1)}, f32[96,128]{1,0:T(8,128)S(1)}, u32[]{:S(2)}, u32[]{:S(2)}) collective-permute-start(f32[96,128]{1,0:T(8,128)S(1)} %get-tuple-element.13), channel_id=1, source_target_pairs={{0,64},{64,128},{128,192},{192,256},{256,320},{320,384},{384,448},... | collective-permute-start | bytes 147464 | tf_op jit(solution)/shard_map/ppermute | solution.py:418
  30.6 9.1 %collective-permute-start.3 = (f32[96,128]{1,0:T(8,128)S(1)}, f32[96,128]{1,0:T(8,128)S(1)}, u32[]{:S(2)}, u32[]{:S(2)}) collective-permute-start(f32[96,128]{1,0:T(8,128)S(1)} %get-tuple-element.14), channel_id=1, source_target_pairs={{64,0},{128,64},{192,128},{256,192},{320,256},{384,320},{448,384},... | collective-permute-start | bytes 147464 | tf_op jit(solution)/shard_map/ppermute | solution.py:419
  39.7 17.1 %collective-permute-start.5 = (f32[96,128]{1,0:T(8,128)S(1)}, f32[96,128]{1,0:T(8,128)S(1)}, u32[]{:S(2)}, u32[]{:S(2)}) collective-permute-start(f32[96,128]{1,0:T(8,128)S(1)} %join.1), channel_id=1, source_target_pairs={{0,1},{1,0},{2,3},{3,2},{4,5},{5,4},{6,7},{7,6},{8,9},{9,8},{10,11... | collective-permute-start | bytes 147464 | tf_op jit(solution)/shard_map/ppermute | solution.py:427
  56.8 7.1 %collective-permute-start.6 = (f32[304,128]{1,0:T(8,128)S(1)}, f32[304,128]{1,0:T(8,128)S(1)}, u32[]{:S(2)}, u32[]{:S(2)}) collective-permute-start(f32[304,128]{1,0:T(8,128)S(1)} %forward.1), channel_id=1, source_target_pairs={{0,2},{2,4},{4,6},{3,1},{5,3},{7,5},{8,10},{10,12},{12,14},{11,9},... | collective-permute-start | bytes 466952 | tf_op jit(solution)/shard_map/ppermute | solution.py:431

commit v5 on v3

--- a/solution.py
+++ b/solution.py
@@ -187,10 +187,10 @@
     more_ref[2 * NEAR + ON : MORE, :] = east_ref[0:ON, :]
 
 
-def forward_kernel(parity_ref, pair_ref, more_ref, far_ref):
+def forward_kernel(parity_ref, pair_ref, later_ref, far_ref):
+    del later_ref
     begin = pl.multiple_of((1 - parity_ref[0]) * (3 * ROW), ROW)
-    far_ref[0:FAR, :] = pair_ref[pl.ds(begin, FAR), :]
-    far_ref[FAR:, :] = more_ref[...]
+    far_ref[...] = pair_ref[pl.ds(begin, FAR), :]
 
 
 def place_strips(wide_ref, base, ref, start):
@@ -245,6 +245,7 @@
     parity_ref,
     given_ref,
     far_ref,
+    far_more_ref,
     outer_ref,
     state_ref,
     adjoint_ref,
@@ -256,12 +257,12 @@
     flat_ref,
     spread_ref,
 ):
-    wide_ref[...] = given_ref[...]
+    wide_ref[...] = given_ref[0:4]
     odd = parity_ref[0]
     for p, (f, l) in enumerate(PLANES):
         begin = pl.multiple_of(jnp.clip(ROW * p - (1 - odd) * (3 * ROW), 0, FAR - ROW), ROW)
         wide_ref[f, odd * 8 + l, 0:ROW, 0:COL] = far_ref[pl.ds(begin, ROW), :]
-    place_more(wide_ref, odd * 8, far_ref, FAR)
+    place_more(wide_ref, odd * 8, far_more_ref, 0)
 
     def plus(x):
         return jnp.maximum(x, 0.0)
@@ -297,7 +298,7 @@
         state = advance(lambda l: first_ref[l], level)
         if 4 <= level < 8:
             state_ref[level - 4] = state[0:ROW, 0:COL]
-        force_ref[level] = wide_ref[4, level] * state - wide_ref[5, level]
+        force_ref[level] = given_ref[4, level] * state - given_ref[5, level]
     for level in range(3, 9):
         back_ref[level] = retreat(lambda l: force_ref[l], level)
     for level in range(4, 8):
@@ -379,26 +380,29 @@
             ((PACKS, COL), F32),
         ],
         [block, fields, before, after],
-        cost=500000000,
-        name="edges",
+        cost=2000000000, name="edges",
     )
     west = lax.ppermute(right, "lon", lon_up)
     east = lax.ppermute(left, "lon", lon_down)
-    more = lax.ppermute(
-        call(join_kernel, [((MORE, COL), F32)], [near, west, east], cost=500000000, name="join"), "lev", pairs
-    )
+    joined = call(join_kernel, [((MORE, COL), F32)], [near, west, east], cost=1000, name="join")
+    more = lax.ppermute(joined, "lev", pairs)
     onward = call(
-        forward_kernel, [((FAR + MORE, COL), F32)], [parity, pair, more], scalars=1, name="forward"
+        forward_kernel,
+        [((FAR, COL), F32)],
+        [parity, pair, joined],
+        scalars=1,
+        places={2: ANY},
+        cost=1000, name="forward",
     )
     far_block = lax.ppermute(onward, "lev", far)
+    far_more = lax.ppermute(more, "lev", far)
     tall = (DEEP, TALL, 2 * COL)
     wide = call(
         assemble_kernel,
         [((6,) + tall, F32)],
         [parity, own, obs, west, east, pair, more],
         scalars=1,
-        cost=1000000,
-        name="assemble",
+        cost=1000000000, name="assemble",
     )
     state, adjoint, outer_next = call(
         step_kernel,
@@ -407,9 +411,9 @@
             ((LEV, ROW, COL), F32),
             (outer_increment.shape, BF16),
         ],
-        [parity, wide, far_block, outer_increment],
+        [parity, wide, far_block, far_more, outer_increment],
         [
-            pltpu.VMEM((6,) + tall, F32),
+            pltpu.VMEM((4,) + tall, F32),
             pltpu.VMEM(tall, F32),
             pltpu.VMEM(tall, F32),
             pltpu.VMEM(tall, F32),

time: 62.8 us -> 61.5 us (0.979)
  the two profiles are of different devices: /device:TPU:30 before, /device:TPU:92 now
where the time goes in v5:
time: 61.5 us; the launch traced here: 61.1 us
  starting transfers between devices  38.8 us (63%)
  waiting for transfers between devices  17.2 us (28%)
  Pallas kernels  4.38 us (7%)
  between operations  0.78 us (1%)
    ppermute x1, starting transfers between devices, shards(): pair = lax.ppermute(block, 'lev', pairs)  18.5 us
    ppermute x1, waiting for transfers between devices, shards(): more = lax.ppermute(joined, 'lev', pairs)  9.8 us
    ppermute x1, waiting for transfers between devices, shards(): east = lax.ppermute(left, 'lon', lon_down)  4.86 us
    ppermute x1, starting transfers between devices, shards(): west = lax.ppermute(right, 'lon', lon_up)  4.69 us
    pallas_call x6, Pallas kernels, call(): pl.pallas_call(kernel, out_shape=shapes[0] if single else shapes, in_spec...  4.38 us
    ppermute x1, starting transfers between devices, shards(): after = lax.ppermute(down, 'lat', lat_down)  3.64 us
    ppermute x1, starting transfers between devices, shards(): far_block = lax.ppermute(onward, 'lev', far)  3.11 us
    ppermute x1, starting transfers between devices, shards(): far_more = lax.ppermute(more, 'lev', far)  3.09 us
  transfers between devices with their start and end apart: 8, of which 3 were waited for; matrix products, arithmetic and copies ran while one was open for 0% of the time, Pallas kernels for 1%

profile of v5, /device:TPU:92, one launch (start us, length us, event | category | flops | bytes accessed | tf_op | source)
XLA Modules:
  0.0 61.1 jit_solution(3943890898130134669)
XLA Ops:
  0.6 2.0 %prepare.1 = (f32[256,128]{1,0:T(8,128)S(1)}, f32[256,128]{1,0:T(8,128)S(1)}, f32[88,128]{1,0:T(8,128)S(1)}, f32[88,128]{1,0:T(8,128)S(1)}) custom-call(s32[1]{0:T(128)} %bitcast.1.lowest_ref, bf16[4,64,512]{2,1,0:T(8,128)(2,1)} %outer_ref.1, bf16[3,4,16,128]{3,2,1,0:T(8,128)(2,1)} %courant_hbm.1, s32[1,2048]{1,0:T(1,128)} %bitcast.5, s32[1,2048]{1,0:T(1,128)} %bitcast.6, ...), custom_call_target="tpu_custom_call" | custom-call | flops 500000 | bytes 500000 | tf_op jit(solution)/shard_map/prepare/pallas_call | solution.py:329
  2.7 1.9 %collective-permute-start = (f32[88,128]{1,0:T(8,128)S(1)}, f32[88,128]{1,0:T(8,128)S(1)}, u32[]{:S(2)}, u32[]{:S(2)}) collective-permute-start(f32[88,128]{1,0:T(8,128)S(1)} %get-tuple-element.14), channel_id=1, source_target_pairs={{0,64},{64,128},{128,192},{192,256},{256,320},{320,384},{384,448},... | collective-permute-start | bytes 135176 | tf_op jit(solution)/shard_map/ppermute | solution.py:370
  4.6 3.6 %collective-permute-start.1 = (f32[88,128]{1,0:T(8,128)S(1)}, f32[88,128]{1,0:T(8,128)S(1)}, u32[]{:S(2)}, u32[]{:S(2)}) collective-permute-start(f32[88,128]{1,0:T(8,128)S(1)} %get-tuple-element.15), channel_id=1, source_target_pairs={{64,0},{128,64},{192,128},{256,192},{320,256},{384,320},{448,384},... | collective-permute-start | bytes 135176 | tf_op jit(solution)/shard_map/ppermute | solution.py:371
  8.3 18.5 %collective-permute-start.4 = (f32[256,128]{1,0:T(8,128)S(1)}, f32[256,128]{1,0:T(8,128)S(1)}, u32[]{:S(2)}, u32[]{:S(2)}) collective-permute-start(f32[256,128]{1,0:T(8,128)S(1)} %get-tuple-element.12.block_ref), channel_id=1, source_target_pairs={{0,1},{1,0},{2,3},{3,2},{4,5},{5,4},{6,7},{7,6},{8,9},{9,8},{10,11... | collective-permute-start | bytes 393224 | tf_op jit(solution)/shard_map/ppermute | solution.py:372
  26.7 0.0 collective-permute-done.before_ref
  26.7 0.0 collective-permute-done.1.after_ref
  26.8 0.2 edges.1
  27.0 4.7 %collective-permute-start.2 = (f32[24,128]{1,0:T(8,128)S(1)}, f32[24,128]{1,0:T(8,128)S(1)}, u32[]{:S(2)}, u32[]{:S(2)}) collective-permute-start(f32[24,128]{1,0:T(8,128)S(1)} %get-tuple-element.18), channel_id=1, source_target_pairs={{0,8},{8,16},{16,24},{24,32},{32,40},{40,48},{48,56},{56,0},{1,9},... | collective-permute-start | bytes 36872 | tf_op jit(solution)/shard_map/ppermute | solution.py:385
  31.7 1.9 %collective-permute-start.3 = (f32[24,128]{1,0:T(8,128)S(1)}, f32[24,128]{1,0:T(8,128)S(1)}, u32[]{:S(2)}, u32[]{:S(2)}) collective-permute-start(f32[24,128]{1,0:T(8,128)S(1)} %get-tuple-element.19), channel_id=1, source_target_pairs={{0,56},{8,0},{16,8},{24,16},{32,24},{40,32},{48,40},{56,48},{1,57}... | collective-permute-start | bytes 36872 | tf_op jit(solution)/shard_map/ppermute | solution.py:386
  33.6 0.0 collective-permute-done.2.west_ref
  33.7 4.9 %collective-permute-done.3.east_ref = f32[24,128]{1,0:T(8,128)S(1)} collective-permute-done((f32[24,128]{1,0:T(8,128)S(1)}, f32[24,128]{1,0:T(8,128)S(1)}, u32[]{:S(2)}, u32[]{:S(2)}) %collective-permute-start.3) | collective-permute-done | bytes 12320 | tf_op jit(solution)/shard_map/ppermute | solution.py:386
  38.5 1.9 %collective-permute-start.5 = (f32[96,128]{1,0:T(8,128)S(1)}, f32[96,128]{1,0:T(8,128)S(1)}, u32[]{:S(2)}, u32[]{:S(2)}) collective-permute-start(f32[96,128]{1,0:T(8,128)S(1)} %join.1.later_ref), channel_id=1, source_target_pairs={{0,1},{1,0},{2,3},{3,2},{4,5},{5,4},{6,7},{7,6},{8,9},{9,8},{10,11... | collective-permute-start | bytes 147464 | tf_op jit(solution)/shard_map/ppermute | solution.py:388
  40.5 0.0 collective-permute-done.4.pair_ref
  40.5 3.1 %collective-permute-start.6 = (f32[208,128]{1,0:T(8,128)S(1)}, f32[208,128]{1,0:T(8,128)S(1)}, u32[]{:S(2)}, u32[]{:S(2)}) collective-permute-start(f32[208,128]{1,0:T(8,128)S(1)} %forward.1), channel_id=1, source_target_pairs={{0,2},{2,4},{4,6},{3,1},{5,3},{7,5},{8,10},{10,12},{12,14},{11,9},... | collective-permute-start | bytes 319496 | tf_op jit(solution)/shard_map/ppermute | solution.py:397
  43.6 9.8 %collective-permute-done.5.more_ref = f32[96,128]{1,0:T(8,128)S(1)} collective-permute-done((f32[96,128]{1,0:T(8,128)S(1)}, f32[96,128]{1,0:T(8,128)S(1)}, u32[]{:S(2)}, u32[]{:S(2)}) %collective-permute-start.5) | collective-permute-done | bytes 49184 | tf_op jit(solution)/shard_map/ppermute | solution.py:388
  53.4 3.1 %collective-permute-start.7 = (f32[96,128]{1,0:T(8,128)S(1)}, f32[96,128]{1,0:T(8,128)S(1)}, u32[]{:S(2)}, u32[]{:S(2)}) collective-permute-start(f32[96,128]{1,0:T(8,128)S(1)} %collective-permute-done.5.more_ref), channel_id=1, source_target_pairs={{0,2},{2,4},{4,6},{3,1},{5,3},{7,5},{8,10},{10,12},{12,14},{11,9},... | collective-permute-start | bytes 147464 | tf_op jit(solution)/shard_map/ppermute | solution.py:398
  56.5 0.0 copy-start
  56.5 0.3 assemble.1.given_ref
  56.9 2.5 %collective-permute-done.7.far_more_ref = f32[96,128]{1,0:T(8,128)S(1)} collective-permute-done((f32[96,128]{1,0:T(8,128)S(1)}, f32[96,128]{1,0:T(8,128)S(1)}, u32[]{:S(2)}, u32[]{:S(2)}) %collective-permute-start.7) | collective-permute-done | bytes 49184 | tf_op jit(solution)/shard_map/ppermute | solution.py:398
  59.4 0.0 collective-permute-done.6.far_ref
  59.4 0.0 copy-done
  59.4 1.7 %steps.1 = (f32[4,16,128]{2,1,0:T(8,128)}, f32[4,16,128]{2,1,0:T(8,128)}, bf16[4,64,512]{2,1,0:T(8,128)(2,1)}) custom-call(s32[1]{0:T(128)} %bitcast.parity_ref, f32[6,12,24,256]{3,2,1,0:T(8,128)S(1)} %assemble.1.given_ref, f32[208,128]{1,0:T(8,128)S(1)} %collective-permute-done.6.far_ref, f32[96,128]{1,0:T(8,128)S(1)} %collective-permute-done.7.far_more_ref, ...), custom_call_target="tpu_custom_call" | custom-call | flops 500000 | bytes 500000 | tf_op jit(solution)/shard_map/steps/pallas_call | solution.py:329
  (2 shorter events, 0.0 us)
Async XLA Ops:
  2.7 24.1 %collective-permute-start = (f32[88,128]{1,0:T(8,128)S(1)}, f32[88,128]{1,0:T(8,128)S(1)}, u32[]{:S(2)}, u32[]{:S(2)}) collective-permute-start(f32[88,128]{1,0:T(8,128)S(1)} %get-tuple-element.14), channel_id=1, source_target_pairs={{0,64},{64,128},{128,192},{192,256},{256,320},{320,384},{384,448},... | collective-permute-start | bytes 135176 | tf_op jit(solution)/shard_map/ppermute | solution.py:370
  4.6 22.1 %collective-permute-start.1 = (f32[88,128]{1,0:T(8,128)S(1)}, f32[88,128]{1,0:T(8,128)S(1)}, u32[]{:S(2)}, u32[]{:S(2)}) collective-permute-start(f32[88,128]{1,0:T(8,128)S(1)} %get-tuple-element.15), channel_id=1, source_target_pairs={{64,0},{128,64},{192,128},{256,192},{320,256},{384,320},{448,384},... | collective-permute-start | bytes 135176 | tf_op jit(solution)/shard_map/ppermute | solution.py:371
  8.3 32.2 %collective-permute-start.4 = (f32[256,128]{1,0:T(8,128)S(1)}, f32[256,128]{1,0:T(8,128)S(1)}, u32[]{:S(2)}, u32[]{:S(2)}) collective-permute-start(f32[256,128]{1,0:T(8,128)S(1)} %get-tuple-element.12.block_ref), channel_id=1, source_target_pairs={{0,1},{1,0},{2,3},{3,2},{4,5},{5,4},{6,7},{7,6},{8,9},{9,8},{10,11... | collective-permute-start | bytes 393224 | tf_op jit(solution)/shard_map/ppermute | solution.py:372
  27.0 6.6 %collective-permute-start.2 = (f32[24,128]{1,0:T(8,128)S(1)}, f32[24,128]{1,0:T(8,128)S(1)}, u32[]{:S(2)}, u32[]{:S(2)}) collective-permute-start(f32[24,128]{1,0:T(8,128)S(1)} %get-tuple-element.18), channel_id=1, source_target_pairs={{0,8},{8,16},{16,24},{24,32},{32,40},{40,48},{48,56},{56,0},{1,9},... | collective-permute-start | bytes 36872 | tf_op jit(solution)/shard_map/ppermute | solution.py:385
  31.7 6.8 %collective-permute-start.3 = (f32[24,128]{1,0:T(8,128)S(1)}, f32[24,128]{1,0:T(8,128)S(1)}, u32[]{:S(2)}, u32[]{:S(2)}) collective-permute-start(f32[24,128]{1,0:T(8,128)S(1)} %get-tuple-element.19), channel_id=1, source_target_pairs={{0,56},{8,0},{16,8},{24,16},{32,24},{40,32},{48,40},{56,48},{1,57}... | collective-permute-start | bytes 36872 | tf_op jit(solution)/shard_map/ppermute | solution.py:386
  38.5 14.9 %collective-permute-start.5 = (f32[96,128]{1,0:T(8,128)S(1)}, f32[96,128]{1,0:T(8,128)S(1)}, u32[]{:S(2)}, u32[]{:S(2)}) collective-permute-start(f32[96,128]{1,0:T(8,128)S(1)} %join.1.later_ref), channel_id=1, source_target_pairs={{0,1},{1,0},{2,3},{3,2},{4,5},{5,4},{6,7},{7,6},{8,9},{9,8},{10,11... | collective-permute-start | bytes 147464 | tf_op jit(solution)/shard_map/ppermute | solution.py:388
  40.5 18.9 %collective-permute-start.6 = (f32[208,128]{1,0:T(8,128)S(1)}, f32[208,128]{1,0:T(8,128)S(1)}, u32[]{:S(2)}, u32[]{:S(2)}) collective-permute-start(f32[208,128]{1,0:T(8,128)S(1)} %forward.1), channel_id=1, source_target_pairs={{0,2},{2,4},{4,6},{3,1},{5,3},{7,5},{8,10},{10,12},{12,14},{11,9},... | collective-permute-start | bytes 319496 | tf_op jit(solution)/shard_map/ppermute | solution.py:397
  53.4 6.0 %collective-permute-start.7 = (f32[96,128]{1,0:T(8,128)S(1)}, f32[96,128]{1,0:T(8,128)S(1)}, u32[]{:S(2)}, u32[]{:S(2)}) collective-permute-start(f32[96,128]{1,0:T(8,128)S(1)} %collective-permute-done.5.more_ref), channel_id=1, source_target_pairs={{0,2},{2,4},{4,6},{3,1},{5,3},{7,5},{8,10},{10,12},{12,14},{11,9},... | collective-permute-start | bytes 147464 | tf_op jit(solution)/shard_map/ppermute | solution.py:398
  56.5 2.9 %copy-start = (bf16[4,64,512]{2,1,0:T(8,128)(2,1)S(1)}, bf16[4,64,512]{2,1,0:T(8,128)(2,1)}, u32[]{:S(2)}) copy-start(bf16[4,64,512]{2,1,0:T(8,128)(2,1)} %outer_ref.1) | copy-start | bytes 786436

commit v6 on v5

--- a/solution.py
+++ b/solution.py
@@ -225,7 +225,22 @@
     )
 
 
-def assemble_kernel(parity_ref, own_ref, obs_ref, west_ref, east_ref, pair_ref, more_ref, wide_ref):
+def assemble_kernel(
+    parity_ref,
+    own_ref,
+    obs_ref,
+    west_ref,
+    east_ref,
+    pair_ref,
+    more_ref,
+    wide_ref,
+    near_first_ref,
+    near_force_ref,
+    near_back_ref,
+    near_state_ref,
+    first_ref,
+    force_ref,
+):
     wide_ref[0:4, 4:8, :, 0:COL] = own_ref[...]
     wide_ref[4:6, 2:10, :, 0:COL] = obs_ref[...]
     place_edges(
@@ -239,11 +254,64 @@
     for p, (f, l) in enumerate(PLANES):
         wide_ref[f, base + l, 0:ROW, 0:COL] = pair_ref[ROW * p : ROW * p + ROW, :]
     place_more(wide_ref, base, more_ref, 0)
+    parity = parity_ref[0]
+    odd = parity == 1
+
+    def field(f, j):
+        return wide_ref[f, level_of(parity, j)]
+
+    for j in range(5, 11):
+        first_ref[j] = advance(odd, field, lambda i: field(0, i), j)
+    for j in range(6, 10):
+        state = advance(odd, field, lambda i: first_ref[i], j)
+        if j < 8:
+            near_state_ref[j - 6] = state[0:ROW, 0:COL]
+        force_ref[j] = field(4, j) * state - field(5, j)
+    for j in range(7, 9):
+        near_back_ref[j - 7] = retreat(odd, field, lambda i: force_ref[i], j)
+    near_first_ref[...] = first_ref[5:7]
+    near_force_ref[...] = force_ref[6:8]
+
+
+def plus(x):
+    return jnp.maximum(x, 0.0)
+
+
+def centre(field, j):
+    return 1.0 - (jnp.abs(field(1, j)) + jnp.abs(field(2, j)) + jnp.abs(field(3, j)))
+
+
+def advance(odd, field, get, j):
+    here = get(j)
+    below, above = jnp.where(odd, get(j + 1), get(j - 1)), jnp.where(odd, get(j - 1), get(j + 1))
+    c0, c1, c2 = (field(1 + k, j) for k in range(3))
+    result = centre(field, j) * here
+    result = result + plus(c0) * below + plus(-c0) * above
+    result = result + plus(c1) * turn(here, 1, 0) + plus(-c1) * turn(here, -1, 0)
+    return result + plus(c2) * turn(here, 1, 1) + plus(-c2) * turn(here, -1, 1)
+
+
+def retreat(odd, field, get, j):
+    here = get(j)
+    sign = jnp.where(odd, -1.0, 1.0)
+    c1, c2 = field(2, j), field(3, j)
+    result = centre(field, j) * here
+    result = result + plus(sign * field(1, j + 1)) * get(j + 1) + plus(-sign * field(1, j - 1)) * get(j - 1)
+    result = result + turn(plus(c1) * here, -1, 0) + turn(plus(-c1) * here, 1, 0)
+    return result + turn(plus(c2) * here, -1, 1) + turn(plus(-c2) * here, 1, 1)
+
+
+def level_of(odd, j):
+    return j + odd * (11 - 2 * j)
 
 
 def step_kernel(
     parity_ref,
     given_ref,
+    given_first_ref,
+    given_force_ref,
+    given_back_ref,
+    given_state_ref,
     far_ref,
     far_more_ref,
     outer_ref,
@@ -257,54 +325,36 @@
     flat_ref,
     spread_ref,
 ):
-    wide_ref[...] = given_ref[0:4]
-    odd = parity_ref[0]
+    parity = parity_ref[0]
+    odd = parity == 1
     for p, (f, l) in enumerate(PLANES):
-        begin = pl.multiple_of(jnp.clip(ROW * p - (1 - odd) * (3 * ROW), 0, FAR - ROW), ROW)
-        wide_ref[f, odd * 8 + l, 0:ROW, 0:COL] = far_ref[pl.ds(begin, ROW), :]
-    place_more(wide_ref, odd * 8, far_more_ref, 0)
-
-    def plus(x):
-        return jnp.maximum(x, 0.0)
-
-    def centre(level):
-        return 1.0 - (
-            jnp.abs(wide_ref[1, level]) + jnp.abs(wide_ref[2, level]) + jnp.abs(wide_ref[3, level])
-        )
-
-    def advance(get, level):
-        here = get(level)
-        c0, c1, c2 = (wide_ref[1 + k, level] for k in range(3))
-        result = centre(level) * here
-        result = result + plus(c0) * get(level - 1) + plus(-c0) * get(level + 1)
-        result = result + plus(c1) * turn(here, 1, 0) + plus(-c1) * turn(here, -1, 0)
-        return result + plus(c2) * turn(here, 1, 1) + plus(-c2) * turn(here, -1, 1)
-
-    def retreat(get, level):
-        here = get(level)
-        c1, c2 = (wide_ref[2 + k, level] for k in range(2))
-        result = centre(level) * here
-        result = (
-            result
-            + plus(wide_ref[1, level + 1]) * get(level + 1)
-            + plus(-wide_ref[1, level - 1]) * get(level - 1)
-        )
-        result = result + turn(plus(c1) * here, -1, 0) + turn(plus(-c1) * here, 1, 0)
-        return result + turn(plus(c2) * here, -1, 1) + turn(plus(-c2) * here, 1, 1)
-
-    for level in range(1, 11):
-        first_ref[level] = advance(lambda l: wide_ref[0, l], level)
-    for level in range(2, 10):
-        state = advance(lambda l: first_ref[l], level)
-        if 4 <= level < 8:
-            state_ref[level - 4] = state[0:ROW, 0:COL]
-        force_ref[level] = given_ref[4, level] * state - given_ref[5, level]
-    for level in range(3, 9):
-        back_ref[level] = retreat(lambda l: force_ref[l], level)
-    for level in range(4, 8):
-        result = retreat(lambda l: back_ref[l], level)[0:ROW, 0:COL]
-        adjoint_ref[level - 4] = result
-        flat_ref[ROW * (level - 4) : ROW * (level - 3), :] = result
+        begin = pl.multiple_of(jnp.clip(ROW * p - (1 - parity) * (3 * ROW), 0, FAR - ROW), ROW)
+        wide_ref[f, l, 0:ROW, 0:COL] = far_ref[pl.ds(begin, ROW), :]
+    place_more(wide_ref, 0, far_more_ref, 0)
+
+    def field(f, j):
+        return wide_ref[f, j + parity * (3 - 2 * j)] if j < 4 else given_ref[f, level_of(parity, j)]
+
+    first_ref[5:7] = given_first_ref[...]
+    force_ref[6:8] = given_force_ref[...]
+    back_ref[7:9] = given_back_ref[...]
+    for j in (6, 7):
+        state_ref[level_of(parity, j) - 4] = given_state_ref[j - 6]
+    for j in range(1, 5):
+        first_ref[j] = advance(odd, field, lambda i: field(0, i), j)
+    for j in range(2, 6):
+        state = advance(odd, field, lambda i: first_ref[i], j)
+        if j >= 4:
+            state_ref[level_of(parity, j) - 4] = state[0:ROW, 0:COL]
+        level = level_of(parity, j)
+        force_ref[j] = given_ref[4, level] * state - given_ref[5, level]
+    for j in range(3, 7):
+        back_ref[j] = retreat(odd, field, lambda i: force_ref[i], j)
+    for j in range(4, 8):
+        result = retreat(odd, field, lambda i: back_ref[i], j)[0:ROW, 0:COL]
+        place = level_of(parity, j) - 4
+        adjoint_ref[place] = result
+        flat_ref[pl.ds(pl.multiple_of(place * ROW, ROW), ROW), :] = result
     flat = flat_ref[...]
     high = flat.astype(BF16)
     rest = flat - high.astype(F32)
@@ -397,12 +447,21 @@
     far_block = lax.ppermute(onward, "lev", far)
     far_more = lax.ppermute(more, "lev", far)
     tall = (DEEP, TALL, 2 * COL)
-    wide = call(
+    plane = (TALL, 2 * COL)
+    near = call(
         assemble_kernel,
-        [((6,) + tall, F32)],
+        [
+            ((6,) + tall, F32),
+            ((2,) + plane, F32),
+            ((2,) + plane, F32),
+            ((2,) + plane, F32),
+            ((2, ROW, COL), F32),
+        ],
         [parity, own, obs, west, east, pair, more],
+        [pltpu.VMEM(tall, F32), pltpu.VMEM(tall, F32)],
         scalars=1,
-        cost=1000000000, name="assemble",
+        cost=1000000000,
+        name="assemble",
     )
     state, adjoint, outer_next = call(
         step_kernel,
@@ -411,9 +470,9 @@
             ((LEV, ROW, COL), F32),
             (outer_increment.shape, BF16),
         ],
-        [parity, wide, far_block, far_more, outer_increment],
+        [parity, *near, far_block, far_more, outer_increment],
         [
-            pltpu.VMEM((4,) + tall, F32),
+            pltpu.VMEM((4, LEV) + plane, F32),
             pltpu.VMEM(tall, F32),
             pltpu.VMEM(tall, F32),
             pltpu.VMEM(tall, F32),

time: 61.5 us -> 61.3 us (level)
  the two profiles are of different devices: /device:TPU:92 before, /device:TPU:90 now
where the time goes in v6:
time: 61.3 us; the launch traced here: 60.9 us
  starting transfers between devices  39.4 us (64%)
  waiting for transfers between devices  16.3 us (27%)
  Pallas kernels  4.48 us (7%)
  between operations  0.78 us (1%)
    ppermute x1, starting transfers between devices, shards(): pair = lax.ppermute(block, 'lev', pairs)  18.5 us
    ppermute x1, waiting for transfers between devices, shards(): more = lax.ppermute(joined, 'lev', pairs)  9.52 us
    ppermute x1, waiting for transfers between devices, shards(): east = lax.ppermute(left, 'lon', lon_down)  4.86 us
    ppermute x1, starting transfers between devices, shards(): west = lax.ppermute(right, 'lon', lon_up)  4.7 us
    pallas_call x6, Pallas kernels, call(): pl.pallas_call(kernel, out_shape=shapes[0] if single else shapes, in_spec...  4.48 us
    ppermute x1, starting transfers between devices, shards(): after = lax.ppermute(down, 'lat', lat_down)  3.64 us
    ppermute x1, starting transfers between devices, shards(): far_block = lax.ppermute(onward, 'lev', far)  3.4 us
    ppermute x1, starting transfers between devices, shards(): far_more = lax.ppermute(more, 'lev', far)  3.39 us
  transfers between devices with their start and end apart: 8, of which 3 were waited for; matrix products, arithmetic and copies ran while one was open for 0% of the time, Pallas kernels for 2%

profile of v6, /device:TPU:90, one launch (start us, length us, event | category | flops | bytes accessed | tf_op | source)
XLA Modules:
  0.0 60.9 jit_solution(68991874532141405)
XLA Ops:
  0.6 2.0 %prepare.1 = (f32[256,128]{1,0:T(8,128)S(1)}, f32[256,128]{1,0:T(8,128)S(1)}, f32[88,128]{1,0:T(8,128)S(1)}, f32[88,128]{1,0:T(8,128)S(1)}) custom-call(s32[1]{0:T(128)} %bitcast.1.lowest_ref, bf16[4,64,512]{2,1,0:T(8,128)(2,1)} %outer_ref.1, bf16[3,4,16,128]{3,2,1,0:T(8,128)(2,1)} %courant_hbm.1, s32[1,2048]{1,0:T(1,128)} %bitcast.5, s32[1,2048]{1,0:T(1,128)} %bitcast.6, ...), custom_call_target="tpu_custom_call" | custom-call | flops 500000 | bytes 500000 | tf_op jit(solution)/shard_map/prepare/pallas_call | solution.py:379
  2.7 1.9 %collective-permute-start = (f32[88,128]{1,0:T(8,128)S(1)}, f32[88,128]{1,0:T(8,128)S(1)}, u32[]{:S(2)}, u32[]{:S(2)}) collective-permute-start(f32[88,128]{1,0:T(8,128)S(1)} %get-tuple-element.19), channel_id=1, source_target_pairs={{0,64},{64,128},{128,192},{192,256},{256,320},{320,384},{384,448},... | collective-permute-start | bytes 135176 | tf_op jit(solution)/shard_map/ppermute | solution.py:420
  4.6 3.6 %collective-permute-start.1 = (f32[88,128]{1,0:T(8,128)S(1)}, f32[88,128]{1,0:T(8,128)S(1)}, u32[]{:S(2)}, u32[]{:S(2)}) collective-permute-start(f32[88,128]{1,0:T(8,128)S(1)} %get-tuple-element.20), channel_id=1, source_target_pairs={{64,0},{128,64},{192,128},{256,192},{320,256},{384,320},{448,384},... | collective-permute-start | bytes 135176 | tf_op jit(solution)/shard_map/ppermute | solution.py:421
  8.3 18.5 %collective-permute-start.4 = (f32[256,128]{1,0:T(8,128)S(1)}, f32[256,128]{1,0:T(8,128)S(1)}, u32[]{:S(2)}, u32[]{:S(2)}) collective-permute-start(f32[256,128]{1,0:T(8,128)S(1)} %get-tuple-element.17.block_ref), channel_id=1, source_target_pairs={{0,1},{1,0},{2,3},{3,2},{4,5},{5,4},{6,7},{7,6},{8,9},{9,8},{10,11... | collective-permute-start | bytes 393224 | tf_op jit(solution)/shard_map/ppermute | solution.py:422
  26.7 0.0 collective-permute-done.before_ref
  26.7 0.0 collective-permute-done.1.after_ref
  26.8 0.2 edges.1
  27.0 4.7 %collective-permute-start.2 = (f32[24,128]{1,0:T(8,128)S(1)}, f32[24,128]{1,0:T(8,128)S(1)}, u32[]{:S(2)}, u32[]{:S(2)}) collective-permute-start(f32[24,128]{1,0:T(8,128)S(1)} %get-tuple-element.23), channel_id=1, source_target_pairs={{0,8},{8,16},{16,24},{24,32},{32,40},{40,48},{48,56},{56,0},{1,9},... | collective-permute-start | bytes 36872 | tf_op jit(solution)/shard_map/ppermute | solution.py:435
  31.7 1.9 %collective-permute-start.3 = (f32[24,128]{1,0:T(8,128)S(1)}, f32[24,128]{1,0:T(8,128)S(1)}, u32[]{:S(2)}, u32[]{:S(2)}) collective-permute-start(f32[24,128]{1,0:T(8,128)S(1)} %get-tuple-element.24), channel_id=1, source_target_pairs={{0,56},{8,0},{16,8},{24,16},{32,24},{40,32},{48,40},{56,48},{1,57}... | collective-permute-start | bytes 36872 | tf_op jit(solution)/shard_map/ppermute | solution.py:436
  33.6 0.0 collective-permute-done.2.west_ref
  33.7 4.9 %collective-permute-done.3.east_ref = f32[24,128]{1,0:T(8,128)S(1)} collective-permute-done((f32[24,128]{1,0:T(8,128)S(1)}, f32[24,128]{1,0:T(8,128)S(1)}, u32[]{:S(2)}, u32[]{:S(2)}) %collective-permute-start.3) | collective-permute-done | bytes 12320 | tf_op jit(solution)/shard_map/ppermute | solution.py:436
  38.5 1.9 %collective-permute-start.5 = (f32[96,128]{1,0:T(8,128)S(1)}, f32[96,128]{1,0:T(8,128)S(1)}, u32[]{:S(2)}, u32[]{:S(2)}) collective-permute-start(f32[96,128]{1,0:T(8,128)S(1)} %join.1.later_ref), channel_id=1, source_target_pairs={{0,1},{1,0},{2,3},{3,2},{4,5},{5,4},{6,7},{7,6},{8,9},{9,8},{10,11... | collective-permute-start | bytes 147464 | tf_op jit(solution)/shard_map/ppermute | solution.py:438
  40.5 0.0 collective-permute-done.4.pair_ref
  40.5 3.4 %collective-permute-start.6 = (f32[208,128]{1,0:T(8,128)S(1)}, f32[208,128]{1,0:T(8,128)S(1)}, u32[]{:S(2)}, u32[]{:S(2)}) collective-permute-start(f32[208,128]{1,0:T(8,128)S(1)} %forward.1), channel_id=1, source_target_pairs={{0,2},{2,4},{4,6},{3,1},{5,3},{7,5},{8,10},{10,12},{12,14},{11,9},... | collective-permute-start | bytes 319496 | tf_op jit(solution)/shard_map/ppermute | solution.py:447
  43.9 9.5 %collective-permute-done.5.more_ref = f32[96,128]{1,0:T(8,128)S(1)} collective-permute-done((f32[96,128]{1,0:T(8,128)S(1)}, f32[96,128]{1,0:T(8,128)S(1)}, u32[]{:S(2)}, u32[]{:S(2)}) %collective-permute-start.5) | collective-permute-done | bytes 49184 | tf_op jit(solution)/shard_map/ppermute | solution.py:438
  53.4 3.4 %collective-permute-start.7 = (f32[96,128]{1,0:T(8,128)S(1)}, f32[96,128]{1,0:T(8,128)S(1)}, u32[]{:S(2)}, u32[]{:S(2)}) collective-permute-start(f32[96,128]{1,0:T(8,128)S(1)} %collective-permute-done.5.more_ref), channel_id=1, source_target_pairs={{0,2},{2,4},{4,6},{3,1},{5,3},{7,5},{8,10},{10,12},{12,14},{11,9},... | collective-permute-start | bytes 147464 | tf_op jit(solution)/shard_map/ppermute | solution.py:448
  56.8 0.0 copy-start
  56.8 0.7 %assemble.1 = (f32[6,12,24,256]{3,2,1,0:T(8,128)S(1)}, f32[2,24,256]{2,1,0:T(8,128)S(1)}, f32[2,24,256]{2,1,0:T(8,128)S(1)}, f32[2,24,256]{2,1,0:T(8,128)S(1)}, f32[2,16,128]{2,1,0:T(8,128)S(1)}) custom-call(s32[1]{0:T(128)} %bitcast.parity_ref, f32[4,4,24,128]{3,2,1,0:T(8,128)S(1)} %get-tuple-element.21.own_ref, ...), custom_call_target="tpu_custom_call" | custom-call | flops 1000000000 | bytes 1000000000 | tf_op jit(solution)/shard_map/assemble/pallas_call | solution.py:379
  57.5 1.9 %collective-permute-done.7.far_more_ref = f32[96,128]{1,0:T(8,128)S(1)} collective-permute-done((f32[96,128]{1,0:T(8,128)S(1)}, f32[96,128]{1,0:T(8,128)S(1)}, u32[]{:S(2)}, u32[]{:S(2)}) %collective-permute-start.7) | collective-permute-done | bytes 49184 | tf_op jit(solution)/shard_map/ppermute | solution.py:448
  59.4 0.0 collective-permute-done.6.far_ref
  59.4 0.0 copy-done
  59.4 1.5 %steps.1 = (f32[4,16,128]{2,1,0:T(8,128)}, f32[4,16,128]{2,1,0:T(8,128)}, bf16[4,64,512]{2,1,0:T(8,128)(2,1)}) custom-call(s32[1]{0:T(128)} %bitcast.parity_ref, f32[6,12,24,256]{3,2,1,0:T(8,128)S(1)} %get-tuple-element.26.given_ref, f32[2,24,256]{2,1,0:T(8,128)S(1)} %get-tuple-element.27.given_first_ref, ...), custom_call_target="tpu_custom_call" | custom-call | flops 500000 | bytes 500000 | tf_op jit(solution)/shard_map/steps/pallas_call | solution.py:379
  (2 shorter events, 0.0 us)
Async XLA Ops:
  2.7 24.1 %collective-permute-start = (f32[88,128]{1,0:T(8,128)S(1)}, f32[88,128]{1,0:T(8,128)S(1)}, u32[]{:S(2)}, u32[]{:S(2)}) collective-permute-start(f32[88,128]{1,0:T(8,128)S(1)} %get-tuple-element.19), channel_id=1, source_target_pairs={{0,64},{64,128},{128,192},{192,256},{256,320},{320,384},{384,448},... | collective-permute-start | bytes 135176 | tf_op jit(solution)/shard_map/ppermute | solution.py:420
  4.6 22.1 %collective-permute-start.1 = (f32[88,128]{1,0:T(8,128)S(1)}, f32[88,128]{1,0:T(8,128)S(1)}, u32[]{:S(2)}, u32[]{:S(2)}) collective-permute-start(f32[88,128]{1,0:T(8,128)S(1)} %get-tuple-element.20), channel_id=1, source_target_pairs={{64,0},{128,64},{192,128},{256,192},{320,256},{384,320},{448,384},... | collective-permute-start | bytes 135176 | tf_op jit(solution)/shard_map/ppermute | solution.py:421
  8.3 32.2 %collective-permute-start.4 = (f32[256,128]{1,0:T(8,128)S(1)}, f32[256,128]{1,0:T(8,128)S(1)}, u32[]{:S(2)}, u32[]{:S(2)}) collective-permute-start(f32[256,128]{1,0:T(8,128)S(1)} %get-tuple-element.17.block_ref), channel_id=1, source_target_pairs={{0,1},{1,0},{2,3},{3,2},{4,5},{5,4},{6,7},{7,6},{8,9},{9,8},{10,11... | collective-permute-start | bytes 393224 | tf_op jit(solution)/shard_map/ppermute | solution.py:422
  27.0 6.6 %collective-permute-start.2 = (f32[24,128]{1,0:T(8,128)S(1)}, f32[24,128]{1,0:T(8,128)S(1)}, u32[]{:S(2)}, u32[]{:S(2)}) collective-permute-start(f32[24,128]{1,0:T(8,128)S(1)} %get-tuple-element.23), channel_id=1, source_target_pairs={{0,8},{8,16},{16,24},{24,32},{32,40},{40,48},{48,56},{56,0},{1,9},... | collective-permute-start | bytes 36872 | tf_op jit(solution)/shard_map/ppermute | solution.py:435
  31.7 6.8 %collective-permute-start.3 = (f32[24,128]{1,0:T(8,128)S(1)}, f32[24,128]{1,0:T(8,128)S(1)}, u32[]{:S(2)}, u32[]{:S(2)}) collective-permute-start(f32[24,128]{1,0:T(8,128)S(1)} %get-tuple-element.24), channel_id=1, source_target_pairs={{0,56},{8,0},{16,8},{24,16},{32,24},{40,32},{48,40},{56,48},{1,57}... | collective-permute-start | bytes 36872 | tf_op jit(solution)/shard_map/ppermute | solution.py:436
  38.5 14.9 %collective-permute-start.5 = (f32[96,128]{1,0:T(8,128)S(1)}, f32[96,128]{1,0:T(8,128)S(1)}, u32[]{:S(2)}, u32[]{:S(2)}) collective-permute-start(f32[96,128]{1,0:T(8,128)S(1)} %join.1.later_ref), channel_id=1, source_target_pairs={{0,1},{1,0},{2,3},{3,2},{4,5},{5,4},{6,7},{7,6},{8,9},{9,8},{10,11... | collective-permute-start | bytes 147464 | tf_op jit(solution)/shard_map/ppermute | solution.py:438
  40.5 18.9 %collective-permute-start.6 = (f32[208,128]{1,0:T(8,128)S(1)}, f32[208,128]{1,0:T(8,128)S(1)}, u32[]{:S(2)}, u32[]{:S(2)}) collective-permute-start(f32[208,128]{1,0:T(8,128)S(1)} %forward.1), channel_id=1, source_target_pairs={{0,2},{2,4},{4,6},{3,1},{5,3},{7,5},{8,10},{10,12},{12,14},{11,9},... | collective-permute-start | bytes 319496 | tf_op jit(solution)/shard_map/ppermute | solution.py:447
  53.4 6.0 %collective-permute-start.7 = (f32[96,128]{1,0:T(8,128)S(1)}, f32[96,128]{1,0:T(8,128)S(1)}, u32[]{:S(2)}, u32[]{:S(2)}) collective-permute-start(f32[96,128]{1,0:T(8,128)S(1)} %collective-permute-done.5.more_ref), channel_id=1, source_target_pairs={{0,2},{2,4},{4,6},{3,1},{5,3},{7,5},{8,10},{10,12},{12,14},{11,9},... | collective-permute-start | bytes 147464 | tf_op jit(solution)/shard_map/ppermute | solution.py:448
  56.8 2.6 %copy-start = (bf16[4,64,512]{2,1,0:T(8,128)(2,1)S(1)}, bf16[4,64,512]{2,1,0:T(8,128)(2,1)}, u32[]{:S(2)}) copy-start(bf16[4,64,512]{2,1,0:T(8,128)(2,1)} %outer_ref.1) | copy-start | bytes 786436

commit v7 on v6

--- a/solution.py
+++ b/solution.py
@@ -430,11 +430,11 @@
             ((PACKS, COL), F32),
         ],
         [block, fields, before, after],
-        cost=2000000000, name="edges",
+        cost=1000, name="edges",
     )
     west = lax.ppermute(right, "lon", lon_up)
     east = lax.ppermute(left, "lon", lon_down)
-    joined = call(join_kernel, [((MORE, COL), F32)], [near, west, east], cost=1000, name="join")
+    joined = call(join_kernel, [((MORE, COL), F32)], [near, west, east], cost=2000000000, name="join")
     more = lax.ppermute(joined, "lev", pairs)
     onward = call(
         forward_kernel,
@@ -460,8 +460,7 @@
         [parity, own, obs, west, east, pair, more],
         [pltpu.VMEM(tall, F32), pltpu.VMEM(tall, F32)],
         scalars=1,
-        cost=1000000000,
-        name="assemble",
+        cost=1000000000, name="assemble",
     )
     state, adjoint, outer_next = call(
         step_kernel,

time: 61.3 us -> 66.4 us (1.083)
  the two profiles are of different devices: /device:TPU:90 before, /device:TPU:38 now
where the time goes in v7:
time: 66.4 us; the launch traced here: 66.1 us
  starting transfers between devices  33 us (50%)
  waiting for transfers between devices  27.8 us (42%)
  Pallas kernels  4.47 us (7%)
  between operations  0.77 us (1%)
    ppermute x1, waiting for transfers between devices, shards(): more = lax.ppermute(joined, 'lev', pairs)  18.6 us
    ppermute x1, starting transfers between devices, shards(): pair = lax.ppermute(block, 'lev', pairs)  18.5 us
    pallas_call x6, Pallas kernels, call(): pl.pallas_call(kernel, out_shape=shapes[0] if single else shapes, in_spec...  4.47 us
    ppermute x1, starting transfers between devices, shards(): east = lax.ppermute(left, 'lon', lon_down)  4.47 us
    ppermute x1, waiting for transfers between devices, shards(): far_more = lax.ppermute(more, 'lev', far)  3.97 us
    ppermute x1, waiting for transfers between devices, shards(): after = lax.ppermute(down, 'lat', lat_down)  3.97 us
    ppermute x1, starting transfers between devices, shards(): west = lax.ppermute(right, 'lon', lon_up)  2.59 us
    ppermute x1, starting transfers between devices, shards(): more = lax.ppermute(joined, 'lev', pairs)  1.92 us
  transfers between devices with their start and end apart: 8, of which 4 were waited for; matrix products, arithmetic and copies ran while one was open for 0% of the time, Pallas kernels for 1%

profile of v7, /device:TPU:38, one launch (start us, length us, event | category | flops | bytes accessed | tf_op | source)
XLA Modules:
  0.0 66.1 jit_solution(15838387115418712052)
XLA Ops:
  0.6 2.0 %prepare.1 = (f32[256,128]{1,0:T(8,128)S(1)}, f32[256,128]{1,0:T(8,128)S(1)}, f32[88,128]{1,0:T(8,128)S(1)}, f32[88,128]{1,0:T(8,128)S(1)}) custom-call(s32[1]{0:T(128)} %bitcast.1.lowest_ref, bf16[4,64,512]{2,1,0:T(8,128)(2,1)} %outer_ref.1, bf16[3,4,16,128]{3,2,1,0:T(8,128)(2,1)} %courant_hbm.1, s32[1,2048]{1,0:T(1,128)} %bitcast.5, s32[1,2048]{1,0:T(1,128)} %bitcast.6, ...), custom_call_target="tpu_custom_call" | custom-call | flops 500000 | bytes 500000 | tf_op jit(solution)/shard_map/prepare/pallas_call | solution.py:379
  2.7 1.7 %collective-permute-start = (f32[88,128]{1,0:T(8,128)S(1)}, f32[88,128]{1,0:T(8,128)S(1)}, u32[]{:S(2)}, u32[]{:S(2)}) collective-permute-start(f32[88,128]{1,0:T(8,128)S(1)} %get-tuple-element.19), channel_id=1, source_target_pairs={{0,64},{64,128},{128,192},{192,256},{256,320},{320,384},{384,448},... | collective-permute-start | bytes 135176 | tf_op jit(solution)/shard_map/ppermute | solution.py:420
  4.4 1.3 %collective-permute-start.1 = (f32[88,128]{1,0:T(8,128)S(1)}, f32[88,128]{1,0:T(8,128)S(1)}, u32[]{:S(2)}, u32[]{:S(2)}) collective-permute-start(f32[88,128]{1,0:T(8,128)S(1)} %get-tuple-element.20), channel_id=1, source_target_pairs={{64,0},{128,64},{192,128},{256,192},{320,256},{384,320},{448,384},... | collective-permute-start | bytes 135176 | tf_op jit(solution)/shard_map/ppermute | solution.py:421
  5.7 0.0 collective-permute-done.before_ref
  5.7 4.0 %collective-permute-done.1.after_ref = f32[88,128]{1,0:T(8,128)S(1)} collective-permute-done((f32[88,128]{1,0:T(8,128)S(1)}, f32[88,128]{1,0:T(8,128)S(1)}, u32[]{:S(2)}, u32[]{:S(2)}) %collective-permute-start.1) | collective-permute-done | bytes 45088 | tf_op jit(solution)/shard_map/ppermute | solution.py:421
  9.7 0.2 edges.1
  10.0 2.6 %collective-permute-start.2 = (f32[24,128]{1,0:T(8,128)S(1)}, f32[24,128]{1,0:T(8,128)S(1)}, u32[]{:S(2)}, u32[]{:S(2)}) collective-permute-start(f32[24,128]{1,0:T(8,128)S(1)} %get-tuple-element.23), channel_id=1, source_target_pairs={{0,8},{8,16},{16,24},{24,32},{32,40},{40,48},{48,56},{56,0},{1,9},... | collective-permute-start | bytes 36872 | tf_op jit(solution)/shard_map/ppermute | solution.py:435
  12.6 4.5 %collective-permute-start.3 = (f32[24,128]{1,0:T(8,128)S(1)}, f32[24,128]{1,0:T(8,128)S(1)}, u32[]{:S(2)}, u32[]{:S(2)}) collective-permute-start(f32[24,128]{1,0:T(8,128)S(1)} %get-tuple-element.24), channel_id=1, source_target_pairs={{0,56},{8,0},{16,8},{24,16},{32,24},{40,32},{48,40},{56,48},{1,57}... | collective-permute-start | bytes 36872 | tf_op jit(solution)/shard_map/ppermute | solution.py:436
  17.0 18.5 %collective-permute-start.4 = (f32[256,128]{1,0:T(8,128)S(1)}, f32[256,128]{1,0:T(8,128)S(1)}, u32[]{:S(2)}, u32[]{:S(2)}) collective-permute-start(f32[256,128]{1,0:T(8,128)S(1)} %get-tuple-element.17.block_ref), channel_id=1, source_target_pairs={{0,1},{1,0},{2,3},{3,2},{4,5},{5,4},{6,7},{7,6},{8,9},{9,8},{10,11... | collective-permute-start | bytes 393224 | tf_op jit(solution)/shard_map/ppermute | solution.py:422
  35.5 0.0 collective-permute-done.2.west_ref
  35.5 0.0 collective-permute-done.3.east_ref
  35.5 1.9 %collective-permute-start.5 = (f32[96,128]{1,0:T(8,128)S(1)}, f32[96,128]{1,0:T(8,128)S(1)}, u32[]{:S(2)}, u32[]{:S(2)}) collective-permute-start(f32[96,128]{1,0:T(8,128)S(1)} %join.1.later_ref), channel_id=1, source_target_pairs={{0,1},{1,0},{2,3},{3,2},{4,5},{5,4},{6,7},{7,6},{8,9},{9,8},{10,11... | collective-permute-start | bytes 147464 | tf_op jit(solution)/shard_map/ppermute | solution.py:438
  37.5 1.2 %collective-permute-done.4.pair_ref = f32[256,128]{1,0:T(8,128)S(1)} collective-permute-done((f32[256,128]{1,0:T(8,128)S(1)}, f32[256,128]{1,0:T(8,128)S(1)}, u32[]{:S(2)}, u32[]{:S(2)}) %collective-permute-start.4) | collective-permute-done | bytes 131104 | tf_op jit(solution)/shard_map/ppermute | solution.py:422
  38.7 1.3 %collective-permute-start.6 = (f32[208,128]{1,0:T(8,128)S(1)}, f32[208,128]{1,0:T(8,128)S(1)}, u32[]{:S(2)}, u32[]{:S(2)}) collective-permute-start(f32[208,128]{1,0:T(8,128)S(1)} %forward.1), channel_id=1, source_target_pairs={{0,2},{2,4},{4,6},{3,1},{5,3},{7,5},{8,10},{10,12},{12,14},{11,9},... | collective-permute-start | bytes 319496 | tf_op jit(solution)/shard_map/ppermute | solution.py:447
  40.0 18.6 %collective-permute-done.5.more_ref = f32[96,128]{1,0:T(8,128)S(1)} collective-permute-done((f32[96,128]{1,0:T(8,128)S(1)}, f32[96,128]{1,0:T(8,128)S(1)}, u32[]{:S(2)}, u32[]{:S(2)}) %collective-permute-start.5) | collective-permute-done | bytes 49184 | tf_op jit(solution)/shard_map/ppermute | solution.py:438
  58.6 1.3 %collective-permute-start.7 = (f32[96,128]{1,0:T(8,128)S(1)}, f32[96,128]{1,0:T(8,128)S(1)}, u32[]{:S(2)}, u32[]{:S(2)}) collective-permute-start(f32[96,128]{1,0:T(8,128)S(1)} %collective-permute-done.5.more_ref), channel_id=1, source_target_pairs={{0,2},{2,4},{4,6},{3,1},{5,3},{7,5},{8,10},{10,12},{12,14},{11,9},... | collective-permute-start | bytes 147464 | tf_op jit(solution)/shard_map/ppermute | solution.py:448
  59.9 0.0 copy-start
  59.9 0.7 %assemble.1 = (f32[6,12,24,256]{3,2,1,0:T(8,128)S(1)}, f32[2,24,256]{2,1,0:T(8,128)S(1)}, f32[2,24,256]{2,1,0:T(8,128)S(1)}, f32[2,24,256]{2,1,0:T(8,128)S(1)}, f32[2,16,128]{2,1,0:T(8,128)S(1)}) custom-call(s32[1]{0:T(128)} %bitcast.parity_ref, f32[4,4,24,128]{3,2,1,0:T(8,128)S(1)} %get-tuple-element.21.own_ref, ...), custom_call_target="tpu_custom_call" | custom-call | flops 1000000000 | bytes 1000000000 | tf_op jit(solution)/shard_map/assemble/pallas_call | solution.py:379
  60.6 4.0 %collective-permute-done.7.far_more_ref = f32[96,128]{1,0:T(8,128)S(1)} collective-permute-done((f32[96,128]{1,0:T(8,128)S(1)}, f32[96,128]{1,0:T(8,128)S(1)}, u32[]{:S(2)}, u32[]{:S(2)}) %collective-permute-start.7) | collective-permute-done | bytes 49184 | tf_op jit(solution)/shard_map/ppermute | solution.py:448
  64.6 0.0 collective-permute-done.6.far_ref
  64.6 0.0 copy-done
  64.6 1.5 %steps.1 = (f32[4,16,128]{2,1,0:T(8,128)}, f32[4,16,128]{2,1,0:T(8,128)}, bf16[4,64,512]{2,1,0:T(8,128)(2,1)}) custom-call(s32[1]{0:T(128)} %bitcast.parity_ref, f32[6,12,24,256]{3,2,1,0:T(8,128)S(1)} %get-tuple-element.26.given_ref, f32[2,24,256]{2,1,0:T(8,128)S(1)} %get-tuple-element.27.given_first_ref, ...), custom_call_target="tpu_custom_call" | custom-call | flops 500000 | bytes 500000 | tf_op jit(solution)/shard_map/steps/pallas_call | solution.py:379
  (2 shorter events, 0.0 us)
Async XLA Ops:
  2.7 3.1 %collective-permute-start = (f32[88,128]{1,0:T(8,128)S(1)}, f32[88,128]{1,0:T(8,128)S(1)}, u32[]{:S(2)}, u32[]{:S(2)}) collective-permute-start(f32[88,128]{1,0:T(8,128)S(1)} %get-tuple-element.19), channel_id=1, source_target_pairs={{0,64},{64,128},{128,192},{192,256},{256,320},{320,384},{384,448},... | collective-permute-start | bytes 135176 | tf_op jit(solution)/shard_map/ppermute | solution.py:420
  4.4 5.3 %collective-permute-start.1 = (f32[88,128]{1,0:T(8,128)S(1)}, f32[88,128]{1,0:T(8,128)S(1)}, u32[]{:S(2)}, u32[]{:S(2)}) collective-permute-start(f32[88,128]{1,0:T(8,128)S(1)} %get-tuple-element.20), channel_id=1, source_target_pairs={{64,0},{128,64},{192,128},{256,192},{320,256},{384,320},{448,384},... | collective-permute-start | bytes 135176 | tf_op jit(solution)/shard_map/ppermute | solution.py:421
  10.0 25.5 %collective-permute-start.2 = (f32[24,128]{1,0:T(8,128)S(1)}, f32[24,128]{1,0:T(8,128)S(1)}, u32[]{:S(2)}, u32[]{:S(2)}) collective-permute-start(f32[24,128]{1,0:T(8,128)S(1)} %get-tuple-element.23), channel_id=1, source_target_pairs={{0,8},{8,16},{16,24},{24,32},{32,40},{40,48},{48,56},{56,0},{1,9},... | collective-permute-start | bytes 36872 | tf_op jit(solution)/shard_map/ppermute | solution.py:435
  12.6 23.0 %collective-permute-start.3 = (f32[24,128]{1,0:T(8,128)S(1)}, f32[24,128]{1,0:T(8,128)S(1)}, u32[]{:S(2)}, u32[]{:S(2)}) collective-permute-start(f32[24,128]{1,0:T(8,128)S(1)} %get-tuple-element.24), channel_id=1, source_target_pairs={{0,56},{8,0},{16,8},{24,16},{32,24},{40,32},{48,40},{56,48},{1,57}... | collective-permute-start | bytes 36872 | tf_op jit(solution)/shard_map/ppermute | solution.py:436
  17.0 21.6 %collective-permute-start.4 = (f32[256,128]{1,0:T(8,128)S(1)}, f32[256,128]{1,0:T(8,128)S(1)}, u32[]{:S(2)}, u32[]{:S(2)}) collective-permute-start(f32[256,128]{1,0:T(8,128)S(1)} %get-tuple-element.17.block_ref), channel_id=1, source_target_pairs={{0,1},{1,0},{2,3},{3,2},{4,5},{5,4},{6,7},{7,6},{8,9},{9,8},{10,11... | collective-permute-start | bytes 393224 | tf_op jit(solution)/shard_map/ppermute | solution.py:422
  35.5 23.1 %collective-permute-start.5 = (f32[96,128]{1,0:T(8,128)S(1)}, f32[96,128]{1,0:T(8,128)S(1)}, u32[]{:S(2)}, u32[]{:S(2)}) collective-permute-start(f32[96,128]{1,0:T(8,128)S(1)} %join.1.later_ref), channel_id=1, source_target_pairs={{0,1},{1,0},{2,3},{3,2},{4,5},{5,4},{6,7},{7,6},{8,9},{9,8},{10,11... | collective-permute-start | bytes 147464 | tf_op jit(solution)/shard_map/ppermute | solution.py:438
  38.7 25.9 %collective-permute-start.6 = (f32[208,128]{1,0:T(8,128)S(1)}, f32[208,128]{1,0:T(8,128)S(1)}, u32[]{:S(2)}, u32[]{:S(2)}) collective-permute-start(f32[208,128]{1,0:T(8,128)S(1)} %forward.1), channel_id=1, source_target_pairs={{0,2},{2,4},{4,6},{3,1},{5,3},{7,5},{8,10},{10,12},{12,14},{11,9},... | collective-permute-start | bytes 319496 | tf_op jit(solution)/shard_map/ppermute | solution.py:447
  58.6 6.0 %collective-permute-start.7 = (f32[96,128]{1,0:T(8,128)S(1)}, f32[96,128]{1,0:T(8,128)S(1)}, u32[]{:S(2)}, u32[]{:S(2)}) collective-permute-start(f32[96,128]{1,0:T(8,128)S(1)} %collective-permute-done.5.more_ref), channel_id=1, source_target_pairs={{0,2},{2,4},{4,6},{3,1},{5,3},{7,5},{8,10},{10,12},{12,14},{11,9},... | collective-permute-start | bytes 147464 | tf_op jit(solution)/shard_map/ppermute | solution.py:448
  59.9 4.7 %copy-start = (bf16[4,64,512]{2,1,0:T(8,128)(2,1)S(1)}, bf16[4,64,512]{2,1,0:T(8,128)(2,1)}, u32[]{:S(2)}) copy-start(bf16[4,64,512]{2,1,0:T(8,128)(2,1)} %outer_ref.1) | copy-start | bytes 786436

commit v8 on v6

--- a/solution.py
+++ b/solution.py
@@ -112,16 +112,14 @@
         cell = column_ref[:, cut]
         place = (level_ref[:, cut] - lowest + 2) * ROW + (cell >> 7)
         value = value_ref[:, cut]
-        high = value.astype(BF16).astype(F32)
-        rest = value - high
-        middle = rest.astype(BF16).astype(F32)
-        low = rest - middle
+        high = value.astype(BF16)
+        rest = value - high.astype(F32)
+        middle = rest.astype(BF16)
+        low = (rest - middle.astype(F32)).astype(BF16)
         index = lax.broadcasted_iota(jnp.int32, (COL, chunk), 0)
-        here = index == place
+        mask = jnp.where(index == place, 1.0, 0.0).astype(BF16)
         across = jnp.where(index == (cell & 127), 1.0, 0.0).astype(BF16)
-        down = jnp.concatenate(
-            [jnp.where(here, part, 0.0).astype(BF16) for part in (1.0, high, middle, low)], axis=0
-        )
+        down = jnp.concatenate([mask, mask * high, mask * middle, mask * low], axis=0)
         total = total + lax.dot_general(
             down, across, (((1,), (1,)), ((), ())), preferred_element_type=F32
         )

time: 61.3 us -> 61.3 us (level)
  the two profiles are of different devices: /device:TPU:90 before, /device:TPU:92 now
where the time goes in v8:
time: 61.3 us; the launch traced here: 60.9 us
  starting transfers between devices  38.8 us (63%)
  waiting for transfers between devices  16.8 us (27%)
  Pallas kernels  4.49 us (7%)
  between operations  0.78 us (1%)
    ppermute x1, starting transfers between devices, shards(): pair = lax.ppermute(block, 'lev', pairs)  18.5 us
    ppermute x1, waiting for transfers between devices, shards(): more = lax.ppermute(joined, 'lev', pairs)  9.8 us
    ppermute x1, waiting for transfers between devices, shards(): east = lax.ppermute(left, 'lon', lon_down)  4.86 us
    ppermute x1, starting transfers between devices, shards(): west = lax.ppermute(right, 'lon', lon_up)  4.69 us
    pallas_call x6, Pallas kernels, call(): pl.pallas_call(kernel, out_shape=shapes[0] if single else shapes, in_spec...  4.49 us
    ppermute x1, starting transfers between devices, shards(): after = lax.ppermute(down, 'lat', lat_down)  3.64 us
    ppermute x1, starting transfers between devices, shards(): far_block = lax.ppermute(onward, 'lev', far)  3.11 us
    ppermute x1, starting transfers between devices, shards(): far_more = lax.ppermute(more, 'lev', far)  3.09 us
  transfers between devices with their start and end apart: 8, of which 3 were waited for; matrix products, arithmetic and copies ran while one was open for 0% of the time, Pallas kernels for 2%

profile of v8, /device:TPU:92, one launch (start us, length us, event | category | flops | bytes accessed | tf_op | source)
XLA Modules:
  0.0 60.9 jit_solution(12953490156540415581)
XLA Ops:
  0.6 2.1 %prepare.1 = (f32[256,128]{1,0:T(8,128)S(1)}, f32[256,128]{1,0:T(8,128)S(1)}, f32[88,128]{1,0:T(8,128)S(1)}, f32[88,128]{1,0:T(8,128)S(1)}) custom-call(s32[1]{0:T(128)} %bitcast.1.lowest_ref, bf16[4,64,512]{2,1,0:T(8,128)(2,1)} %outer_ref.1, bf16[3,4,16,128]{3,2,1,0:T(8,128)(2,1)} %courant_hbm.1, s32[1,2048]{1,0:T(1,128)} %bitcast.5, s32[1,2048]{1,0:T(1,128)} %bitcast.6, ...), custom_call_target="tpu_custom_call" | custom-call | flops 500000 | bytes 500000 | tf_op jit(solution)/shard_map/prepare/pallas_call | solution.py:377
  2.7 1.9 %collective-permute-start = (f32[88,128]{1,0:T(8,128)S(1)}, f32[88,128]{1,0:T(8,128)S(1)}, u32[]{:S(2)}, u32[]{:S(2)}) collective-permute-start(f32[88,128]{1,0:T(8,128)S(1)} %get-tuple-element.19), channel_id=1, source_target_pairs={{0,64},{64,128},{128,192},{192,256},{256,320},{320,384},{384,448},... | collective-permute-start | bytes 135176 | tf_op jit(solution)/shard_map/ppermute | solution.py:418
  4.6 3.6 %collective-permute-start.1 = (f32[88,128]{1,0:T(8,128)S(1)}, f32[88,128]{1,0:T(8,128)S(1)}, u32[]{:S(2)}, u32[]{:S(2)}) collective-permute-start(f32[88,128]{1,0:T(8,128)S(1)} %get-tuple-element.20), channel_id=1, source_target_pairs={{64,0},{128,64},{192,128},{256,192},{320,256},{384,320},{448,384},... | collective-permute-start | bytes 135176 | tf_op jit(solution)/shard_map/ppermute | solution.py:419
  8.3 18.5 %collective-permute-start.4 = (f32[256,128]{1,0:T(8,128)S(1)}, f32[256,128]{1,0:T(8,128)S(1)}, u32[]{:S(2)}, u32[]{:S(2)}) collective-permute-start(f32[256,128]{1,0:T(8,128)S(1)} %get-tuple-element.17.block_ref), channel_id=1, source_target_pairs={{0,1},{1,0},{2,3},{3,2},{4,5},{5,4},{6,7},{7,6},{8,9},{9,8},{10,11... | collective-permute-start | bytes 393224 | tf_op jit(solution)/shard_map/ppermute | solution.py:420
  26.7 0.0 collective-permute-done.before_ref
  26.8 0.0 collective-permute-done.1.after_ref
  26.8 0.2 edges.1
  27.0 4.7 %collective-permute-start.2 = (f32[24,128]{1,0:T(8,128)S(1)}, f32[24,128]{1,0:T(8,128)S(1)}, u32[]{:S(2)}, u32[]{:S(2)}) collective-permute-start(f32[24,128]{1,0:T(8,128)S(1)} %get-tuple-element.23), channel_id=1, source_target_pairs={{0,8},{8,16},{16,24},{24,32},{32,40},{40,48},{48,56},{56,0},{1,9},... | collective-permute-start | bytes 36872 | tf_op jit(solution)/shard_map/ppermute | solution.py:433
  31.7 1.9 %collective-permute-start.3 = (f32[24,128]{1,0:T(8,128)S(1)}, f32[24,128]{1,0:T(8,128)S(1)}, u32[]{:S(2)}, u32[]{:S(2)}) collective-permute-start(f32[24,128]{1,0:T(8,128)S(1)} %get-tuple-element.24), channel_id=1, source_target_pairs={{0,56},{8,0},{16,8},{24,16},{32,24},{40,32},{48,40},{56,48},{1,57}... | collective-permute-start | bytes 36872 | tf_op jit(solution)/shard_map/ppermute | solution.py:434
  33.7 0.0 collective-permute-done.2.west_ref
  33.7 4.9 %collective-permute-done.3.east_ref = f32[24,128]{1,0:T(8,128)S(1)} collective-permute-done((f32[24,128]{1,0:T(8,128)S(1)}, f32[24,128]{1,0:T(8,128)S(1)}, u32[]{:S(2)}, u32[]{:S(2)}) %collective-permute-start.3) | collective-permute-done | bytes 12320 | tf_op jit(solution)/shard_map/ppermute | solution.py:434
  38.5 1.9 %collective-permute-start.5 = (f32[96,128]{1,0:T(8,128)S(1)}, f32[96,128]{1,0:T(8,128)S(1)}, u32[]{:S(2)}, u32[]{:S(2)}) collective-permute-start(f32[96,128]{1,0:T(8,128)S(1)} %join.1.later_ref), channel_id=1, source_target_pairs={{0,1},{1,0},{2,3},{3,2},{4,5},{5,4},{6,7},{7,6},{8,9},{9,8},{10,11... | collective-permute-start | bytes 147464 | tf_op jit(solution)/shard_map/ppermute | solution.py:436
  40.5 0.0 collective-permute-done.4.pair_ref
  40.5 3.1 %collective-permute-start.6 = (f32[208,128]{1,0:T(8,128)S(1)}, f32[208,128]{1,0:T(8,128)S(1)}, u32[]{:S(2)}, u32[]{:S(2)}) collective-permute-start(f32[208,128]{1,0:T(8,128)S(1)} %forward.1), channel_id=1, source_target_pairs={{0,2},{2,4},{4,6},{3,1},{5,3},{7,5},{8,10},{10,12},{12,14},{11,9},... | collective-permute-start | bytes 319496 | tf_op jit(solution)/shard_map/ppermute | solution.py:445
  43.6 9.8 %collective-permute-done.5.more_ref = f32[96,128]{1,0:T(8,128)S(1)} collective-permute-done((f32[96,128]{1,0:T(8,128)S(1)}, f32[96,128]{1,0:T(8,128)S(1)}, u32[]{:S(2)}, u32[]{:S(2)}) %collective-permute-start.5) | collective-permute-done | bytes 49184 | tf_op jit(solution)/shard_map/ppermute | solution.py:436
  53.4 3.1 %collective-permute-start.7 = (f32[96,128]{1,0:T(8,128)S(1)}, f32[96,128]{1,0:T(8,128)S(1)}, u32[]{:S(2)}, u32[]{:S(2)}) collective-permute-start(f32[96,128]{1,0:T(8,128)S(1)} %collective-permute-done.5.more_ref), channel_id=1, source_target_pairs={{0,2},{2,4},{4,6},{3,1},{5,3},{7,5},{8,10},{10,12},{12,14},{11,9},... | collective-permute-start | bytes 147464 | tf_op jit(solution)/shard_map/ppermute | solution.py:446
  56.5 0.0 copy-start
  56.6 0.7 %assemble.1 = (f32[6,12,24,256]{3,2,1,0:T(8,128)S(1)}, f32[2,24,256]{2,1,0:T(8,128)S(1)}, f32[2,24,256]{2,1,0:T(8,128)S(1)}, f32[2,24,256]{2,1,0:T(8,128)S(1)}, f32[2,16,128]{2,1,0:T(8,128)S(1)}) custom-call(s32[1]{0:T(128)} %bitcast.parity_ref, f32[4,4,24,128]{3,2,1,0:T(8,128)S(1)} %get-tuple-element.21.own_ref, ...), custom_call_target="tpu_custom_call" | custom-call | flops 1000000000 | bytes 1000000000 | tf_op jit(solution)/shard_map/assemble/pallas_call | solution.py:377
  57.3 2.2 %collective-permute-done.7.far_more_ref = f32[96,128]{1,0:T(8,128)S(1)} collective-permute-done((f32[96,128]{1,0:T(8,128)S(1)}, f32[96,128]{1,0:T(8,128)S(1)}, u32[]{:S(2)}, u32[]{:S(2)}) %collective-permute-start.7) | collective-permute-done | bytes 49184 | tf_op jit(solution)/shard_map/ppermute | solution.py:446
  59.4 0.0 collective-permute-done.6.far_ref
  59.4 0.0 copy-done
  59.4 1.5 %steps.1 = (f32[4,16,128]{2,1,0:T(8,128)}, f32[4,16,128]{2,1,0:T(8,128)}, bf16[4,64,512]{2,1,0:T(8,128)(2,1)}) custom-call(s32[1]{0:T(128)} %bitcast.parity_ref, f32[6,12,24,256]{3,2,1,0:T(8,128)S(1)} %get-tuple-element.26.given_ref, f32[2,24,256]{2,1,0:T(8,128)S(1)} %get-tuple-element.27.given_first_ref, ...), custom_call_target="tpu_custom_call" | custom-call | flops 500000 | bytes 500000 | tf_op jit(solution)/shard_map/steps/pallas_call | solution.py:377
  (2 shorter events, 0.0 us)
Async XLA Ops:
  2.7 24.1 %collective-permute-start = (f32[88,128]{1,0:T(8,128)S(1)}, f32[88,128]{1,0:T(8,128)S(1)}, u32[]{:S(2)}, u32[]{:S(2)}) collective-permute-start(f32[88,128]{1,0:T(8,128)S(1)} %get-tuple-element.19), channel_id=1, source_target_pairs={{0,64},{64,128},{128,192},{192,256},{256,320},{320,384},{384,448},... | collective-permute-start | bytes 135176 | tf_op jit(solution)/shard_map/ppermute | solution.py:418
  4.6 22.1 %collective-permute-start.1 = (f32[88,128]{1,0:T(8,128)S(1)}, f32[88,128]{1,0:T(8,128)S(1)}, u32[]{:S(2)}, u32[]{:S(2)}) collective-permute-start(f32[88,128]{1,0:T(8,128)S(1)} %get-tuple-element.20), channel_id=1, source_target_pairs={{64,0},{128,64},{192,128},{256,192},{320,256},{384,320},{448,384},... | collective-permute-start | bytes 135176 | tf_op jit(solution)/shard_map/ppermute | solution.py:419
  8.3 32.2 %collective-permute-start.4 = (f32[256,128]{1,0:T(8,128)S(1)}, f32[256,128]{1,0:T(8,128)S(1)}, u32[]{:S(2)}, u32[]{:S(2)}) collective-permute-start(f32[256,128]{1,0:T(8,128)S(1)} %get-tuple-element.17.block_ref), channel_id=1, source_target_pairs={{0,1},{1,0},{2,3},{3,2},{4,5},{5,4},{6,7},{7,6},{8,9},{9,8},{10,11... | collective-permute-start | bytes 393224 | tf_op jit(solution)/shard_map/ppermute | solution.py:420
  27.0 6.6 %collective-permute-start.2 = (f32[24,128]{1,0:T(8,128)S(1)}, f32[24,128]{1,0:T(8,128)S(1)}, u32[]{:S(2)}, u32[]{:S(2)}) collective-permute-start(f32[24,128]{1,0:T(8,128)S(1)} %get-tuple-element.23), channel_id=1, source_target_pairs={{0,8},{8,16},{16,24},{24,32},{32,40},{40,48},{48,56},{56,0},{1,9},... | collective-permute-start | bytes 36872 | tf_op jit(solution)/shard_map/ppermute | solution.py:433
  31.7 6.8 %collective-permute-start.3 = (f32[24,128]{1,0:T(8,128)S(1)}, f32[24,128]{1,0:T(8,128)S(1)}, u32[]{:S(2)}, u32[]{:S(2)}) collective-permute-start(f32[24,128]{1,0:T(8,128)S(1)} %get-tuple-element.24), channel_id=1, source_target_pairs={{0,56},{8,0},{16,8},{24,16},{32,24},{40,32},{48,40},{56,48},{1,57}... | collective-permute-start | bytes 36872 | tf_op jit(solution)/shard_map/ppermute | solution.py:434
  38.5 14.9 %collective-permute-start.5 = (f32[96,128]{1,0:T(8,128)S(1)}, f32[96,128]{1,0:T(8,128)S(1)}, u32[]{:S(2)}, u32[]{:S(2)}) collective-permute-start(f32[96,128]{1,0:T(8,128)S(1)} %join.1.later_ref), channel_id=1, source_target_pairs={{0,1},{1,0},{2,3},{3,2},{4,5},{5,4},{6,7},{7,6},{8,9},{9,8},{10,11... | collective-permute-start | bytes 147464 | tf_op jit(solution)/shard_map/ppermute | solution.py:436
  40.5 18.9 %collective-permute-start.6 = (f32[208,128]{1,0:T(8,128)S(1)}, f32[208,128]{1,0:T(8,128)S(1)}, u32[]{:S(2)}, u32[]{:S(2)}) collective-permute-start(f32[208,128]{1,0:T(8,128)S(1)} %forward.1), channel_id=1, source_target_pairs={{0,2},{2,4},{4,6},{3,1},{5,3},{7,5},{8,10},{10,12},{12,14},{11,9},... | collective-permute-start | bytes 319496 | tf_op jit(solution)/shard_map/ppermute | solution.py:445
  53.4 6.0 %collective-permute-start.7 = (f32[96,128]{1,0:T(8,128)S(1)}, f32[96,128]{1,0:T(8,128)S(1)}, u32[]{:S(2)}, u32[]{:S(2)}) collective-permute-start(f32[96,128]{1,0:T(8,128)S(1)} %collective-permute-done.5.more_ref), channel_id=1, source_target_pairs={{0,2},{2,4},{4,6},{3,1},{5,3},{7,5},{8,10},{10,12},{12,14},{11,9},... | collective-permute-start | bytes 147464 | tf_op jit(solution)/shard_map/ppermute | solution.py:446
  56.5 2.9 %copy-start = (bf16[4,64,512]{2,1,0:T(8,128)(2,1)S(1)}, bf16[4,64,512]{2,1,0:T(8,128)(2,1)}, u32[]{:S(2)}) copy-start(bf16[4,64,512]{2,1,0:T(8,128)(2,1)} %outer_ref.1) | copy-start | bytes 786436

commit v9 on v8

--- a/solution.py
+++ b/solution.py
@@ -386,16 +386,19 @@
     )(*ins)
 
 
-def shift(size, by, wrap):
-    return [
-        (i, (i + by) % size) for i in range(size) if wrap or 0 <= i + by < size
-    ]
+def exchange(upper, lower, axis, wrap):
+    size = lax.axis_size(axis)
+    even = (lax.axis_index(axis) & 1) == 0
+    first = [(i, i ^ 1) for i in range(size)]
+    second = [(i, i + 1 if i % 2 else i - 1) for i in range(size)]
+    second = [(i, j % size) for i, j in second if wrap or 0 <= j < size]
+    one = lax.ppermute(jnp.where(even, upper, lower), axis, first)
+    two = lax.ppermute(jnp.where(even, lower, upper), axis, second)
+    return jnp.where(even, two, one), jnp.where(even, one, two)
 
 
 def shards(outer_increment, courant, obs_column, obs_level, obs_value):
     lev = lax.axis_size("lev")
-    lat_up, lat_down = (shift(lax.axis_size("lat"), by, False) for by in (1, -1))
-    lon_up, lon_down = (shift(lax.axis_size("lon"), by, True) for by in (1, -1))
     pairs = [(i, i ^ 1) for i in range(lev)]
     far = [(i, i + 2) for i in range(0, lev - 2, 2)] + [(i, i - 2) for i in range(3, lev, 2)]
     position = lax.axis_index("lev").astype(jnp.int32)
@@ -415,8 +418,7 @@
         places={i: HBM for i in range(1, 6)},
         name="prepare",
     )
-    before = lax.ppermute(up, "lat", lat_up)
-    after = lax.ppermute(down, "lat", lat_down)
+    before, after = exchange(up, down, "lat", False)
     pair = lax.ppermute(block, "lev", pairs)
     own, obs, near, right, left = call(
         edges_kernel,
@@ -430,8 +432,9 @@
         [block, fields, before, after],
         cost=2000000000, name="edges",
     )
-    west = lax.ppermute(right, "lon", lon_up)
-    east = lax.ppermute(left, "lon", lon_down)
+    lon = lax.axis_size("lon")
+    west = lax.ppermute(right, "lon", [(i, (i + 1) % lon) for i in range(lon)])
+    east = lax.ppermute(left, "lon", [(i, (i - 1) % lon) for i in range(lon)])
     joined = call(join_kernel, [((MORE, COL), F32)], [near, west, east], cost=1000, name="join")
     more = lax.ppermute(joined, "lev", pairs)
     onward = call(

time: 61.3 us -> 62.4 us (1.018)
  the two profiles are of different devices: /device:TPU:92 before, /device:TPU:30 now
where the time goes in v9:
time: 62.4 us; the launch traced here: 62 us
  starting transfers between devices  35.9 us (58%)
  waiting for transfers between devices  20.9 us (33%)
  Pallas kernels  4.49 us (7%)
  between operations  0.8 us (1%)
    ppermute x1, starting transfers between devices, shards(): pair = lax.ppermute(block, 'lev', pairs)  18.5 us
    ppermute x1, waiting for transfers between devices, shards(): more = lax.ppermute(joined, 'lev', pairs)  12 us
    ppermute x1, starting transfers between devices, exchange(): one = lax.ppermute(jnp.where(even, upper, lower), axis, first)  5.64 us
    ppermute x1, waiting for transfers between devices, shards(): east = lax.ppermute(left, 'lon', [(i, (i - 1) % lon) for i in range(lon)])  4.86 us
    ppermute x1, starting transfers between devices, shards(): west = lax.ppermute(right, 'lon', [(i, (i + 1) % lon) for i in range(lon)])  4.7 us
    pallas_call x6, Pallas kernels, call(): pl.pallas_call(kernel, out_shape=shapes[0] if single else shapes, in_spec...  4.49 us
    ppermute x1, waiting for transfers between devices, shards(): far_more = lax.ppermute(more, 'lev', far)  3.97 us
    ppermute x1, starting transfers between devices, shards(): east = lax.ppermute(left, 'lon', [(i, (i - 1) % lon) for i in range(lon)])  1.92 us
  transfers between devices with their start and end apart: 8, of which 3 were waited for; matrix products, arithmetic and copies ran while one was open for 0% of the time, Pallas kernels for 2%

profile of v9, /device:TPU:30, one launch (start us, length us, event | category | flops | bytes accessed | tf_op | source)
XLA Modules:
  0.0 62.0 jit_solution(16196309135995823908)
XLA Ops:
  0.6 2.1 %prepare.1 = (f32[256,128]{1,0:T(8,128)S(1)}, f32[256,128]{1,0:T(8,128)S(1)}, f32[88,128]{1,0:T(8,128)S(1)}, f32[88,128]{1,0:T(8,128)S(1)}) custom-call(s32[1]{0:T(128)} %bitcast.1.lowest_ref, bf16[4,64,512]{2,1,0:T(8,128)(2,1)} %outer_ref.1, bf16[3,4,16,128]{3,2,1,0:T(8,128)(2,1)} %courant_hbm.1, s32[1,2048]{1,0:T(1,128)} %bitcast.5, s32[1,2048]{1,0:T(1,128)} %bitcast.6, ...), custom_call_target="tpu_custom_call" | custom-call | flops 500000 | bytes 500000 | tf_op jit(solution)/shard_map/prepare/pallas_call | solution.py:377
  2.7 0.7 %collective-permute-start = (f32[88,128]{1,0:T(8,128)S(1)}, f32[88,128]{1,0:T(8,128)S(1)}, u32[]{:S(2)}, u32[]{:S(2)}) collective-permute-start(f32[88,128]{1,0:T(8,128)S(1)} %get-tuple-element.34), channel_id=1, source_target_pairs={{64,128},{128,64},{192,256},{256,192},{320,384},{384,320},{448,512... | collective-permute-start | bytes 135176 | tf_op jit(solution)/shard_map/ppermute | solution.py:396
  3.4 5.6 %collective-permute-start.1 = (f32[88,128]{1,0:T(8,128)S(1)}, f32[88,128]{1,0:T(8,128)S(1)}, u32[]{:S(2)}, u32[]{:S(2)}) collective-permute-start(f32[88,128]{1,0:T(8,128)S(1)} %get-tuple-element.33), channel_id=1, source_target_pairs={{0,64},{64,0},{128,192},{192,128},{256,320},{320,256},{384,448},{4... | collective-permute-start | bytes 135176 | tf_op jit(solution)/shard_map/ppermute | solution.py:395
  9.0 18.5 %collective-permute-start.4 = (f32[256,128]{1,0:T(8,128)S(1)}, f32[256,128]{1,0:T(8,128)S(1)}, u32[]{:S(2)}, u32[]{:S(2)}) collective-permute-start(f32[256,128]{1,0:T(8,128)S(1)} %get-tuple-element.17.block_ref), channel_id=1, source_target_pairs={{0,1},{1,0},{2,3},{3,2},{4,5},{5,4},{6,7},{7,6},{8,9},{9,8},{10,11... | collective-permute-start | bytes 393224 | tf_op jit(solution)/shard_map/ppermute | solution.py:422
  27.5 0.0 collective-permute-done
  27.5 0.0 collective-permute-done.1
  27.5 0.3 edges.1
  27.8 4.7 %collective-permute-start.2 = (f32[24,128]{1,0:T(8,128)S(1)}, f32[24,128]{1,0:T(8,128)S(1)}, u32[]{:S(2)}, u32[]{:S(2)}) collective-permute-start(f32[24,128]{1,0:T(8,128)S(1)} %get-tuple-element.23), channel_id=1, source_target_pairs={{0,8},{8,16},{16,24},{24,32},{32,40},{40,48},{48,56},{56,0},{1,9},... | collective-permute-start | bytes 36872 | tf_op jit(solution)/shard_map/ppermute | solution.py:436
  32.5 1.9 %collective-permute-start.3 = (f32[24,128]{1,0:T(8,128)S(1)}, f32[24,128]{1,0:T(8,128)S(1)}, u32[]{:S(2)}, u32[]{:S(2)}) collective-permute-start(f32[24,128]{1,0:T(8,128)S(1)} %get-tuple-element.24), channel_id=1, source_target_pairs={{0,56},{8,0},{16,8},{24,16},{32,24},{40,32},{48,40},{56,48},{1,57}... | collective-permute-start | bytes 36872 | tf_op jit(solution)/shard_map/ppermute | solution.py:437
  34.4 0.0 collective-permute-done.2.west_ref
  34.5 4.9 %collective-permute-done.3.east_ref = f32[24,128]{1,0:T(8,128)S(1)} collective-permute-done((f32[24,128]{1,0:T(8,128)S(1)}, f32[24,128]{1,0:T(8,128)S(1)}, u32[]{:S(2)}, u32[]{:S(2)}) %collective-permute-start.3) | collective-permute-done | bytes 12320 | tf_op jit(solution)/shard_map/ppermute | solution.py:437
  39.3 1.9 %collective-permute-start.5 = (f32[96,128]{1,0:T(8,128)S(1)}, f32[96,128]{1,0:T(8,128)S(1)}, u32[]{:S(2)}, u32[]{:S(2)}) collective-permute-start(f32[96,128]{1,0:T(8,128)S(1)} %join.1.later_ref), channel_id=1, source_target_pairs={{0,1},{1,0},{2,3},{3,2},{4,5},{5,4},{6,7},{7,6},{8,9},{9,8},{10,11... | collective-permute-start | bytes 147464 | tf_op jit(solution)/shard_map/ppermute | solution.py:439
  41.2 0.0 collective-permute-done.4.pair_ref
  41.3 1.3 %collective-permute-start.6 = (f32[208,128]{1,0:T(8,128)S(1)}, f32[208,128]{1,0:T(8,128)S(1)}, u32[]{:S(2)}, u32[]{:S(2)}) collective-permute-start(f32[208,128]{1,0:T(8,128)S(1)} %forward.1), channel_id=1, source_target_pairs={{0,2},{2,4},{4,6},{3,1},{5,3},{7,5},{8,10},{10,12},{12,14},{11,9},... | collective-permute-start | bytes 319496 | tf_op jit(solution)/shard_map/ppermute | solution.py:448
  42.6 12.0 %collective-permute-done.5.more_ref = f32[96,128]{1,0:T(8,128)S(1)} collective-permute-done((f32[96,128]{1,0:T(8,128)S(1)}, f32[96,128]{1,0:T(8,128)S(1)}, u32[]{:S(2)}, u32[]{:S(2)}) %collective-permute-start.5) | collective-permute-done | bytes 49184 | tf_op jit(solution)/shard_map/ppermute | solution.py:439
  54.6 1.3 %collective-permute-start.7 = (f32[96,128]{1,0:T(8,128)S(1)}, f32[96,128]{1,0:T(8,128)S(1)}, u32[]{:S(2)}, u32[]{:S(2)}) collective-permute-start(f32[96,128]{1,0:T(8,128)S(1)} %collective-permute-done.5.more_ref), channel_id=1, source_target_pairs={{0,2},{2,4},{4,6},{3,1},{5,3},{7,5},{8,10},{10,12},{12,14},{11,9},... | collective-permute-start | bytes 147464 | tf_op jit(solution)/shard_map/ppermute | solution.py:449
  55.9 0.0 copy-start
  55.9 0.7 %assemble.1 = (f32[6,12,24,256]{3,2,1,0:T(8,128)S(1)}, f32[2,24,256]{2,1,0:T(8,128)S(1)}, f32[2,24,256]{2,1,0:T(8,128)S(1)}, f32[2,24,256]{2,1,0:T(8,128)S(1)}, f32[2,16,128]{2,1,0:T(8,128)S(1)}) custom-call(s32[1]{0:T(128)} %bitcast.parity_ref, f32[4,4,24,128]{3,2,1,0:T(8,128)S(1)} %get-tuple-element.21.own_ref, ...), custom_call_target="tpu_custom_call" | custom-call | flops 1000000000 | bytes 1000000000 | tf_op jit(solution)/shard_map/assemble/pallas_call | solution.py:377
  56.6 4.0 %collective-permute-done.7.far_more_ref = f32[96,128]{1,0:T(8,128)S(1)} collective-permute-done((f32[96,128]{1,0:T(8,128)S(1)}, f32[96,128]{1,0:T(8,128)S(1)}, u32[]{:S(2)}, u32[]{:S(2)}) %collective-permute-start.7) | collective-permute-done | bytes 49184 | tf_op jit(solution)/shard_map/ppermute | solution.py:449
  60.6 0.0 collective-permute-done.6.far_ref
  60.6 0.0 copy-done
  60.6 1.5 %steps.1 = (f32[4,16,128]{2,1,0:T(8,128)}, f32[4,16,128]{2,1,0:T(8,128)}, bf16[4,64,512]{2,1,0:T(8,128)(2,1)}) custom-call(s32[1]{0:T(128)} %bitcast.parity_ref, f32[6,12,24,256]{3,2,1,0:T(8,128)S(1)} %get-tuple-element.26.given_ref, f32[2,24,256]{2,1,0:T(8,128)S(1)} %get-tuple-element.27.given_first_ref, ...), custom_call_target="tpu_custom_call" | custom-call | flops 500000 | bytes 500000 | tf_op jit(solution)/shard_map/steps/pallas_call | solution.py:377
  (4 shorter events, 0.0 us)
Async XLA Ops:
  2.7 24.8 %collective-permute-start = (f32[88,128]{1,0:T(8,128)S(1)}, f32[88,128]{1,0:T(8,128)S(1)}, u32[]{:S(2)}, u32[]{:S(2)}) collective-permute-start(f32[88,128]{1,0:T(8,128)S(1)} %get-tuple-element.34), channel_id=1, source_target_pairs={{64,128},{128,64},{192,256},{256,192},{320,384},{384,320},{448,512... | collective-permute-start | bytes 135176 | tf_op jit(solution)/shard_map/ppermute | solution.py:396
  3.4 24.1 %collective-permute-start.1 = (f32[88,128]{1,0:T(8,128)S(1)}, f32[88,128]{1,0:T(8,128)S(1)}, u32[]{:S(2)}, u32[]{:S(2)}) collective-permute-start(f32[88,128]{1,0:T(8,128)S(1)} %get-tuple-element.33), channel_id=1, source_target_pairs={{0,64},{64,0},{128,192},{192,128},{256,320},{320,256},{384,448},{4... | collective-permute-start | bytes 135176 | tf_op jit(solution)/shard_map/ppermute | solution.py:395
  9.0 32.2 %collective-permute-start.4 = (f32[256,128]{1,0:T(8,128)S(1)}, f32[256,128]{1,0:T(8,128)S(1)}, u32[]{:S(2)}, u32[]{:S(2)}) collective-permute-start(f32[256,128]{1,0:T(8,128)S(1)} %get-tuple-element.17.block_ref), channel_id=1, source_target_pairs={{0,1},{1,0},{2,3},{3,2},{4,5},{5,4},{6,7},{7,6},{8,9},{9,8},{10,11... | collective-permute-start | bytes 393224 | tf_op jit(solution)/shard_map/ppermute | solution.py:422
  27.8 6.6 %collective-permute-start.2 = (f32[24,128]{1,0:T(8,128)S(1)}, f32[24,128]{1,0:T(8,128)S(1)}, u32[]{:S(2)}, u32[]{:S(2)}) collective-permute-start(f32[24,128]{1,0:T(8,128)S(1)} %get-tuple-element.23), channel_id=1, source_target_pairs={{0,8},{8,16},{16,24},{24,32},{32,40},{40,48},{48,56},{56,0},{1,9},... | collective-permute-start | bytes 36872 | tf_op jit(solution)/shard_map/ppermute | solution.py:436
  32.5 6.8 %collective-permute-start.3 = (f32[24,128]{1,0:T(8,128)S(1)}, f32[24,128]{1,0:T(8,128)S(1)}, u32[]{:S(2)}, u32[]{:S(2)}) collective-permute-start(f32[24,128]{1,0:T(8,128)S(1)} %get-tuple-element.24), channel_id=1, source_target_pairs={{0,56},{8,0},{16,8},{24,16},{32,24},{40,32},{48,40},{56,48},{1,57}... | collective-permute-start | bytes 36872 | tf_op jit(solution)/shard_map/ppermute | solution.py:437
  39.3 15.3 %collective-permute-start.5 = (f32[96,128]{1,0:T(8,128)S(1)}, f32[96,128]{1,0:T(8,128)S(1)}, u32[]{:S(2)}, u32[]{:S(2)}) collective-permute-start(f32[96,128]{1,0:T(8,128)S(1)} %join.1.later_ref), channel_id=1, source_target_pairs={{0,1},{1,0},{2,3},{3,2},{4,5},{5,4},{6,7},{7,6},{8,9},{9,8},{10,11... | collective-permute-start | bytes 147464 | tf_op jit(solution)/shard_map/ppermute | solution.py:439
  41.3 19.3 %collective-permute-start.6 = (f32[208,128]{1,0:T(8,128)S(1)}, f32[208,128]{1,0:T(8,128)S(1)}, u32[]{:S(2)}, u32[]{:S(2)}) collective-permute-start(f32[208,128]{1,0:T(8,128)S(1)} %forward.1), channel_id=1, source_target_pairs={{0,2},{2,4},{4,6},{3,1},{5,3},{7,5},{8,10},{10,12},{12,14},{11,9},... | collective-permute-start | bytes 319496 | tf_op jit(solution)/shard_map/ppermute | solution.py:448
  54.6 6.0 %collective-permute-start.7 = (f32[96,128]{1,0:T(8,128)S(1)}, f32[96,128]{1,0:T(8,128)S(1)}, u32[]{:S(2)}, u32[]{:S(2)}) collective-permute-start(f32[96,128]{1,0:T(8,128)S(1)} %collective-permute-done.5.more_ref), channel_id=1, source_target_pairs={{0,2},{2,4},{4,6},{3,1},{5,3},{7,5},{8,10},{10,12},{12,14},{11,9},... | collective-permute-start | bytes 147464 | tf_op jit(solution)/shard_map/ppermute | solution.py:449
  55.9 4.7 %copy-start = (bf16[4,64,512]{2,1,0:T(8,128)(2,1)S(1)}, bf16[4,64,512]{2,1,0:T(8,128)(2,1)}, u32[]{:S(2)}) copy-start(bf16[4,64,512]{2,1,0:T(8,128)(2,1)} %outer_ref.1) | copy-start | bytes 786436
